TPU v7x, 32 devices: a whole 2x2x4 slice. The times are simulated.
32 devices in a mesh: runs: 2 (over y), sec: 4 (over z), mpo: 2 (over x), rep: 2 (over core).
Axes of the slice: x: 2, y: 2, z: 4, core: 2. Of those that a mesh axis runs over, the one named last changes fastest.
Arguments:
- psi: bfloat16 [32, 128, 16, 128], P(('runs', 'sec', 'rep')), parts along dimension 0, may hold values from -6 to 6
- dims: int32 [32], P('runs'), parts along dimension 0, may hold values from 1 to 128, 1280 in all
- left_env: bfloat16 [16, 32, 128, 128], P('mpo', ('runs', 'sec', 'rep')), parts along dimension 1, may hold values from -0.5 to 0.5
- right_env: bfloat16 [16, 32, 128, 128], P('mpo', ('runs', 'sec', 'rep')), parts along dimension 1, may hold values from -0.5 to 0.5
- shift: int32 [16], P('mpo'), may hold values from -2 to 2, as said below
- mpo_coef: bfloat16 [16, 16, 16, 16], P('mpo'), may hold values from -0.09375 to 0.09375
- mpo_mask: int32 [16, 16], P('mpo'), may hold values 0 or 1
Outputs:
- result: bfloat16 [32, 128, 16, 128], P(('runs', 'sec', 'rep'), None, 'mpo'), parts along dimension 0
There are 2 independent parts, one for each index of `runs`. A program takes and returns all parts, laid end to end along the dimension named above; an argument that names none is the same for every part. Nothing has to cross between parts.
Inputs may be any that keep to these rules, and one draw needn't show every extreme that they name: `shift`: every offset from -2 to 2 is carried by some channel.
All inputs are finite; a program needn't handle non-finite values. No bound on the sum of `mpo_mask` on one device may be relied on, other than what follows from the above.
Results may differ from a plain program's by a relative error of at most 0.011.
Values may be sent and summed in bfloat16 or wider, within the bound.
No kernel may reach another device: no remote copies, remote signals or barrier semaphores. Data moves between devices by JAX's collectives and lax.ppermute only.
A program may use at most 128 MiB of HBM per device.

v0:
```python
import jax
import jax.numpy as jnp
from jax import lax
from jax.sharding import PartitionSpec as P


def padded(cells, sides, width):
    for axis, dim in sides:
        count = lax.axis_size(axis)
        ends = count - 1
        head = lax.slice_in_dim(cells, 0, width, axis=dim)
        tail = lax.slice_in_dim(cells, cells.shape[dim] - width, cells.shape[dim], axis=dim)
        cells = jnp.concatenate(
            [
                lax.ppermute(tail, axis, [(i, (i + 1) % count) for i in range(ends)]),
                cells,
                lax.ppermute(head, axis, [((i + 1) % count, i) for i in range(ends)]),
            ],
            axis=dim,
        )
    return cells


def partner(block, axis, distance):
    count = lax.axis_size(axis)
    route = []
    for low in range(count):
        high = low | 1 << distance
        if high != low and high < count:
            route += [(low, high), (high, low)]
    return lax.ppermute(block, axis, route)


def on_device(psi, dims, left_env, right_env, shift, mpo_coef, mpo_mask):
    sec_dev, block, states, _ = psi.shape
    w_dev = left_env.shape[0]
    groups = lax.axis_size("mpo")
    places = lax.axis_size(("sec", "rep"))
    total = sec_dev * places
    first_sector = lax.axis_index(("sec", "rep")) * sec_dev
    sectors = first_sector + jnp.arange(sec_dev, dtype=jnp.int32)
    mirrored = total - 1 - sectors
    lanes = jnp.arange(block, dtype=jnp.int32)
    row_keep = lanes[None, :] < dims[sectors][:, None]
    col_keep = lanes[None, :] < dims[mirrored][:, None]
    keep = row_keep[:, :, None, None] & col_keep[:, None, None, :]
    masked = psi * keep.astype(jnp.bfloat16)
    extended = padded(masked, ((("sec", "rep"), 0),), sec_dev)
    position = jnp.arange(sec_dev, dtype=jnp.int32)[None, :] + sec_dev - shift[:, None]
    sources = jnp.take(extended, position.reshape(-1), axis=0).reshape(
        w_dev, sec_dev, block, states, block
    )
    first = jnp.einsum(
        "wkac,wkcsb->wkasb", left_env, sources, preferred_element_type=jnp.float32
    ).astype(jnp.bfloat16)
    picked = right_env
    for bit_number in range(places.bit_length() - 1):
        picked = partner(picked, ("sec", "rep"), bit_number)
    flipped = picked[:, ::-1]
    right_all = lax.all_gather(flipped, "mpo", axis=0, tiled=True)
    coupling = mpo_coef * mpo_mask.astype(jnp.bfloat16)[:, :, None, None]
    channels = right_all.shape[0]
    applied = jnp.zeros((sec_dev, block, states, block), jnp.float32)
    for begin in range(0, channels, 4):
        mixed = jnp.einsum(
            "wvst,wkatb->vkasb",
            coupling[:, begin : begin + 4],
            first,
            preferred_element_type=jnp.float32,
        ).astype(jnp.bfloat16)
        applied = applied + jnp.einsum(
            "vkasc,vkbc->kasb",
            mixed,
            right_all[begin : begin + 4],
            preferred_element_type=jnp.float32,
        )
    applied = applied * keep.astype(jnp.float32)
    summed = lax.psum(applied.astype(jnp.bfloat16), "mpo").astype(jnp.float32)
    share = states // groups
    result = lax.dynamic_slice_in_dim(summed, lax.axis_index("mpo") * share, share, 2)
    return result.astype(jnp.bfloat16)


def solution(mesh):
    return jax.shard_map(
        on_device,
        mesh=mesh,
        in_specs=(
            P(("runs", "sec", "rep"), None, None, None),
            P("runs"),
            P("mpo", ("runs", "sec", "rep"), None, None),
            P("mpo", ("runs", "sec", "rep"), None, None),
            P("mpo"),
            P("mpo", None, None, None),
            P("mpo", None),
        ),
        out_specs=P(("runs", "sec", "rep"), None, "mpo", None),
        check_vma=False,
    )
```

profile of v0, /device:TPU:9, one launch (start us, length us, event | category | flops | bytes accessed | tf_op | source)
XLA Modules:
  0.0 199.8 jit_solution(13800235655971318084)
XLA Ops:
  6.5 0.0 copy-start
  6.5 0.0 copy-start.7
  6.5 0.0 copy-start.6
  6.5 0.0 copy-start.4
  6.5 0.0 all-gather.2.cloned.1.call-start
  6.6 1.4 gather_fusion.1
  8.0 0.1 iota_compare_fusion
  8.1 1.3 gather_fusion
  9.4 0.1 iota_compare_fusion.1
  9.4 0.1 and_convert_fusion
  9.6 1.3 broadcast_multiply_fusion
  10.9 3.8 %collective-permute-start = (bf16[2,128,16,128]{3,2,1,0:T(8,128)(2,1)S(1)}, bf16[2,128,16,128]{3,2,1,0:T(8,128)(2,1)S(1)}, u32[]{:S(2)}, u32[]{:S(2)}) collective-permute-start(bf16[2,128,16,128]{3,2,1,0:T(8,128)(2,1)S(1)} %broadcast_multiply_fusion), channel_id=1, source_target_pairs={{0,1},{1,4},{4,5},{5,8},{8,9},{9,12},{12,13},{2,3},{3,6},{6,7},{7,... | collective-permute-start | bytes 3145736 | tf_op jit(solution)/shard_map/ppermute | solution.py:15
  14.7 1.9 collective-permute-start.1
  16.6 1.9 copy.12
  18.5 0.6 collective-permute-start.2
  19.0 0.0 copy-done.7
  19.0 0.1 broadcast_subtract_fusion
  19.1 0.1 sub.41
  19.2 0.1 compare_and_fusion
  19.3 0.0 copy-done.6
  19.3 0.0 copy-done.4
  19.3 0.2 broadcast_multiply_fusion.1
  19.6 1.3 collective-permute-done.2
  20.9 0.0 collective-permute-start.3
  20.9 5.5 %collective-permute-done = bf16[2,128,16,128]{3,2,1,0:T(8,128)(2,1)S(1)} collective-permute-done((bf16[2,128,16,128]{3,2,1,0:T(8,128)(2,1)S(1)}, bf16[2,128,16,128]{3,2,1,0:T(8,128)(2,1)S(1)}, u32[]{:S(2)}, u32[]{:S(2)}) %collective-permute-start) | collective-permute-done | bytes 1048608 | tf_op jit(solution)/shard_map/ppermute | solution.py:15
  26.4 4.8 %collective-permute-done.1 = bf16[2,128,16,128]{3,2,1,0:T(8,128)(2,1)} collective-permute-done((bf16[2,128,16,128]{3,2,1,0:T(8,128)(2,1)S(1)}, bf16[2,128,16,128]{3,2,1,0:T(8,128)(2,1)}, u32[]{:S(2)}, u32[]{:S(2)}) %collective-permute-start.1) | collective-permute-done | bytes 1048608 | tf_op jit(solution)/shard_map/ppermute | solution.py:17
  31.2 2.9 %pad_maximum_fusion = bf16[6,128,16,128]{3,2,1,0:T(8,128)(2,1)} fusion(bf16[2,128,16,128]{3,2,1,0:T(8,128)(2,1)} %collective-permute-done.1, bf16[2,128,16,128]{3,2,1,0:T(8,128)(2,1)S(1)} %broadcast_multiply_fusion, bf16[2,128,16,128]{3,2,1,0:T(8,128)(2,1)S(1)} %collective-permute-done), kind=kLoop, calls=%fused_computation.20 | loop fusion | flops 3145728 | bytes 6291456 | tf_op jit(solution)/shard_map/concatenate | solution.py:13
  34.1 6.7 %gather_fusion.2 = bf16[16,128,16,128]{3,2,1,0:T(8,128)(2,1)} fusion(bf16[6,128,16,128]{3,2,1,0:T(8,128)(2,1)} %pad_maximum_fusion, s32[1024]{0:T(1024)S(1)} %pad_clamp_fusion), kind=kCustom, calls=%fused_computation.2 | custom fusion | bytes 16777280 | tf_op jit(solution)/shard_map/jit(_take)/gather | solution.py:50
  40.8 12.6 %copy.11 = bf16[8,2,128,16,128]{2,4,3,1,0:T(8,128)(2,1)} copy(bf16[8,2,128,16,128]{4,3,2,1,0:T(8,128)(2,1)} %bitcast.104) | data formatting | bytes 16777216 | tf_op jit(solution)/shard_map/jit(_take)/gather | solution.py:50
  53.4 0.0 copy-done
  53.4 9.0 %convert_bitcast_fusion = bf16[8,2,128,16,128,1]{2,4,3,1,0,5:T(8,128)(2,1)} fusion(bf16[8,2,128,16,128]{2,4,3,1,0:T(8,128)(2,1)} %copy.11, pred[8,2]{1,0:T(8,128)(4,1)S(1)} %compare_and_fusion, bf16[8,2,128,128]{3,2,1,0:T(8,128)(2,1)S(1)} %copy-done), kind=kOutput, calls=%fused_computation.7 | convolution fusion | flops 1082130432 | bytes 17301520 | tf_op jit(solution)/shard_map/wkac,wkcsb->wkasb/dot_general | solution.py:53
  62.5 12.3 %copy.15 = bf16[8,2,128,16,128,1]{4,3,0,5,2,1:T(8,128)(2,1)} copy(bf16[8,2,128,16,128,1]{2,4,3,1,0,5:T(8,128)(2,1)} %convert_bitcast_fusion) | data formatting | bytes 16777216 | tf_op jit(solution)/shard_map/convert_element_type | solution.py:55
  74.7 0.0 copy-start.2
  74.7 5.9 %fusion.25 = bf16[2,128,128,4,16,1]{2,4,5,3,1,0:T(8,128)(2,1)} fusion(bf16[8,2,128,16,128,1]{4,3,0,5,2,1:T(8,128)(2,1)} %copy.15, bf16[8,4,16,16,1,1]{3,2,1,0,4,5:T(8,128)(2,1)S(1)} %get-tuple-element.6), kind=kOutput, calls=%fused_computation.42 | convolution fusion | flops 536870912 | bytes 12599296 | tf_op jit(solution)/shard_map/wvst,wkatb->vkasb/dot_general | solution.py:65
  80.6 0.0 collective-permute-done.3
  80.6 0.0 collective-permute-start.4
  80.6 1.5 copy-done.2
  82.1 2.9 %fusion.29 = bf16[2,128,128,4,16,1]{2,4,5,3,1,0:T(8,128)(2,1)} fusion(bf16[8,2,128,16,128,1]{4,3,0,5,2,1:T(8,128)(2,1)S(1)} %copy-done.2, bf16[8,4,16,16,1,1]{3,2,1,0,4,5:T(8,128)(2,1)S(1)} %get-tuple-element.8), kind=kOutput, calls=%fused_computation.46 | convolution fusion | flops 536870912 | bytes 12599296 | tf_op jit(solution)/shard_map/wvst,wkatb->vkasb/dot_general | solution.py:65
  84.9 17.9 %collective-permute-done.4 = bf16[8,2,128,128]{3,2,0,1:T(8,128)(2,1)S(1)} collective-permute-done((bf16[8,2,128,128]{3,2,0,1:T(8,128)(2,1)}, bf16[8,2,128,128]{3,2,0,1:T(8,128)(2,1)S(1)}, u32[]{:S(2)}, u32[]{:S(2)}) %collective-permute-start.4) | collective-permute-done | bytes 524320 | tf_op jit(solution)/shard_map/ppermute | solution.py:31
  102.8 0.8 rev.3
  103.6 0.0 all-gather.2.cloned.1.call-update
  103.7 0.0 all-reduce.2.cloned.1.call-start
  103.7 5.6 %fusion.27 = bf16[2,128,128,4,16,1]{2,4,5,3,1,0:T(8,128)(2,1)} fusion(bf16[8,2,128,16,128,1]{4,3,0,5,2,1:T(8,128)(2,1)} %copy.15, bf16[8,4,16,16,1,1]{3,2,1,0,4,5:T(8,128)(2,1)S(1)} %get-tuple-element.7), kind=kOutput, calls=%fused_computation.44 | convolution fusion | flops 536870912 | bytes 12599296 | tf_op jit(solution)/shard_map/wvst,wkatb->vkasb/dot_general | solution.py:65
  109.3 5.6 %fusion.23 = bf16[2,128,128,4,16,1]{2,4,5,3,1,0:T(8,128)(2,1)} fusion(bf16[8,2,128,16,128,1]{4,3,0,5,2,1:T(8,128)(2,1)} %copy.15, bf16[8,4,16,16,1,1]{3,2,1,0,4,5:T(8,128)(2,1)S(1)} %get-tuple-element.5), kind=kOutput, calls=%fused_computation.40 | convolution fusion | flops 536870912 | bytes 12599296 | tf_op jit(solution)/shard_map/wvst,wkatb->vkasb/dot_general | solution.py:65
  114.9 12.8 %all-gather.2.cloned.1.call-done = bf16[16,2,128,128]{3,2,0,1:T(8,128)(2,1)} async-done(((bf16[8,2,128,128]{3,2,0,1:T(8,128)(2,1)}), bf16[16,2,128,128]{3,2,0,1:T(8,128)(2,1)}) %all-gather.2.cloned.1.call-update) | async-done | bytes 1048592 | tf_op jit(solution)/shard_map/all_gather | solution.py:60
  127.7 0.0 copy-start.5
  127.7 0.0 copy-start.8
  127.7 7.1 %fusion.12 = f32[2,128,16,128,1]{3,1,4,2,0:T(8,128)S(1)} fusion(bf16[2,128,128,4,16,1]{2,4,5,3,1,0:T(8,128)(2,1)} %fusion.25, bf16[16,2,128,128]{3,2,0,1:T(8,128)(2,1)} %all-gather.2.cloned.1.call-done), kind=kOutput, calls=%fused_computation.16 | convolution fusion | flops 536870912 | bytes 6553600 | tf_op jit(solution)/shard_map/vkasc,vkbc->kasb/dot_general | solution.py:71
  134.8 0.0 copy-done.5
  134.8 0.0 copy-done.8
  134.8 0.0 copy-start.9
  134.8 4.8 %fusion.6 = f32[2,128,16,128,1]{3,1,4,2,0:T(8,128)S(1)} fusion(bf16[2,128,128,4,16,1]{2,4,5,3,1,0:T(8,128)(2,1)S(1)} %copy-done.8, bf16[16,2,128,128]{3,2,0,1:T(8,128)(2,1)S(1)} %copy-done.5), kind=kOutput, calls=%fused_computation.12 | convolution fusion | flops 536870912 | bytes 6553600 | tf_op jit(solution)/shard_map/vkasc,vkbc->kasb/dot_general | solution.py:71
  139.6 0.0 copy-done.9
  139.6 0.0 copy-start.3
  139.6 4.9 %fusion.9 = f32[2,128,16,128,1]{3,1,4,2,0:T(8,128)S(1)} fusion(bf16[2,128,128,4,16,1]{2,4,5,3,1,0:T(8,128)(2,1)S(1)} %copy-done.9, bf16[16,2,128,128]{3,2,0,1:T(8,128)(2,1)S(1)} %copy-done.5), kind=kOutput, calls=%fused_computation.14 | convolution fusion | flops 536870912 | bytes 6553600 | tf_op jit(solution)/shard_map/vkasc,vkbc->kasb/dot_general | solution.py:71
  144.5 0.0 copy-done.3
  144.5 0.0 copy-start.1
  144.5 5.9 %fusion.19 = bf16[2,128,16,128]{3,1,2,0:T(8,128)(2,1)} fusion(f32[2,128,16,128,1]{3,1,4,2,0:T(8,128)S(1)} %fusion.12, f32[2,128,16,128,1]{3,1,4,2,0:T(8,128)S(1)} %fusion.9, f32[2,128,16,128,1]{3,1,4,2,0:T(8,128)S(1)} %fusion.6, bf16[2,128,128,4,16,1]{2,4,5,3,1,0:T(8,128)(2,1)S(1)} %copy-done.3, f32[2,128,128]{2,1,0:T(8,128)S(1)} %get-tuple-element.9, ...), kind=kOutput, calls=%fused_computation.23 | convolution fusion | flops 539492352 | bytes 11927552 | tf_op jit(solution)/shard_map/vkasc,vkbc->kasb/dot_general | solution.py:71
  150.4 0.0 all-reduce.2.cloned.1.call-update
  150.5 40.2 %all-reduce.2.cloned.1.call-done = bf16[2,128,16,128]{3,1,2,0:T(8,128)(2,1)} async-done(((bf16[2,128,16,128]{3,1,2,0:T(8,128)(2,1)}), bf16[2,128,16,128]{3,1,2,0:T(8,128)(2,1)}) %all-reduce.2.cloned.1.call-update) | async-done | bytes 1048592 | tf_op jit(solution)/shard_map/psum | solution.py:78
  190.7 1.1 convert_convert_fusion
  191.8 1.1 copy.13
  192.9 0.0 copy-done.1
  (8 shorter events, 0.1 us)
Async XLA Ops:
  6.5 46.9 %copy-start = (bf16[8,2,128,128]{3,2,1,0:T(8,128)(2,1)S(1)}, bf16[8,2,128,128]{3,2,1,0:T(8,128)(2,1)}, u32[]{:S(2)}) copy-start(bf16[8,2,128,128]{3,2,1,0:T(8,128)(2,1)} %param.9) | copy-start | bytes 1572868
  6.5 12.5 %copy-start.7 = (s32[8]{0:T(128)S(1)}, s32[8]{0:T(128)}, u32[]{:S(2)}) copy-start(s32[8]{0:T(128)} %param.11) | copy-start | bytes 100
  6.5 12.8 %copy-start.6 = (s32[8,16]{1,0:T(8,128)S(1)}, s32[8,16]{1,0:T(8,128)}, u32[]{:S(2)}) copy-start(s32[8,16]{1,0:T(8,128)} %param.13) | copy-start | bytes 1540
  6.5 12.8 %copy-start.4 = (bf16[8,16,16,16]{3,2,1,0:T(8,128)(2,1)S(1)}, bf16[8,16,16,16]{3,2,1,0:T(8,128)(2,1)}, u32[]{:S(2)}) copy-start(bf16[8,16,16,16]{3,2,1,0:T(8,128)(2,1)} %param.12) | copy-start | bytes 196612
  6.5 121.1 %all-gather.2.cloned.1.call-start = ((), (), s32[]{:S(2)}) async-start(), calls=%async_computation | async-start | bytes 1572864 | tf_op jit(solution)/shard_map/all_gather | solution.py:60
  10.9 15.5 %collective-permute-start = (bf16[2,128,16,128]{3,2,1,0:T(8,128)(2,1)S(1)}, bf16[2,128,16,128]{3,2,1,0:T(8,128)(2,1)S(1)}, u32[]{:S(2)}, u32[]{:S(2)}) collective-permute-start(bf16[2,128,16,128]{3,2,1,0:T(8,128)(2,1)S(1)} %broadcast_multiply_fusion), channel_id=1, source_target_pairs={{0,1},{1,4},{4,5},{5,8},{8,9},{9,12},{12,13},{2,3},{3,6},{6,7},{7,... | collective-permute-start | bytes 3145736 | tf_op jit(solution)/shard_map/ppermute | solution.py:15
  14.7 16.5 %collective-permute-start.1 = (bf16[2,128,16,128]{3,2,1,0:T(8,128)(2,1)S(1)}, bf16[2,128,16,128]{3,2,1,0:T(8,128)(2,1)}, u32[]{:S(2)}, u32[]{:S(2)}) collective-permute-start(bf16[2,128,16,128]{3,2,1,0:T(8,128)(2,1)S(1)} %broadcast_multiply_fusion), channel_id=1, source_target_pairs={{1,0},{4,1},{5,4},{8,5},{9,8},{12,9},{13,12},{3,2},{6,3},{7,6},{10... | collective-permute-start | bytes 3145736 | tf_op jit(solution)/shard_map/ppermute | solution.py:17
  18.5 2.4 %collective-permute-start.2 = (bf16[8,2,128,128]{3,2,0,1:T(8,128)(2,1)}, bf16[8,2,128,128]{3,2,0,1:T(8,128)(2,1)}, u32[]{:S(2)}, u32[]{:S(2)}) collective-permute-start(bf16[8,2,128,128]{3,2,0,1:T(8,128)(2,1)} %copy.12), channel_id=1, source_target_pairs={{0,1},{1,0},{4,5},{5,4},{8,9},{9,8},{12,13},{13,12},{2,3},{3,2},{6... | collective-permute-start | bytes 1572872 | tf_op jit(solution)/shard_map/ppermute | solution.py:31
  20.9 59.7 %collective-permute-start.3 = (bf16[8,2,128,128]{3,2,0,1:T(8,128)(2,1)}, bf16[8,2,128,128]{3,2,0,1:T(8,128)(2,1)}, u32[]{:S(2)}, u32[]{:S(2)}) collective-permute-start(bf16[8,2,128,128]{3,2,0,1:T(8,128)(2,1)} %collective-permute-done.2), channel_id=1, source_target_pairs={{0,4},{4,0},{1,5},{5,1},{8,12},{12,8},{9,13},{13,9},{2,6},{6,2},{3... | collective-permute-start | bytes 1572872 | tf_op jit(solution)/shard_map/ppermute | solution.py:31
  74.7 7.3 %copy-start.2 = (bf16[8,2,128,16,128,1]{4,3,0,5,2,1:T(8,128)(2,1)S(1)}, bf16[8,2,128,16,128,1]{4,3,0,5,2,1:T(8,128)(2,1)}, u32[]{:S(2)}) copy-start(bf16[8,2,128,16,128,1]{4,3,0,5,2,1:T(8,128)(2,1)} %copy.15) | copy-start | bytes 25165828
  80.6 22.2 %collective-permute-start.4 = (bf16[8,2,128,128]{3,2,0,1:T(8,128)(2,1)}, bf16[8,2,128,128]{3,2,0,1:T(8,128)(2,1)S(1)}, u32[]{:S(2)}, u32[]{:S(2)}) collective-permute-start(bf16[8,2,128,128]{3,2,0,1:T(8,128)(2,1)} %collective-permute-done.3), channel_id=1, source_target_pairs={{0,8},{8,0},{1,9},{9,1},{4,12},{12,4},{5,13},{13,5},{2,10},{10,2},... | collective-permute-start | bytes 1572872 | tf_op jit(solution)/shard_map/ppermute | solution.py:31
  103.7 87.0 %all-reduce.2.cloned.1.call-start = ((), (), s32[]{:S(2)}) async-start(), calls=%async_computation.1 | async-start | bytes 2097152 | tf_op jit(solution)/shard_map/psum | solution.py:78
  127.7 7.1 %copy-start.5 = (bf16[16,2,128,128]{3,2,0,1:T(8,128)(2,1)S(1)}, bf16[16,2,128,128]{3,2,0,1:T(8,128)(2,1)}, u32[]{:S(2)}) copy-start(bf16[16,2,128,128]{3,2,0,1:T(8,128)(2,1)} %all-gather.2.cloned.1.call-done) | copy-start | bytes 3145732
  127.7 7.1 %copy-start.8 = (bf16[2,128,128,4,16,1]{2,4,5,3,1,0:T(8,128)(2,1)S(1)}, bf16[2,128,128,4,16,1]{2,4,5,3,1,0:T(8,128)(2,1)}, u32[]{:S(2)}) copy-start(bf16[2,128,128,4,16,1]{2,4,5,3,1,0:T(8,128)(2,1)} %fusion.29) | copy-start | bytes 12582916
  134.8 4.8 %copy-start.9 = (bf16[2,128,128,4,16,1]{2,4,5,3,1,0:T(8,128)(2,1)S(1)}, bf16[2,128,128,4,16,1]{2,4,5,3,1,0:T(8,128)(2,1)}, u32[]{:S(2)}) copy-start(bf16[2,128,128,4,16,1]{2,4,5,3,1,0:T(8,128)(2,1)} %fusion.27) | copy-start | bytes 12582916
  139.6 4.9 %copy-start.3 = (bf16[2,128,128,4,16,1]{2,4,5,3,1,0:T(8,128)(2,1)S(1)}, bf16[2,128,128,4,16,1]{2,4,5,3,1,0:T(8,128)(2,1)}, u32[]{:S(2)}) copy-start(bf16[2,128,128,4,16,1]{2,4,5,3,1,0:T(8,128)(2,1)} %fusion.23) | copy-start | bytes 12582916
  144.5 48.4 %copy-start.1 = (bf16[8,2,128,128]{3,2,1,0:T(8,128)(2,1)S(1)}, bf16[8,2,128,128]{3,2,1,0:T(8,128)(2,1)}, u32[]{:S(2)}) copy-start(bf16[8,2,128,128]{3,2,1,0:T(8,128)(2,1)} %param.9) | copy-start | bytes 1572868
Sparse Core Ops, SparseCore 0:
  103.8 23.8 all-gather.1
  150.6 40.0 all-reduce.1
where the time goes:
time: 202 us; the launch traced here: 200 us
  waiting for transfers between devices  82.5 us (41%)
  matrix products  51.6 us (26%)
  local copies, waits for them, and re-layouts  39.7 us (20%)
  between operations  13.6 us (7%)
  starting transfers between devices  6.32 us (3%)
  other arithmetic  5.97 us (3%)
    psum x1, waiting for transfers between devices, on_device(): summed = lax.psum(applied.astype(jnp.bfloat16), 'mpo').astype(jnp.float32)  40.2 us
    dot_general x4, matrix products, on_device(): jnp.einsum('vkasc,vkbc->kasb', mixed, right_all[begin:begin + 4], preferr...  22.7 us
    dot_general x4, matrix products, on_device(): jnp.einsum('wvst,wkatb->vkasb', coupling[:, begin:begin + 4], first, pref...  19.9 us
    gather x2, local copies, waits for them, and re-layouts, on_device(): jnp.take(extended, position.reshape(-1), axis=0)  19.3 us
    ppermute x3, waiting for transfers between devices, partner(): return lax.ppermute(block, axis, route)  19.2 us
    all_gather x1, waiting for transfers between devices, on_device(): right_all = lax.all_gather(flipped, 'mpo', axis=0, tiled=True)  12.8 us
    convert_element_type x1, local copies, waits for them, and re-layouts, on_device(): first = jnp.einsum('wkac,wkcsb->wkasb', left_env, sources, preferred_elem...  12.3 us
    dot_general x1, matrix products, on_device(): jnp.einsum('wkac,wkcsb->wkasb', left_env, sources, preferred_element_type...  9.03 us
  transfers between devices with their start and end apart: 7, of which 6 were waited for; matrix products, arithmetic and copies ran while one was open for 33% of the time, Pallas kernels for 0%

commit v1 on v0

v1 whole, which is shorter than its diff:
```python
import functools

import jax
import jax.numpy as jnp
from jax import lax
from jax.experimental import pallas as pl
from jax.experimental.pallas import tpu as pltpu
from jax.sharding import PartitionSpec as P

F32 = jnp.float32
BF16 = jnp.bfloat16
VMEM = pltpu.VMEM
SMEM = pltpu.SMEM
PAD = 1


def ring(block, axis, step):
    count = lax.axis_size(axis)
    return lax.ppermute(block, axis, [((i + step) % count, i) for i in range(count)])


def mix_kernel(entry, info, dims, shift, own, near, far, left_own, *rest):
    *left_other, coupling, mixed, turned, first, plane = rest
    lefts = [left_own, *left_other]
    _, block, states, width = own.shape
    w_dev = left_own.shape[0]
    place = info[0]
    places = info[1]
    first_sector = place * 2
    sector = first_sector + entry
    rows = lax.broadcasted_iota(jnp.int32, (block, width), 0)
    lanes = lax.broadcasted_iota(jnp.int32, (block, width), 1)
    near_place = place + 1 - 2 * lax.rem(place, 2)
    far_place = place - 1 + 2 * lax.rem(place, 2)
    for which, (ref, home) in enumerate(((own, place), (near, near_place), (far, far_place))):
        for e in range(2):
            source = jnp.clip(home * 2 + e, 0, 2 * places - 1)
            keep = (rows < dims[source]) & (lanes < dims[2 * places - 1 - source])
            plane[...] = ref[e].astype(F32).reshape(block * states, width)
            for t in range(states):
                piece = plane[pl.ds(t, block, stride=states), :]
                turned[which * 2 + e, :, t * width : (t + 1) * width] = jnp.where(
                    keep, piece, 0.0
                ).astype(BF16)
    step = block + PAD

    for j, left in enumerate(lefts):

        def stage1(w, carry, j=j, left=left):
            source = sector - shift[j * w_dev + w]
            at = source >> 1
            which = jnp.where(at == place, 0, jnp.where(at == near_place, 1, 2))
            slot = which * 2 + (source & 1)
            matrix = left[w, entry]
            for t in range(0, states, 2):
                product = jnp.dot(
                    matrix,
                    turned[slot, :, t * width : (t + 2) * width],
                    preferred_element_type=F32,
                )
                for h in range(2):
                    row = ((j * w_dev + w) * states + t + h) * step
                    first[pl.ds(row, block), :] = product[:, h * width : (h + 1) * width]
            return carry

        lax.fori_loop(0, w_dev, stage1, 0)

    inner = len(lefts) * w_dev * states
    outer = coupling.shape[0]
    channels = outer // 8

    def stage2(i, carry):
        for u in range(4):
            a = i * 8 + u * 2
            pair = [first[pl.ds(a + h, inner, stride=step), :].astype(BF16) for h in range(2)]
            product = jnp.dot(
                coupling[...], jnp.concatenate(pair, axis=1), preferred_element_type=F32
            )
            halves = [
                product[:, h * width : (h + 1) * width].reshape(channels, 1, 8, width)
                for h in range(2)
            ]
            both = jnp.concatenate(halves, axis=1).reshape(channels, 16, width).astype(BF16)
            for v in range(channels):
                mixed[pl.ds(pl.multiple_of(a * 8, 16), 16), v * width : (v + 1) * width] = both[v]
        return carry

    lax.fori_loop(0, block // 8, stage2, 0)


def mix(entry, info, dims, shift, psis, lefts, coupling):
    _, block, states, width = psis[0].shape
    channels = coupling.shape[0] // 8
    inner = coupling.shape[1]
    return pl.pallas_call(
        functools.partial(mix_kernel, entry),
        out_shape=jax.ShapeDtypeStruct((block * 8, channels * width), BF16),
        in_specs=[pl.BlockSpec(memory_space=SMEM)] * 3
        + [pl.BlockSpec(memory_space=VMEM)] * (len(psis) + len(lefts) + 1),
        out_specs=pl.BlockSpec(memory_space=VMEM),
        scratch_shapes=[
            VMEM((6, block, states * width), BF16),
            VMEM((inner * (block + PAD), width), F32),
            VMEM((block * states, width), F32),
        ],
        compiler_params=pltpu.CompilerParams(vmem_limit_bytes=(36 if inner <= 256 else 60) << 20),
        cost_estimate=pl.CostEstimate(
            flops=2 * inner * block * width * (block + channels * 8),
            bytes_accessed=8 << 20,
            transcendentals=0,
        ),
        name=f"mix_{entry}",
    )(info, dims, shift, *psis, *lefts, coupling)


def apply_kernel(entry, info, dims, mixed, *rest):
    n = mixed.shape[1] // (rest[0].shape[0] * rest[0].shape[2])
    rights = rest[:n]
    out = rest[-1]
    v_dev, width, depth = rights[0].shape
    block = out.shape[1]
    place, places, group = info[0], info[1], info[2]
    total = jnp.zeros((block * 8, width), F32)
    for j, right in enumerate(rights):
        where = lax.rem(group + j, len(rights)) * v_dev
        for v in range(0, v_dev, 2):
            column = pl.multiple_of((where + v) * depth, 2 * depth)
            weights = jnp.concatenate([right[v], right[v + 1]], axis=1)
            total += lax.dot_general(
                mixed[:, pl.ds(column, 2 * depth)],
                weights,
                (((1,), (1,)), ((), ())),
                preferred_element_type=F32,
            )
    sector = place * 2 + entry
    cube = (block, 8, width)
    keep = (lax.broadcasted_iota(jnp.int32, cube, 0) < dims[sector]) & (
        lax.broadcasted_iota(jnp.int32, cube, 2) < dims[2 * places - 1 - sector]
    )
    out[0] = jnp.where(keep, total.reshape(cube), 0.0).astype(BF16)


def apply(entry, info, dims, mixed, rights, before, width):
    block = mixed.shape[0] // 8
    out_shape = jax.ShapeDtypeStruct((2, block, 8, width), BF16)
    whole = lambda a: pl.BlockSpec(a.shape, lambda i, n=a.ndim: (0,) * n)
    return pl.pallas_call(
        functools.partial(apply_kernel, entry),
        grid=(1,),
        out_shape=out_shape,
        in_specs=[pl.BlockSpec(memory_space=SMEM)] * 2
        + [whole(mixed)]
        + [whole(r) for r in rights]
        + [pl.BlockSpec(memory_space=pl.ANY)] * len(before),
        out_specs=pl.BlockSpec((1, block, 8, width), lambda i: (entry, 0, 0, 0)),
        input_output_aliases={3 + len(rights): 0} if before else {},
        compiler_params=pltpu.CompilerParams(vmem_limit_bytes=32 << 20),
        cost_estimate=pl.CostEstimate(
            flops=2 * mixed.size * width, bytes_accessed=6 << 20, transcendentals=0
        ),
        name=f"apply_{entry}",
    )(info, dims, mixed, *rights, *before)


def on_device(psi, dims, left_env, right_env, shift, mpo_coef, mpo_mask):
    sec_dev, block, states, width = psi.shape
    w_dev = left_env.shape[0]
    groups = lax.axis_size("mpo")
    spots = ("sec", "rep")
    places = lax.axis_size(spots)
    place = lax.axis_index(spots)
    group = lax.axis_index("mpo")
    info = jnp.stack([place, jnp.int32(places), group]).astype(jnp.int32)
    share = states // groups

    def swap(block, begin):
        route = []
        for low in range(begin, places - 1, 2):
            route += [(low, low + 1), (low + 1, low)]
        return lax.ppermute(block, spots, route)

    far = swap(psi, 1)
    near = swap(psi, 0)
    lefts = [left_env] + [ring(left_env, "mpo", j) for j in range(1, groups)]
    mirror = [(i, places - 1 - i) for i in range(places)]
    coupling = mpo_coef * mpo_mask.astype(BF16)[:, :, None, None]
    channels = coupling.shape[1]
    packed = jnp.transpose(coupling, (1, 2, 0, 3)).reshape(channels, states, w_dev * states)
    offsets = jnp.broadcast_to(
        jnp.pad(shift, (0, w_dev * states - w_dev)).astype(BF16), (1, states, w_dev * states)
    )
    packed = jnp.concatenate([packed, offsets], axis=0)
    parcels = [packed] + [ring(packed, "mpo", j) for j in range(1, groups)]
    shifts = jnp.concatenate([p[channels, 0, :w_dev] for p in parcels]).astype(jnp.int32)
    begin = (group * share) // 8 * 8
    matrix = jnp.concatenate(
        [lax.dynamic_slice_in_dim(p[:channels], begin, 8, 1) for p in parcels], axis=2
    ).reshape(channels * 8, groups * w_dev * states)
    psis = [psi, near, far]
    result = ()
    for entry in range(sec_dev):
        chunk = lax.ppermute(right_env[:, sec_dev - 1 - entry], spots, mirror)
        rights = [chunk] + [ring(chunk, "mpo", j) for j in range(1, groups)]
        mixed = mix(entry, info, dims, shifts, psis, lefts, matrix)
        result = (apply(entry, info, dims, mixed, rights, result, width),)
    result = result[0]
    if share != 8:
        result = lax.dynamic_slice_in_dim(result, group * share - begin, share, 2)
    return result


def solution(mesh):
    return jax.shard_map(
        on_device,
        mesh=mesh,
        in_specs=(
            P(("runs", "sec", "rep"), None, None, None),
            P("runs"),
            P("mpo", ("runs", "sec", "rep"), None, None),
            P("mpo", ("runs", "sec", "rep"), None, None),
            P("mpo"),
            P("mpo", None, None, None),
            P("mpo", None),
        ),
        out_specs=P(("runs", "sec", "rep"), None, "mpo", None),
        check_vma=False,
    )
```

time: 202 us -> 73.6 us (0.36)
  waiting for transfers between devices: 82.5 us -> 22.4 us
  matrix products: 51.6 us -> 0 us
  local copies, waits for them, and re-layouts: 39.7 us -> 7.02 us
  Pallas kernels: 0 us -> 31.4 us
  between operations: 13.6 us -> 0.1 us
  other arithmetic: 5.97 us -> 2.76 us
  starting transfers between devices: 6.32 us -> 9.48 us
    dot_general x9 -> x0, matrix products: 51.6 us -> none  [the longest x4 22.7 us: on_device(): jnp.einsum('vkasc,vkbc->kasb', mixed, right_all[begin:begin + 4], preferr...]
    psum x1 -> x0, waiting for transfers between devices: 40.2 us -> none  [on_device(): summed = lax.psum(applied.astype(jnp.bfloat16), 'mpo').astype(jnp.float32)]
    pallas_call x0 -> x4, Pallas kernels: none -> 31.4 us  [the longest x2 26.4 us: mix(): pl.pallas_call(functools.partial(mix_kernel, entry), out_shape=jax.ShapeD...]
    gather x4 -> x0, local copies, waits for them, and re-layouts: 22 us -> none  [the longest x2 19.3 us: on_device(): jnp.take(extended, position.reshape(-1), axis=0)]
    convert_element_type x2 -> x0, local copies, waits for them, and re-layouts: 13.4 us -> none  [the longest x1 12.3 us: on_device(): first = jnp.einsum('wkac,wkcsb->wkasb', left_env, sources, preferred_elem...]
    all_gather x1 -> x0, waiting for transfers between devices: 12.8 us -> none  [on_device(): right_all = lax.all_gather(flipped, 'mpo', axis=0, tiled=True)]
    ppermute x5 -> x8, waiting for transfers between devices: 29.5 us -> 22.4 us  [the longest x2 22.4 us: on_device(): chunk = lax.ppermute(right_env[:, sec_dev - 1 - entry], spots, mirror)]
    ppermute x5 -> x8, starting transfers between devices: 6.24 us -> 9.48 us  [the longest x2 3.9 us: swap(): return lax.ppermute(block, spots, route)]
  transfers between devices with their start and end apart: 7 -> 8, of which waited for: 6 -> 2; matrix products, arithmetic and copies ran while one was open for 33% -> 12% of each run, Pallas kernels for 0% -> 39%
where the time goes in v1:
time: 73.6 us; the launch traced here: 73.2 us
  Pallas kernels  31.4 us (43%)
  waiting for transfers between devices  22.4 us (30%)
  starting transfers between devices  9.48 us (13%)
  local copies, waits for them, and re-layouts  7.02 us (10%)
  other arithmetic  2.76 us (4%)
    pallas_call x2, Pallas kernels, mix(): pl.pallas_call(functools.partial(mix_kernel, entry), out_shape=jax.ShapeD...  26.4 us
    ppermute x2, waiting for transfers between devices, on_device(): chunk = lax.ppermute(right_env[:, sec_dev - 1 - entry], spots, mirror)  22.4 us
    pallas_call x2, Pallas kernels, apply(): pl.pallas_call(functools.partial(apply_kernel, entry), grid=(1,), out_sha...  5 us
    ppermute x2, starting transfers between devices, swap(): return lax.ppermute(block, spots, route)  3.9 us
    ppermute x4, starting transfers between devices, ring(): lax.ppermute(block, axis, [((i + step) % count, i) for i in range(count)])  3.73 us
    squeeze x1, local copies, waits for them, and re-layouts, on_device(): chunk = lax.ppermute(right_env[:, sec_dev - 1 - entry], spots, mirror)  1.87 us
    ppermute x2, starting transfers between devices, on_device(): chunk = lax.ppermute(right_env[:, sec_dev - 1 - entry], spots, mirror)  1.84 us
  transfers between devices with their start and end apart: 8, of which 2 were waited for; matrix products, arithmetic and copies ran while one was open for 12% of the time, Pallas kernels for 39%

profile of v1, /device:TPU:9, one launch (start us, length us, event | category | flops | bytes accessed | tf_op | source)
XLA Modules:
  0.0 73.2 jit_solution(12392807264277530287)
XLA Ops:
  0.0 0.0 copy-start
  0.0 0.0 copy-start.2
  0.0 0.7 collective-permute-start.1
  0.7 3.2 %collective-permute-start.2 = (bf16[2,128,16,128]{3,2,1,0:T(8,128)(2,1)}, bf16[2,128,16,128]{3,2,1,0:T(8,128)(2,1)S(1)}, u32[]{:S(2)}, u32[]{:S(2)}) collective-permute-start(bf16[2,128,16,128]{3,2,1,0:T(8,128)(2,1)} %own.3), channel_id=1, source_target_pairs={{1,4},{4,1},{5,8},{8,5},{9,12},{12,9},{3,6},{6,3},{7,10},{10,7},{1... | collective-permute-start | bytes 3145736 | tf_op jit(solution)/shard_map/ppermute | solution.py:180
  3.9 0.7 convert_element_type.7
  4.6 1.2 %multiply_bitcast_fusion = bf16[16,16,8,16]{3,1,0,2:T(8,128)(2,1)S(1)} fusion(bf16[8,16,16,16]{3,2,1,0:T(8,128)(2,1)} %param.12, bf16[8,16]{1,0:T(8,128)(2,1)S(1)} %convert_element_type.7), kind=kLoop, calls=%fused_computation | loop fusion | flops 32768 | bytes 131328 | tf_op jit(solution)/shard_map/transpose | solution.py:188
  5.9 1.1 %copy.11 = bf16[16,16,8,16]{3,2,1,0:T(8,128)(2,1)} copy(bf16[16,16,8,16]{3,1,0,2:T(8,128)(2,1)S(1)} %multiply_bitcast_fusion) | data formatting | bytes 131072 | tf_op jit(solution)/shard_map/transpose | solution.py:188
  7.0 1.4 %reshape.7 = bf16[16,16,128]{2,1,0:T(8,128)(2,1)S(1)} reshape(bf16[16,16,8,16]{3,2,1,0:T(8,128)(2,1)} %copy.11) | data formatting | bytes 131072 | tf_op jit(solution)/shard_map/reshape | solution.py:188
  8.4 0.7 slice.16
  9.1 1.3 %collective-permute-start = (bf16[17,16,128]{2,1,0:T(8,128)(2,1)S(1)}, bf16[17,16,128]{2,1,0:T(8,128)(2,1)}, u32[]{:S(2)}, u32[]{:S(2)}) collective-permute-start(bf16[17,16,128]{2,1,0:T(8,128)(2,1)S(1)} %pad_maximum_fusion), channel_id=1, source_target_pairs={{2,0},{0,2},{3,1},{1,3},{6,4},{4,6},{7,5},{5,7},{10,8},{8,10},{11,... | collective-permute-start | bytes 208904 | tf_op jit(solution)/shard_map/ppermute | solution.py:19
  10.4 0.3 collective-permute-start.3
  10.6 1.9 %slice_bitcast_fusion = (bf16[8,128,128]{2,1,0:T(8,128)(2,1)}, bf16[8,128,128]{2,1,0:T(8,128)(2,1)}) fusion(bf16[8,2,128,128]{3,2,1,0:T(8,128)(2,1)} %param.10), kind=kLoop, calls=%fused_computation.1 | loop fusion | bytes 1048576 | tf_op jit(solution)/shard_map/squeeze | solution.py:202
  12.5 1.0 %collective-permute-start.6 = (bf16[8,128,128]{2,1,0:T(8,128)(2,1)}, bf16[8,128,128]{2,1,0:T(8,128)(2,1)S(1)}, u32[]{:S(2)}, u32[]{:S(2)}) collective-permute-start(bf16[8,128,128]{2,1,0:T(8,128)(2,1)} %get-tuple-element.5), channel_id=1, source_target_pairs={{0,13},{1,12},{4,9},{5,8},{8,5},{9,4},{12,1},{13,0},{2,15},{3,14},... | collective-permute-start | bytes 786440 | tf_op jit(solution)/shard_map/ppermute | solution.py:202
  13.5 0.1 pad_add_fusion.info
  13.6 0.0 collective-permute-done
  13.6 0.9 %collective-permute-start.4 = (bf16[8,128,128]{2,1,0:T(8,128)(2,1)}, bf16[8,128,128]{2,1,0:T(8,128)(2,1)S(1)}, u32[]{:S(2)}, u32[]{:S(2)}) collective-permute-start(bf16[8,128,128]{2,1,0:T(8,128)(2,1)} %get-tuple-element.6), channel_id=1, source_target_pairs={{0,13},{1,12},{4,9},{5,8},{8,5},{9,4},{12,1},{13,0},{2,15},{3,14},... | collective-permute-start | bytes 786440 | tf_op jit(solution)/shard_map/ppermute | solution.py:202
  14.4 0.7 slice_bitcast_fusion.2
  15.1 0.8 %slice.22 = bf16[16,16,128]{2,1,0:T(8,128)(2,1)S(1)} slice(bf16[17,16,128]{2,1,0:T(8,128)(2,1)} %collective-permute-done), slice={[0:16], [0:16], [0:128]} | slice | bytes 131072 | tf_op jit(solution)/shard_map/slice | solution.py:197
  16.0 20.8 %collective-permute-done.6.rest_0_ = bf16[8,128,128]{2,1,0:T(8,128)(2,1)S(1)} collective-permute-done((bf16[8,128,128]{2,1,0:T(8,128)(2,1)}, bf16[8,128,128]{2,1,0:T(8,128)(2,1)S(1)}, u32[]{:S(2)}, u32[]{:S(2)}) %collective-permute-start.6) | collective-permute-done | bytes 262176 | tf_op jit(solution)/shard_map/ppermute | solution.py:202
  36.8 1.0 %collective-permute-start.7 = (bf16[8,128,128]{2,1,0:T(8,128)(2,1)S(1)}, bf16[8,128,128]{2,1,0:T(8,128)(2,1)S(1)}, u32[]{:S(2)}, u32[]{:S(2)}) collective-permute-start(bf16[8,128,128]{2,1,0:T(8,128)(2,1)S(1)} %collective-permute-done.6.rest_0_), channel_id=1, source_target_pairs={{2,0},{0,2},{3,1},{1,3},{6,4},{4,6},{7,5},{5,7},{10,8},{8,10},{11,... | collective-permute-start | bytes 786440 | tf_op jit(solution)/shard_map/ppermute | solution.py:19
  37.8 0.1 maximum_convert_fusion.shift
  37.8 1.6 %collective-permute-done.4.rest_0_ = bf16[8,128,128]{2,1,0:T(8,128)(2,1)S(1)} collective-permute-done((bf16[8,128,128]{2,1,0:T(8,128)(2,1)}, bf16[8,128,128]{2,1,0:T(8,128)(2,1)S(1)}, u32[]{:S(2)}, u32[]{:S(2)}) %collective-permute-start.4) | collective-permute-done | bytes 262176 | tf_op jit(solution)/shard_map/ppermute | solution.py:202
  39.5 1.2 %collective-permute-start.5 = (bf16[8,128,128]{2,1,0:T(8,128)(2,1)S(1)}, bf16[8,128,128]{2,1,0:T(8,128)(2,1)S(1)}, u32[]{:S(2)}, u32[]{:S(2)}) collective-permute-start(bf16[8,128,128]{2,1,0:T(8,128)(2,1)S(1)} %collective-permute-done.4.rest_0_), channel_id=1, source_target_pairs={{2,0},{0,2},{3,1},{1,3},{6,4},{4,6},{7,5},{5,7},{10,8},{8,10},{11,... | collective-permute-start | bytes 786440 | tf_op jit(solution)/shard_map/ppermute | solution.py:19
  40.7 0.0 collective-permute-done.3.rest_0_
  40.7 0.0 collective-permute-done.1.near
  40.7 0.0 collective-permute-done.2.far
  40.7 0.0 copy-done
  40.7 0.0 copy-done.2
  40.7 0.0 copy-start.1
  40.7 1.0 %copy-done.1 = bf16[8,2,128,128]{3,2,1,0:T(8,128)(2,1)S(1)} copy-done((bf16[8,2,128,128]{3,2,1,0:T(8,128)(2,1)S(1)}, bf16[8,2,128,128]{3,2,1,0:T(8,128)(2,1)}, u32[]{:S(2)}) %copy-start.1) | copy-done | bytes 524312
  41.8 13.2 %mix_0.1.mixed = bf16[1024,2048]{1,0:T(8,128)(2,1)S(1)} custom-call(s32[3]{0:T(128)S(1)} %pad_add_fusion.info, s32[16]{0:T(128)S(1)} %copy-done.2, s32[16]{0:T(128)S(1)} %maximum_convert_fusion.shift, bf16[2,128,16,128]{3,2,1,0:T(8,128)(2,1)S(1)} %copy-done, bf16[2,128,16,128]{3,2,1,0:T(8,128)(2,1)S(1)} %collective-permute-done.1.near, ...), custom_call_target="tpu_custom_call" | custom-call | flops 2147483648 | bytes 8388608 | tf_op jit(solution)/shard_map/mix_0/pallas_call | solution.py:95
  54.9 0.0 collective-permute-done.7.rest_1_
  55.0 2.5 %apply_0.1.rest_2_ = bf16[2,128,8,128]{3,2,1,0:T(8,128)(2,1)} custom-call(s32[3]{0:T(128)S(1)} %pad_add_fusion.info, s32[16]{0:T(128)S(1)} %copy-done.2, bf16[1024,2048]{1,0:T(8,128)(2,1)S(1)} %mix_0.1.mixed, bf16[8,128,128]{2,1,0:T(8,128)(2,1)S(1)} %collective-permute-done.6.rest_0_, bf16[8,128,128]{2,1,0:T(8,128)(2,1)S(1)} %collective-permute-done.7.rest_1_), custom_call_target="tpu_custom_call" | custom-call | flops 536870912 | bytes 6291456 | tf_op jit(solution)/shard_map/apply_0/pallas_call | solution.py:147
  57.5 13.2 %mix_1.1.mixed = bf16[1024,2048]{1,0:T(8,128)(2,1)S(1)} custom-call(s32[3]{0:T(128)S(1)} %pad_add_fusion.info, s32[16]{0:T(128)S(1)} %copy-done.2, s32[16]{0:T(128)S(1)} %maximum_convert_fusion.shift, bf16[2,128,16,128]{3,2,1,0:T(8,128)(2,1)S(1)} %copy-done, bf16[2,128,16,128]{3,2,1,0:T(8,128)(2,1)S(1)} %collective-permute-done.1.near, ...), custom_call_target="tpu_custom_call" | custom-call | flops 2147483648 | bytes 8388608 | tf_op jit(solution)/shard_map/mix_1/pallas_call | solution.py:95
  70.6 0.0 collective-permute-done.5.rest_1_
  70.7 2.5 %apply_1.1 = bf16[2,128,8,128]{3,2,1,0:T(8,128)(2,1)} custom-call(s32[3]{0:T(128)S(1)} %pad_add_fusion.info, s32[16]{0:T(128)S(1)} %copy-done.2, bf16[1024,2048]{1,0:T(8,128)(2,1)S(1)} %mix_1.1.mixed, bf16[8,128,128]{2,1,0:T(8,128)(2,1)S(1)} %collective-permute-done.4.rest_0_, ...), custom_call_target="tpu_custom_call", output_to_operand_aliasing={{}: (5, {})} | custom-call | flops 536870912 | bytes 6291456 | tf_op jit(solution)/shard_map/apply_1/pallas_call | solution.py:147
  (6 shorter events, 0.0 us)
Async XLA Ops:
  0.0 40.7 %copy-start = (bf16[2,128,16,128]{3,2,1,0:T(8,128)(2,1)S(1)}, bf16[2,128,16,128]{3,2,1,0:T(8,128)(2,1)}, u32[]{:S(2)}) copy-start(bf16[2,128,16,128]{3,2,1,0:T(8,128)(2,1)} %own.3) | copy-start | bytes 3145732
  0.0 40.7 %copy-start.2 = (s32[16]{0:T(128)S(1)}, s32[16]{0:T(128)}, u32[]{:S(2)}) copy-start(s32[16]{0:T(128)} %dims.7) | copy-start | bytes 196
  0.0 40.7 %collective-permute-start.1 = (bf16[2,128,16,128]{3,2,1,0:T(8,128)(2,1)}, bf16[2,128,16,128]{3,2,1,0:T(8,128)(2,1)S(1)}, u32[]{:S(2)}, u32[]{:S(2)}) collective-permute-start(bf16[2,128,16,128]{3,2,1,0:T(8,128)(2,1)} %own.3), channel_id=1, source_target_pairs={{0,1},{1,0},{4,5},{5,4},{8,9},{9,8},{12,13},{13,12},{2,3},{3,2},{6... | collective-permute-start | bytes 3145736 | tf_op jit(solution)/shard_map/ppermute | solution.py:180
  0.7 40.0 %collective-permute-start.2 = (bf16[2,128,16,128]{3,2,1,0:T(8,128)(2,1)}, bf16[2,128,16,128]{3,2,1,0:T(8,128)(2,1)S(1)}, u32[]{:S(2)}, u32[]{:S(2)}) collective-permute-start(bf16[2,128,16,128]{3,2,1,0:T(8,128)(2,1)} %own.3), channel_id=1, source_target_pairs={{1,4},{4,1},{5,8},{8,5},{9,12},{12,9},{3,6},{6,3},{7,10},{10,7},{1... | collective-permute-start | bytes 3145736 | tf_op jit(solution)/shard_map/ppermute | solution.py:180
  9.1 4.5 %collective-permute-start = (bf16[17,16,128]{2,1,0:T(8,128)(2,1)S(1)}, bf16[17,16,128]{2,1,0:T(8,128)(2,1)}, u32[]{:S(2)}, u32[]{:S(2)}) collective-permute-start(bf16[17,16,128]{2,1,0:T(8,128)(2,1)S(1)} %pad_maximum_fusion), channel_id=1, source_target_pairs={{2,0},{0,2},{3,1},{1,3},{6,4},{4,6},{7,5},{5,7},{10,8},{8,10},{11,... | collective-permute-start | bytes 208904 | tf_op jit(solution)/shard_map/ppermute | solution.py:19
  10.4 30.3 %collective-permute-start.3 = (bf16[8,2,128,128]{3,2,1,0:T(8,128)(2,1)}, bf16[8,2,128,128]{3,2,1,0:T(8,128)(2,1)}, u32[]{:S(2)}, u32[]{:S(2)}) collective-permute-start(bf16[8,2,128,128]{3,2,1,0:T(8,128)(2,1)} %left_own.3), channel_id=1, source_target_pairs={{2,0},{0,2},{3,1},{1,3},{6,4},{4,6},{7,5},{5,7},{10,8},{8,10},{11,... | collective-permute-start | bytes 1572872 | tf_op jit(solution)/shard_map/ppermute | solution.py:19
  12.5 24.3 %collective-permute-start.6 = (bf16[8,128,128]{2,1,0:T(8,128)(2,1)}, bf16[8,128,128]{2,1,0:T(8,128)(2,1)S(1)}, u32[]{:S(2)}, u32[]{:S(2)}) collective-permute-start(bf16[8,128,128]{2,1,0:T(8,128)(2,1)} %get-tuple-element.5), channel_id=1, source_target_pairs={{0,13},{1,12},{4,9},{5,8},{8,5},{9,4},{12,1},{13,0},{2,15},{3,14},... | collective-permute-start | bytes 786440 | tf_op jit(solution)/shard_map/ppermute | solution.py:202
  13.6 25.9 %collective-permute-start.4 = (bf16[8,128,128]{2,1,0:T(8,128)(2,1)}, bf16[8,128,128]{2,1,0:T(8,128)(2,1)S(1)}, u32[]{:S(2)}, u32[]{:S(2)}) collective-permute-start(bf16[8,128,128]{2,1,0:T(8,128)(2,1)} %get-tuple-element.6), channel_id=1, source_target_pairs={{0,13},{1,12},{4,9},{5,8},{8,5},{9,4},{12,1},{13,0},{2,15},{3,14},... | collective-permute-start | bytes 786440 | tf_op jit(solution)/shard_map/ppermute | solution.py:202
  36.8 18.2 %collective-permute-start.7 = (bf16[8,128,128]{2,1,0:T(8,128)(2,1)S(1)}, bf16[8,128,128]{2,1,0:T(8,128)(2,1)S(1)}, u32[]{:S(2)}, u32[]{:S(2)}) collective-permute-start(bf16[8,128,128]{2,1,0:T(8,128)(2,1)S(1)} %collective-permute-done.6.rest_0_), channel_id=1, source_target_pairs={{2,0},{0,2},{3,1},{1,3},{6,4},{4,6},{7,5},{5,7},{10,8},{8,10},{11,... | collective-permute-start | bytes 786440 | tf_op jit(solution)/shard_map/ppermute | solution.py:19
  39.5 31.2 %collective-permute-start.5 = (bf16[8,128,128]{2,1,0:T(8,128)(2,1)S(1)}, bf16[8,128,128]{2,1,0:T(8,128)(2,1)S(1)}, u32[]{:S(2)}, u32[]{:S(2)}) collective-permute-start(bf16[8,128,128]{2,1,0:T(8,128)(2,1)S(1)} %collective-permute-done.4.rest_0_), channel_id=1, source_target_pairs={{2,0},{0,2},{3,1},{1,3},{6,4},{4,6},{7,5},{5,7},{10,8},{8,10},{11,... | collective-permute-start | bytes 786440 | tf_op jit(solution)/shard_map/ppermute | solution.py:19
  40.7 1.0 %copy-start.1 = (bf16[8,2,128,128]{3,2,1,0:T(8,128)(2,1)S(1)}, bf16[8,2,128,128]{3,2,1,0:T(8,128)(2,1)}, u32[]{:S(2)}) copy-start(bf16[8,2,128,128]{3,2,1,0:T(8,128)(2,1)} %left_own.3) | copy-start | bytes 1572868

commit v2 on v1

v2 whole, which is shorter than its diff:
```python
import functools

import jax
import jax.numpy as jnp
from jax import lax
from jax.experimental import pallas as pl
from jax.experimental.pallas import tpu as pltpu
from jax.sharding import PartitionSpec as P

F32 = jnp.float32
BF16 = jnp.bfloat16
VMEM = pltpu.VMEM
SMEM = pltpu.SMEM
SMALL = pl.CostEstimate(flops=1 << 10, bytes_accessed=1 << 10, transcendentals=0)
SOME = pl.CostEstimate(flops=1 << 28, bytes_accessed=1 << 20, transcendentals=0)
PAD = 1


def ring(block, axis, step):
    count = lax.axis_size(axis)
    return lax.ppermute(block, axis, [((i + step) % count, i) for i in range(count)])


def turn_kernel(which, info, dims, *refs):
    turned, plane = refs[-2:]
    _, block, states, width = refs[0].shape
    place, places = info[0], info[1]
    odd = lax.rem(place, 2)
    home = (place, place + 1 - 2 * odd, place - 1 + 2 * odd)[which]
    rows = lax.broadcasted_iota(jnp.int32, (block, width), 0)
    lanes = lax.broadcasted_iota(jnp.int32, (block, width), 1)

    def move(psi, entry):
        source = jnp.clip(home * 2 + entry, 0, 2 * places - 1)
        keep = (rows < dims[source]) & (lanes < dims[2 * places - 1 - source])
        plane[...] = psi.astype(F32).reshape(block * states, width)
        for t in range(states):
            piece = plane[pl.ds(t, block, stride=states), :]
            turned[entry, :, t * width : (t + 1) * width] = jnp.where(keep, piece, 0.0).astype(BF16)

    for e in range(2):
        move(refs[0][e], e)


def turn(which, info, dims, psi, *before):
    _, block, states, width = psi.shape
    return pl.pallas_call(
        functools.partial(turn_kernel, which),
        grid=(1,),
        out_shape=jax.ShapeDtypeStruct((6, block, states * width), BF16),
        in_specs=[pl.BlockSpec(memory_space=SMEM)] * 2
        + [pl.BlockSpec(psi.shape, lambda i: (0, 0, 0, 0))]
        + [pl.BlockSpec(memory_space=pl.ANY)] * len(before),
        out_specs=pl.BlockSpec((2, block, states * width), lambda i: (which, 0, 0)),
        scratch_shapes=[VMEM((block * states, width), F32)],
        input_output_aliases={3: 0} if before else {},
        compiler_params=pltpu.CompilerParams(vmem_limit_bytes=16 << 20),
        cost_estimate=SMALL,
        name=f"turn_{which}",
    )(info, dims, psi, *before)


def pack_kernel(info, mask, shift, coef, left, *outs):
    w_dev, channels, states, _ = coef.shape
    block = left.shape[2]
    base = w_dev * block
    lanes = lax.broadcasted_iota(jnp.int32, (states, w_dev * states), 1)
    offsets = jnp.zeros(lanes.shape, F32)
    for w in range(w_dev):
        offsets = jnp.where(lanes == w, shift[w].astype(F32), offsets)
    for j, out in enumerate(outs):
        entry = lax.rem(info[3] + j + 1, 2)
        for w in range(w_dev):
            out[w * block : (w + 1) * block] = left[w, entry]
        for v in range(channels):
            pieces = [coef[w, v].astype(F32) * mask[w, v].astype(F32) for w in range(w_dev)]
            out[base + v * states : base + (v + 1) * states] = jnp.concatenate(
                pieces, axis=1
            ).astype(BF16)
        out[base + channels * states : base + (channels + 1) * states] = offsets.astype(BF16)


def pack(info, mask, shift, coef, left, copies):
    w_dev, channels, states, _ = coef.shape
    rows = w_dev * left.shape[2] + (channels + 1) * states
    return pl.pallas_call(
        pack_kernel,
        out_shape=[jax.ShapeDtypeStruct((rows, w_dev * states), BF16)] * copies,
        in_specs=[pl.BlockSpec(memory_space=SMEM)] * 3 + [pl.BlockSpec(memory_space=VMEM)] * 2,
        out_specs=[pl.BlockSpec(memory_space=VMEM)] * copies,
        compiler_params=pltpu.CompilerParams(vmem_limit_bytes=16 << 20),
        cost_estimate=SMALL,
        name="pack",
    )(info, mask, shift, coef, left)


def cut_env_kernel(entries, rows, info, env, *outs):
    for entry, (begin, size), out in zip(entries, rows, outs):
        at = lax.rem(info[3] + entry, 2)
        for v in range(env.shape[0]):
            out[v] = env[v, at, begin : begin + size, :]


def cut_env(info, env, entries, rows):
    return pl.pallas_call(
        functools.partial(cut_env_kernel, entries, rows),
        out_shape=[
            jax.ShapeDtypeStruct((env.shape[0], size, env.shape[3]), BF16) for _, size in rows
        ],
        in_specs=[pl.BlockSpec(memory_space=SMEM), pl.BlockSpec(memory_space=VMEM)],
        out_specs=[pl.BlockSpec(memory_space=VMEM)] * len(rows),
        compiler_params=pltpu.CompilerParams(vmem_limit_bytes=8 << 20),
        cost_estimate=SMALL,
        name="cut_env",
    )(info, env)


def mix_kernel(info, shift, *refs):
    turned, own, *parcels = refs[:-4]
    given, kept, first, coupling = refs[-4:]
    groups = len(parcels)
    w_dev, _, block, _ = own.shape
    width = block
    states = turned.shape[2] // width
    channels = coupling.shape[0] // 16
    base = w_dev * block
    place, parity = info[0], info[3]
    near_place = place + 1 - 2 * lax.rem(place, 2)
    sector = place * 2 + parity
    step = block + PAD
    for j, parcel in enumerate(parcels):
        cube = parcel[base : base + channels * states].astype(F32)
        cube = cube.reshape(channels, states, w_dev * states)
        for h in range(2):
            rows = jnp.where(info[4 + h] == 0, cube[:, :8], cube[:, 8:]).reshape(channels * 8, -1)
            coupling[
                h * channels * 8 : (h + 1) * channels * 8,
                j * w_dev * states : (j + 1) * w_dev * states,
            ] = rows.astype(BF16)

    for j, parcel in enumerate(parcels):
        for w in range(w_dev):
            source = sector - shift[j * w_dev + w]
            at = source >> 1
            which = jnp.where(at == place, 0, jnp.where(at == near_place, 1, 2))
            slot = which * 2 + (source & 1)
            matrix = own[w, parity] if j == 0 else parcel[w * block : (w + 1) * block]
            for t in range(0, states, 2):
                product = jnp.dot(
                    matrix,
                    turned[slot, :, t * width : (t + 2) * width],
                    preferred_element_type=F32,
                )
                for h in range(2):
                    row = ((j * w_dev + w) * states + t + h) * step
                    first[pl.ds(row, block), :] = product[:, h * width : (h + 1) * width]

    inner = groups * w_dev * states

    def stage2(i, carry):
        for u in range(4):
            a = i * 8 + u * 2
            pair = [first[pl.ds(a + h, inner, stride=step), :].astype(BF16) for h in range(2)]
            product = jnp.dot(
                coupling[...], jnp.concatenate(pair, axis=1), preferred_element_type=F32
            )
            for half, mixed in enumerate((given, kept)):
                part = product[half * channels * 8 : (half + 1) * channels * 8]
                halves = [
                    part[:, h * width : (h + 1) * width].reshape(channels, 1, 8, width)
                    for h in range(2)
                ]
                both = jnp.concatenate(halves, axis=1).reshape(channels, 16, width).astype(BF16)
                for v in range(channels):
                    mixed[pl.ds(pl.multiple_of(a * 8, 16), 16), v * width : (v + 1) * width] = both[
                        v
                    ]
        return carry

    lax.fori_loop(0, block // 8, stage2, 0, unroll=True)


def mix(info, shift, channels, turned, own, parcels):
    _, block, flat = turned.shape
    width = block
    inner = parcels[0].shape[1] * len(parcels)
    return pl.pallas_call(
        mix_kernel,
        out_shape=[jax.ShapeDtypeStruct((block * 8, channels * width), BF16)] * 2,
        in_specs=[pl.BlockSpec(memory_space=SMEM)] * 2
        + [pl.BlockSpec(memory_space=VMEM)] * (2 + len(parcels)),
        out_specs=[pl.BlockSpec(memory_space=VMEM)] * 2,
        scratch_shapes=[
            VMEM((inner * (block + PAD), width), F32),
            VMEM((channels * 16, inner), BF16),
        ],
        compiler_params=pltpu.CompilerParams(vmem_limit_bytes=(40 if inner <= 256 else 62) << 20),
        cost_estimate=SMALL,
        name="mix",
    )(info, shift, turned, own, *parcels)


def product(mixed, rights, wheres):
    total = None
    for right, where in zip(rights, wheres):
        depth = right[0].shape[1]
        column = pl.multiple_of(where * depth, depth)
        part = lax.dot_general(
            mixed[:, pl.ds(column, len(right) * depth)],
            jnp.concatenate(right, axis=1),
            (((1,), (1,)), ((), ())),
            preferred_element_type=F32,
        )
        total = part if total is None else total + part
    return total


def masked(total, info, dims, begin):
    rows, size = total.shape
    sector = info[0] * 2 + info[3]
    cube = (rows // 8, 8, size)
    a = lax.broadcasted_iota(jnp.int32, cube, 0)
    b = lax.broadcasted_iota(jnp.int32, cube, 2) + begin
    keep = (a < dims[sector]) & (b < dims[2 * info[1] - 1 - sector])
    return jnp.where(keep, total.reshape(cube), 0.0)


def begin_kernel(info, given, kept, right, given_out, kept_out):
    v_dev = right.shape[0]
    blocks = [[right[v] for v in range(v_dev)]]
    given_out[...] = product(given, blocks, [info[2] * v_dev])
    kept_out[...] = product(kept, blocks, [info[2] * v_dev])


def begin(info, given, kept, right):
    rows, width = given.shape[0], right.shape[1]
    return pl.pallas_call(
        begin_kernel,
        out_shape=[jax.ShapeDtypeStruct((rows, width), F32)] * 2,
        in_specs=[pl.BlockSpec(memory_space=SMEM)] + [pl.BlockSpec(memory_space=VMEM)] * 3,
        out_specs=[pl.BlockSpec(memory_space=VMEM)] * 2,
        compiler_params=pltpu.CompilerParams(vmem_limit_bytes=24 << 20),
        cost_estimate=SOME,
        name="begin",
    )(info, given, kept, right)


def others(info, v_dev, groups):
    return [lax.rem(info[2] + j, groups) * v_dev for j in range(1, groups)]


def give_kernel(piece, info, dims, mixed, before, *refs):
    rights, out = refs[:-1], refs[-1]
    v_dev, size, _ = rights[0].shape
    blocks = [[right[v] for v in range(v_dev)] for right in rights]
    total = product(mixed, blocks, others(info, v_dev, len(rights) + 1))
    total += before[:, piece * size : (piece + 1) * size]
    cube = masked(total, info, dims, piece * size)
    half = cube.shape[0] // 2
    out[:half] = jnp.concatenate([cube[:half], cube[half:]], axis=2).astype(BF16)
    if out.shape[0] > half:
        out[half:] = jnp.zeros((1, *out.shape[1:]), BF16)


def give(piece, info, dims, mixed, before, rights):
    size = rights[0].shape[1]
    return pl.pallas_call(
        functools.partial(give_kernel, piece),
        out_shape=jax.ShapeDtypeStruct((mixed.shape[0] // 16 + 1 - piece, 8, 2 * size), BF16),
        in_specs=[pl.BlockSpec(memory_space=SMEM)] * 2
        + [pl.BlockSpec(memory_space=VMEM)] * (2 + len(rights)),
        out_specs=pl.BlockSpec(memory_space=VMEM),
        compiler_params=pltpu.CompilerParams(vmem_limit_bytes=24 << 20),
        cost_estimate=SOME,
        name=f"give_{piece}",
    )(info, dims, mixed, before, *rights)


def keep_kernel(info, dims, mixed, before, *refs):
    rights, out = refs[:-1], refs[-1]
    half = len(rights) // 2
    v_dev = rights[0].shape[0]
    blocks = [
        [jnp.concatenate([low[v], high[v]], axis=0) for v in range(v_dev)]
        for low, high in zip(rights[:half], rights[half:])
    ]
    total = before[...] + product(mixed, blocks, others(info, v_dev, half + 1))
    out[0] = masked(total, info, dims, 0).astype(BF16)


def keep(info, dims, mixed, before, rights):
    rows, width = before.shape
    whole = lambda a: pl.BlockSpec(a.shape, lambda i, info, dims, n=a.ndim: (0,) * n)
    return pl.pallas_call(
        keep_kernel,
        out_shape=jax.ShapeDtypeStruct((2, rows // 8, 8, width), BF16),
        grid_spec=pltpu.PrefetchScalarGridSpec(
            num_scalar_prefetch=2,
            grid=(1,),
            in_specs=[whole(a) for a in (mixed, before, *rights)],
            out_specs=pl.BlockSpec(
                (1, rows // 8, 8, width), lambda i, info, dims: (info[3], 0, 0, 0)
            ),
        ),
        compiler_params=pltpu.CompilerParams(vmem_limit_bytes=24 << 20),
        cost_estimate=SMALL,
        name="keep",
    )(info, dims, mixed, before, *rights)


def finish_kernel(info, zero, one, result, out):
    half, _, width = one.shape
    lower = lax.broadcasted_iota(jnp.int32, one.shape, 2) < width // 2

    def halves(ref):
        cube = ref[:half].astype(F32)
        turned = pltpu.roll(cube.reshape(half * 8, width), width // 2, 1)
        return cube, turned.reshape(cube.shape)

    first, first_turned = halves(zero)
    second, second_turned = halves(one)
    out[0, :half] = jnp.where(lower, first, second_turned).astype(BF16)
    out[0, half:] = jnp.where(lower, first_turned, second).astype(BF16)


def finish(info, zero, one, result):
    half, _, width = one.shape
    whole = [pl.BlockSpec(a.shape, lambda i, info: (0, 0, 0)) for a in (zero, one)]
    return pl.pallas_call(
        finish_kernel,
        out_shape=jax.ShapeDtypeStruct(result.shape, BF16),
        grid_spec=pltpu.PrefetchScalarGridSpec(
            num_scalar_prefetch=1,
            grid=(1,),
            in_specs=[*whole, pl.BlockSpec(memory_space=pl.ANY)],
            out_specs=pl.BlockSpec(
                (1, 2 * half, 8, width), lambda i, info: (1 - info[3], 0, 0, 0)
            ),
        ),
        input_output_aliases={3: 0},
        compiler_params=pltpu.CompilerParams(vmem_limit_bytes=16 << 20),
        cost_estimate=SMALL,
        name="finish",
    )(info, zero, one, result)


def after(value, *others):
    return lax.optimization_barrier((value, *others))[0]


def on_device(psi, dims, left_env, right_env, shift, mpo_coef, mpo_mask):
    sec_dev, block, states, width = psi.shape
    w_dev = left_env.shape[0]
    channels = mpo_coef.shape[1]
    groups = lax.axis_size("mpo")
    spots = ("sec", "rep")
    places = lax.axis_size(spots)
    place = lax.axis_index(spots)
    group = lax.axis_index("mpo")
    parity = group % 2
    share = states // groups
    begin_given = ((group + 1 - 2 * parity) * share) // 8 * 8
    begin_kept = (group * share) // 8 * 8
    info = jnp.stack([place, places, group, parity, begin_given, begin_kept]).astype(jnp.int32)

    def swap(block, begin):
        route = []
        for low in range(begin, places - 1, 2):
            route += [(low, low + 1), (low + 1, low)]
        return lax.ppermute(block, spots, route)

    def mirrored(block):
        return lax.ppermute(block, spots, [(i, places - 1 - i) for i in range(places)])

    def beside(block):
        return lax.ppermute(block, "mpo", [(g, g ^ 1) for g in range(groups)])

    steps = range(1, groups)
    far = swap(psi, 1)
    near = swap(psi, 0)
    turned = turn(0, info, dims, psi)
    sent = pack(after(info, turned), mpo_mask, shift, mpo_coef, left_env, groups - 1)
    parcels = [sent[0]] + [ring(p, "mpo", j) for j, p in zip(steps, sent)]
    size = width // 2
    pairs = [(0, (0, width))] + [(j, (r, size)) for r in (0, size) for j in steps]
    entries, rows = [(1 + j) % 2 for j, _ in pairs], [r for _, r in pairs]
    cuts = cut_env(after(info, *sent), right_env, entries, rows)
    passed = [ring(c, "mpo", j) for c, (j, _) in zip(cuts[1:], pairs[1:])]
    turned = turn(1, after(info, *cuts), dims, near, turned)
    same = mirrored(after(cuts[0], turned))
    rights = [mirrored(after(c, turned)) for c in passed]
    turned = turn(2, info, dims, far, turned)
    last = w_dev * block + channels * states
    shifts = jnp.concatenate([p[last, :w_dev] for p in parcels]).astype(jnp.int32)
    given, kept = mix(info, shifts, channels, turned, left_env, parcels)
    given_sum, kept_sum = begin(info, given, kept, same)
    low, high = rights[: groups - 1], rights[groups - 1 :]
    to_give = give(0, after(info, given_sum), dims, given, given_sum, low)
    zero = beside(to_give)
    part = give(1, after(info, given_sum, to_give), dims, given, given_sum, high)
    one = beside(part)
    result = keep(after(info, part), dims, kept, kept_sum, rights)
    result = finish(info, zero, one, result)
    if share != 8:
        result = lax.dynamic_slice_in_dim(result, group * share - begin_kept, share, 2)
    return result


def solution(mesh):
    return jax.shard_map(
        on_device,
        mesh=mesh,
        in_specs=(
            P(("runs", "sec", "rep"), None, None, None),
            P("runs"),
            P("mpo", ("runs", "sec", "rep"), None, None),
            P("mpo", ("runs", "sec", "rep"), None, None),
            P("mpo"),
            P("mpo", None, None, None),
            P("mpo", None),
        ),
        out_specs=P(("runs", "sec", "rep"), None, "mpo", None),
        check_vma=False,
    )
```

time: 73.6 us -> 49 us (0.67)
  Pallas kernels: 31.4 us -> 19.5 us
  waiting for transfers between devices: 22.4 us -> 13.7 us
  local copies, waits for them, and re-layouts: 7.02 us -> 1.99 us
  starting transfers between devices: 9.48 us -> 13.4 us
  other arithmetic: 2.76 us -> 0.08 us
    ppermute x2 -> x5, waiting for transfers between devices: 22.4 us -> 1.84 us  [the longest x2 1.84 us: beside(): return lax.ppermute(block, 'mpo', [(g, g ^ 1) for g in range(groups)])]
    pallas_call x4 -> x11, Pallas kernels: 31.4 us -> 19.5 us  [the longest x3 5.23 us: turn(): pl.pallas_call(functools.partial(turn_kernel, which), grid=(1,), out_shap...]
    ppermute x4 -> x3, waiting for transfers between devices: 0.01 us -> 7.28 us  [ring(): lax.ppermute(block, axis, [((i + step) % count, i) for i in range(count)])]
    ppermute x2 -> x5, starting transfers between devices: 1.84 us -> 6.65 us  [the longest x3 4.03 us: mirrored(): lax.ppermute(block, spots, [(i, places - 1 - i) for i in range(places)])]
    ppermute x2, waiting for transfers between devices: 0.01 us -> 4.6 us  [swap(): return lax.ppermute(block, spots, route)]
    squeeze x2, local copies, waits for them, and re-layouts: 2.54 us -> 0.01 us  [on_device(): p[last, :w_dev]]
    reshape x1 -> x0, local copies, waits for them, and re-layouts: 1.43 us -> none  [on_device(): jnp.transpose(coupling, (1, 2, 0, 3))]
    transpose x1 -> x0, other arithmetic: 1.24 us -> none  [on_device(): jnp.transpose(coupling, (1, 2, 0, 3))]
  transfers between devices with their start and end apart: 8 -> 10, of which waited for: 2 -> 5; matrix products, arithmetic and copies ran while one was open for 12% -> 0% of each run, Pallas kernels for 39% -> 37%
where the time goes in v2:
time: 49 us; the launch traced here: 48.9 us
  Pallas kernels  19.5 us (40%)
  waiting for transfers between devices  13.7 us (28%)
  starting transfers between devices  13.4 us (27%)
  local copies, waits for them, and re-layouts  1.99 us (4%)
    ppermute x3, waiting for transfers between devices, ring(): lax.ppermute(block, axis, [((i + step) % count, i) for i in range(count)])  7.28 us
    pallas_call x3, Pallas kernels, turn(): pl.pallas_call(functools.partial(turn_kernel, which), grid=(1,), out_shap...  5.23 us
    pallas_call x1, Pallas kernels, mix(): pl.pallas_call(mix_kernel, out_shape=[jax.ShapeDtypeStruct((block * 8, ch...  5.19 us
    ppermute x2, waiting for transfers between devices, swap(): return lax.ppermute(block, spots, route)  4.6 us
    ppermute x3, starting transfers between devices, mirrored(): lax.ppermute(block, spots, [(i, places - 1 - i) for i in range(places)])  4.03 us
    ppermute x2, starting transfers between devices, swap(): return lax.ppermute(block, spots, route)  3.9 us
    ppermute x3, starting transfers between devices, ring(): lax.ppermute(block, axis, [((i + step) % count, i) for i in range(count)])  2.81 us
    ppermute x2, starting transfers between devices, beside(): return lax.ppermute(block, 'mpo', [(g, g ^ 1) for g in range(groups)])  2.62 us
  transfers between devices with their start and end apart: 10, of which 5 were waited for; matrix products, arithmetic and copies ran while one was open for 0% of the time, Pallas kernels for 37%

profile of v2, /device:TPU:9, one launch (start us, length us, event | category | flops | bytes accessed | tf_op | source)
XLA Modules:
  0.0 48.9 jit_solution(17955007251823456519)
XLA Ops:
  0.0 0.0 copy-start
  0.0 0.7 %collective-permute-start.2 = (bf16[2,128,16,128]{3,2,1,0:T(8,128)(2,1)}, bf16[2,128,16,128]{3,2,1,0:T(8,128)(2,1)S(1)}, u32[]{:S(2)}, u32[]{:S(2)}) collective-permute-start(bf16[2,128,16,128]{3,2,1,0:T(8,128)(2,1)} %refs_0_.1), channel_id=1, source_target_pairs={{0,1},{1,0},{4,5},{5,4},{8,9},{9,8},{12,13},{13,12},{2,3},{3,2},{6... | collective-permute-start | bytes 3145736 | tf_op jit(solution)/shard_map/ppermute | solution.py:370
  0.7 3.2 %collective-permute-start.1 = (bf16[2,128,16,128]{3,2,1,0:T(8,128)(2,1)}, bf16[2,128,16,128]{3,2,1,0:T(8,128)(2,1)S(1)}, u32[]{:S(2)}, u32[]{:S(2)}) collective-permute-start(bf16[2,128,16,128]{3,2,1,0:T(8,128)(2,1)} %refs_0_.1), channel_id=1, source_target_pairs={{1,4},{4,1},{5,8},{8,5},{9,12},{12,9},{3,6},{6,3},{7,10},{10,7},{1... | collective-permute-start | bytes 3145736 | tf_op jit(solution)/shard_map/ppermute | solution.py:370
  4.0 0.1 stack.23.info
  4.0 0.0 copy-start.1
  4.0 1.2 %copy-done.1 = bf16[2,128,16,128]{3,2,1,0:T(8,128)(2,1)S(1)} copy-done((bf16[2,128,16,128]{3,2,1,0:T(8,128)(2,1)S(1)}, bf16[2,128,16,128]{3,2,1,0:T(8,128)(2,1)}, u32[]{:S(2)}) %copy-start.1) | copy-done | bytes 1048600
  5.3 0.0 copy-start.4
  5.3 0.7 %copy-done.4 = s32[16]{0:T(128)S(1)} copy-done((s32[16]{0:T(128)S(1)}, s32[16]{0:T(128)}, u32[]{:S(2)}) %copy-start.4) | copy-done | bytes 88
  5.9 0.0 copy-start.3
  5.9 0.0 copy-start.5
  5.9 0.0 copy-start.6
  5.9 0.0 copy-start.2
  5.9 1.7 %turn_0.1.refs_1_ = bf16[6,128,2048]{2,1,0:T(8,128)(2,1)S(1)} custom-call(s32[6]{0:T(128)S(1)} %stack.23.info, s32[16]{0:T(128)S(1)} %copy-done.4, bf16[2,128,16,128]{3,2,1,0:T(8,128)(2,1)S(1)} %copy-done.1), custom_call_target="tpu_custom_call" | custom-call | flops 1024 | bytes 1024 | tf_op jit(solution)/shard_map/turn_0/pallas_call | solution.py:47
  7.7 0.0 copy-done
  7.7 0.0 copy-done.3
  7.7 0.0 copy-done.5
  7.7 0.0 copy-done.6
  7.7 0.8 %pack.1.refs_2_ = bf16[1296,128]{1,0:T(8,128)(2,1)S(1)} custom-call(s32[6]{0:T(128)S(1)} %stack.23.info, s32[8,16]{1,0:T(8,128)S(1)} %copy-done.5, s32[8]{0:T(128)S(1)} %copy-done.6, bf16[8,16,16,16]{3,2,1,0:T(8,128)(2,1)S(1)} %copy-done.3, bf16[8,2,128,128]{3,2,1,0:T(8,128)(2,1)S(1)} %copy-done), custom_call_target="tpu_custom_call" | custom-call | flops 1024 | bytes 1024 | tf_op jit(solution)/shard_map/pack/pallas_call | solution.py:86
  8.5 1.3 %collective-permute-start = (bf16[1296,128]{1,0:T(8,128)(2,1)S(1)}, bf16[1296,128]{1,0:T(8,128)(2,1)S(1)}, u32[]{:S(2)}, u32[]{:S(2)}) collective-permute-start(bf16[1296,128]{1,0:T(8,128)(2,1)S(1)} %pack.1.refs_2_), channel_id=1, source_target_pairs={{2,0},{0,2},{3,1},{1,3},{6,4},{4,6},{7,5},{5,7},{10,8},{8,10},{11,... | collective-permute-start | bytes 995336 | tf_op jit(solution)/shard_map/ppermute | solution.py:21
  9.8 0.0 copy-done.2
  9.8 0.6 %cut_env.1 = (bf16[8,128,128]{2,1,0:T(8,128)(2,1)S(1)}, bf16[8,64,128]{2,1,0:T(8,128)(2,1)S(1)}, bf16[8,64,128]{2,1,0:T(8,128)(2,1)S(1)}) custom-call(s32[6]{0:T(128)S(1)} %stack.23.info, bf16[8,2,128,128]{3,2,1,0:T(8,128)(2,1)S(1)} %copy-done.2), custom_call_target="tpu_custom_call" | custom-call | flops 1024 | bytes 1024 | tf_op jit(solution)/shard_map/cut_env/pallas_call | solution.py:105
  10.4 0.3 collective-permute-start.4
  10.7 1.2 %collective-permute-start.7 = (bf16[8,64,128]{2,1,0:T(8,128)(2,1)S(1)}, bf16[8,64,128]{2,1,0:T(8,128)(2,1)S(1)}, u32[]{:S(2)}, u32[]{:S(2)}) collective-permute-start(bf16[8,64,128]{2,1,0:T(8,128)(2,1)S(1)} %get-tuple-element.25), channel_id=1, source_target_pairs={{2,0},{0,2},{3,1},{1,3},{6,4},{4,6},{7,5},{5,7},{10,8},{8,10},{11,... | collective-permute-start | bytes 393224 | tf_op jit(solution)/shard_map/ppermute | solution.py:21
  11.9 0.0 collective-permute-done.2.refs_0_
  11.9 1.7 %turn_1.1.refs_1_ = bf16[6,128,2048]{2,1,0:T(8,128)(2,1)S(1)} custom-call(s32[6]{0:T(128)S(1)} %stack.23.info, s32[16]{0:T(128)S(1)} %copy-done.4, bf16[2,128,16,128]{3,2,1,0:T(8,128)(2,1)S(1)} %collective-permute-done.2.refs_0_, bf16[6,128,2048]{2,1,0:T(8,128)(2,1)S(1)} %turn_0.1.refs_1_), custom_call_target="tpu_custom_call", output_to_operand_aliasing={{}: (3, {})} | custom-call | flops 1024 | bytes 1024 | tf_op jit(solution)/shard_map/turn_1/pallas_call | solution.py:47
  13.7 1.3 %collective-permute-start.3 = (bf16[8,128,128]{2,1,0:T(8,128)(2,1)S(1)}, bf16[8,128,128]{2,1,0:T(8,128)(2,1)S(1)}, u32[]{:S(2)}, u32[]{:S(2)}) collective-permute-start(bf16[8,128,128]{2,1,0:T(8,128)(2,1)S(1)} %get-tuple-element.29), channel_id=1, source_target_pairs={{0,13},{1,12},{4,9},{5,8},{8,5},{9,4},{12,1},{13,0},{2,15},{3,14},... | collective-permute-start | bytes 786440 | tf_op jit(solution)/shard_map/ppermute | solution.py:373
  15.0 3.4 %collective-permute-done.refs_3_ = bf16[1296,128]{1,0:T(8,128)(2,1)S(1)} collective-permute-done((bf16[1296,128]{1,0:T(8,128)(2,1)S(1)}, bf16[1296,128]{1,0:T(8,128)(2,1)S(1)}, u32[]{:S(2)}, u32[]{:S(2)}) %collective-permute-start) | collective-permute-done | bytes 331808 | tf_op jit(solution)/shard_map/ppermute | solution.py:21
  18.4 2.8 %collective-permute-done.4 = bf16[8,64,128]{2,1,0:T(8,128)(2,1)S(1)} collective-permute-done((bf16[8,64,128]{2,1,0:T(8,128)(2,1)S(1)}, bf16[8,64,128]{2,1,0:T(8,128)(2,1)S(1)}, u32[]{:S(2)}, u32[]{:S(2)}) %collective-permute-start.4) | collective-permute-done | bytes 131104 | tf_op jit(solution)/shard_map/ppermute | solution.py:21
  21.2 1.0 %collective-permute-start.5 = (bf16[8,64,128]{2,1,0:T(8,128)(2,1)S(1)}, bf16[8,64,128]{2,1,0:T(8,128)(2,1)S(1)}, u32[]{:S(2)}, u32[]{:S(2)}) collective-permute-start(bf16[8,64,128]{2,1,0:T(8,128)(2,1)S(1)} %collective-permute-done.4), channel_id=1, source_target_pairs={{0,13},{1,12},{4,9},{5,8},{8,5},{9,4},{12,1},{13,0},{2,15},{3,14},... | collective-permute-start | bytes 393224 | tf_op jit(solution)/shard_map/ppermute | solution.py:373
  22.2 1.1 %collective-permute-done.7 = bf16[8,64,128]{2,1,0:T(8,128)(2,1)S(1)} collective-permute-done((bf16[8,64,128]{2,1,0:T(8,128)(2,1)S(1)}, bf16[8,64,128]{2,1,0:T(8,128)(2,1)S(1)}, u32[]{:S(2)}, u32[]{:S(2)}) %collective-permute-start.7) | collective-permute-done | bytes 131104 | tf_op jit(solution)/shard_map/ppermute | solution.py:21
  23.3 1.7 %collective-permute-start.8 = (bf16[8,64,128]{2,1,0:T(8,128)(2,1)S(1)}, bf16[8,64,128]{2,1,0:T(8,128)(2,1)S(1)}, u32[]{:S(2)}, u32[]{:S(2)}) collective-permute-start(bf16[8,64,128]{2,1,0:T(8,128)(2,1)S(1)} %collective-permute-done.7), channel_id=1, source_target_pairs={{0,13},{1,12},{4,9},{5,8},{8,5},{9,4},{12,1},{13,0},{2,15},{3,14},... | collective-permute-start | bytes 393224 | tf_op jit(solution)/shard_map/ppermute | solution.py:373
  25.0 0.1 maximum_convert_fusion.shift
  25.1 4.6 %collective-permute-done.1.refs_0_ = bf16[2,128,16,128]{3,2,1,0:T(8,128)(2,1)S(1)} collective-permute-done((bf16[2,128,16,128]{3,2,1,0:T(8,128)(2,1)}, bf16[2,128,16,128]{3,2,1,0:T(8,128)(2,1)S(1)}, u32[]{:S(2)}, u32[]{:S(2)}) %collective-permute-start.1) | collective-permute-done | bytes 1048608 | tf_op jit(solution)/shard_map/ppermute | solution.py:370
  29.7 1.7 %turn_2.1.refs_0_ = bf16[6,128,2048]{2,1,0:T(8,128)(2,1)S(1)} custom-call(s32[6]{0:T(128)S(1)} %stack.23.info, s32[16]{0:T(128)S(1)} %copy-done.4, bf16[2,128,16,128]{3,2,1,0:T(8,128)(2,1)S(1)} %collective-permute-done.1.refs_0_, bf16[6,128,2048]{2,1,0:T(8,128)(2,1)S(1)} %turn_1.1.refs_1_), custom_call_target="tpu_custom_call", output_to_operand_aliasing={{}: (3, {})} | custom-call | flops 1024 | bytes 1024 | tf_op jit(solution)/shard_map/turn_2/pallas_call | solution.py:47
  31.4 5.2 %mix.1 = (bf16[1024,2048]{1,0:T(8,128)(2,1)S(1)}, bf16[1024,2048]{1,0:T(8,128)(2,1)S(1)}) custom-call(s32[6]{0:T(128)S(1)} %stack.23.info, s32[16]{0:T(128)S(1)} %maximum_convert_fusion.shift, bf16[6,128,2048]{2,1,0:T(8,128)(2,1)S(1)} %turn_2.1.refs_0_, bf16[8,2,128,128]{3,2,1,0:T(8,128)(2,1)S(1)} %copy-done, bf16[1296,128]{1,0:T(8,128)(2,1)S(1)} %pack.1.refs_2_, ...), custom_call_target="tpu_custom_call" | custom-call | flops 1024 | bytes 1024 | tf_op jit(solution)/shard_map/mix/pallas_call | solution.py:187
  36.6 0.0 collective-permute-done.3.right
  36.6 1.8 %begin.1 = (f32[1024,128]{1,0:T(8,128)S(1)}, f32[1024,128]{1,0:T(8,128)S(1)}) custom-call(s32[6]{0:T(128)S(1)} %stack.23.info, bf16[1024,2048]{1,0:T(8,128)(2,1)S(1)} %get-tuple-element.27.given.mixed, bf16[1024,2048]{1,0:T(8,128)(2,1)S(1)} %get-tuple-element.28.kept.mixed, bf16[8,128,128]{2,1,0:T(8,128)(2,1)S(1)} %collective-permute-done.3.right), custom_call_target="tpu_custom_call" | custom-call | flops 268435456 | bytes 1048576 | tf_op jit(solution)/shard_map/begin/pallas_call | solution.py:237
  38.4 0.0 collective-permute-done.5.refs_0_
  38.4 1.3 %give_0.1 = bf16[65,8,128]{2,1,0:T(8,128)(2,1)S(1)} custom-call(s32[6]{0:T(128)S(1)} %stack.23.info, s32[16]{0:T(128)S(1)} %copy-done.4, bf16[1024,2048]{1,0:T(8,128)(2,1)S(1)} %get-tuple-element.27.given.mixed, f32[1024,128]{1,0:T(8,128)S(1)} %get-tuple-element.30.before, bf16[8,64,128]{2,1,0:T(8,128)(2,1)S(1)} %collective-permute-done.5.refs_0_), custom_call_target="tpu_custom_call" | custom-call | flops 268435456 | bytes 1048576 | tf_op jit(solution)/shard_map/give_0/pallas_call | solution.py:267
  39.7 2.5 %collective-permute-start.6 = (bf16[65,8,128]{2,1,0:T(8,128)(2,1)S(1)}, bf16[65,8,128]{2,1,0:T(8,128)(2,1)S(1)}, u32[]{:S(2)}, u32[]{:S(2)}) collective-permute-start(bf16[65,8,128]{2,1,0:T(8,128)(2,1)S(1)} %give_0.1), channel_id=1, source_target_pairs={{0,2},{2,0},{1,3},{3,1},{4,6},{6,4},{5,7},{7,5},{8,10},{10,8},{9,1... | collective-permute-start | bytes 399368 | tf_op jit(solution)/shard_map/ppermute | solution.py:376
  42.3 0.0 collective-permute-done.8.refs_0_.refs_1_
  42.3 1.3 %give_1.1 = bf16[64,8,128]{2,1,0:T(8,128)(2,1)S(1)} custom-call(s32[6]{0:T(128)S(1)} %stack.23.info, s32[16]{0:T(128)S(1)} %copy-done.4, bf16[1024,2048]{1,0:T(8,128)(2,1)S(1)} %get-tuple-element.27.given.mixed, f32[1024,128]{1,0:T(8,128)S(1)} %get-tuple-element.30.before, bf16[8,64,128]{2,1,0:T(8,128)(2,1)S(1)} %collective-permute-done.8.refs_0_.refs_1_), custom_call_target="tpu_custom_call" | custom-call | flops 268435456 | bytes 1048576 | tf_op jit(solution)/shard_map/give_1/pallas_call | solution.py:267
  43.6 0.1 collective-permute-start.9
  43.7 2.0 %keep.1.result = bf16[2,128,8,128]{3,2,1,0:T(8,128)(2,1)} custom-call(s32[6]{0:T(128)S(1)} %stack.23.info, s32[16]{0:T(128)S(1)} %copy-done.4, bf16[1024,2048]{1,0:T(8,128)(2,1)S(1)} %get-tuple-element.28.kept.mixed, f32[1024,128]{1,0:T(8,128)S(1)} %get-tuple-element.36.before, bf16[8,64,128]{2,1,0:T(8,128)(2,1)S(1)} %collective-permute-done.5.refs_0_, ...), custom_call_target="tpu_custom_call" | custom-call | flops 1024 | bytes 1024 | tf_op jit(solution)/shard_map/keep/pallas_call | solution.py:294
  45.6 1.8 %collective-permute-done.9.one = bf16[64,8,128]{2,1,0:T(8,128)(2,1)S(1)} collective-permute-done((bf16[64,8,128]{2,1,0:T(8,128)(2,1)S(1)}, bf16[64,8,128]{2,1,0:T(8,128)(2,1)S(1)}, u32[]{:S(2)}, u32[]{:S(2)}) %collective-permute-start.9) | collective-permute-done | bytes 131104 | tf_op jit(solution)/shard_map/ppermute | solution.py:376
  47.5 0.0 collective-permute-done.6.zero
  47.5 1.4 %finish.1 = bf16[2,128,8,128]{3,2,1,0:T(8,128)(2,1)} custom-call(s32[6]{0:T(128)S(1)} %stack.23.info, bf16[65,8,128]{2,1,0:T(8,128)(2,1)S(1)} %collective-permute-done.6.zero, bf16[64,8,128]{2,1,0:T(8,128)(2,1)S(1)} %collective-permute-done.9.one, bf16[2,128,8,128]{3,2,1,0:T(8,128)(2,1)} %keep.1.result), custom_call_target="tpu_custom_call", output_to_operand_aliasing={{}: (3, {})} | custom-call | flops 1024 | bytes 1024 | tf_op jit(solution)/shard_map/finish/pallas_call | solution.py:329
  (2 shorter events, 0.0 us)
Async XLA Ops:
  0.0 7.7 %copy-start = (bf16[8,2,128,128]{3,2,1,0:T(8,128)(2,1)S(1)}, bf16[8,2,128,128]{3,2,1,0:T(8,128)(2,1)}, u32[]{:S(2)}) copy-start(bf16[8,2,128,128]{3,2,1,0:T(8,128)(2,1)} %refs_1_.1) | copy-start | bytes 1572868
  0.0 11.9 %collective-permute-start.2 = (bf16[2,128,16,128]{3,2,1,0:T(8,128)(2,1)}, bf16[2,128,16,128]{3,2,1,0:T(8,128)(2,1)S(1)}, u32[]{:S(2)}, u32[]{:S(2)}) collective-permute-start(bf16[2,128,16,128]{3,2,1,0:T(8,128)(2,1)} %refs_0_.1), channel_id=1, source_target_pairs={{0,1},{1,0},{4,5},{5,4},{8,9},{9,8},{12,13},{13,12},{2,3},{3,2},{6... | collective-permute-start | bytes 3145736 | tf_op jit(solution)/shard_map/ppermute | solution.py:370
  0.7 29.0 %collective-permute-start.1 = (bf16[2,128,16,128]{3,2,1,0:T(8,128)(2,1)}, bf16[2,128,16,128]{3,2,1,0:T(8,128)(2,1)S(1)}, u32[]{:S(2)}, u32[]{:S(2)}) collective-permute-start(bf16[2,128,16,128]{3,2,1,0:T(8,128)(2,1)} %refs_0_.1), channel_id=1, source_target_pairs={{1,4},{4,1},{5,8},{8,5},{9,12},{12,9},{3,6},{6,3},{7,10},{10,7},{1... | collective-permute-start | bytes 3145736 | tf_op jit(solution)/shard_map/ppermute | solution.py:370
  4.0 1.2 %copy-start.1 = (bf16[2,128,16,128]{3,2,1,0:T(8,128)(2,1)S(1)}, bf16[2,128,16,128]{3,2,1,0:T(8,128)(2,1)}, u32[]{:S(2)}) copy-start(bf16[2,128,16,128]{3,2,1,0:T(8,128)(2,1)} %refs_0_.1) | copy-start | bytes 3145732
  5.3 0.7 %copy-start.4 = (s32[16]{0:T(128)S(1)}, s32[16]{0:T(128)}, u32[]{:S(2)}) copy-start(s32[16]{0:T(128)} %dims.11) | copy-start | bytes 196
  5.9 1.8 %copy-start.3 = (bf16[8,16,16,16]{3,2,1,0:T(8,128)(2,1)S(1)}, bf16[8,16,16,16]{3,2,1,0:T(8,128)(2,1)}, u32[]{:S(2)}) copy-start(bf16[8,16,16,16]{3,2,1,0:T(8,128)(2,1)} %coef.1) | copy-start | bytes 196612
  5.9 1.8 %copy-start.5 = (s32[8,16]{1,0:T(8,128)S(1)}, s32[8,16]{1,0:T(8,128)}, u32[]{:S(2)}) copy-start(s32[8,16]{1,0:T(8,128)} %mask.1) | copy-start | bytes 1540
  5.9 1.8 %copy-start.6 = (s32[8]{0:T(128)S(1)}, s32[8]{0:T(128)}, u32[]{:S(2)}) copy-start(s32[8]{0:T(128)} %shift.1) | copy-start | bytes 100
  5.9 3.9 %copy-start.2 = (bf16[8,2,128,128]{3,2,1,0:T(8,128)(2,1)S(1)}, bf16[8,2,128,128]{3,2,1,0:T(8,128)(2,1)}, u32[]{:S(2)}) copy-start(bf16[8,2,128,128]{3,2,1,0:T(8,128)(2,1)} %env.1) | copy-start | bytes 1572868
  8.5 9.8 %collective-permute-start = (bf16[1296,128]{1,0:T(8,128)(2,1)S(1)}, bf16[1296,128]{1,0:T(8,128)(2,1)S(1)}, u32[]{:S(2)}, u32[]{:S(2)}) collective-permute-start(bf16[1296,128]{1,0:T(8,128)(2,1)S(1)} %pack.1.refs_2_), channel_id=1, source_target_pairs={{2,0},{0,2},{3,1},{1,3},{6,4},{4,6},{7,5},{5,7},{10,8},{8,10},{11,... | collective-permute-start | bytes 995336 | tf_op jit(solution)/shard_map/ppermute | solution.py:21
  10.4 10.8 %collective-permute-start.4 = (bf16[8,64,128]{2,1,0:T(8,128)(2,1)S(1)}, bf16[8,64,128]{2,1,0:T(8,128)(2,1)S(1)}, u32[]{:S(2)}, u32[]{:S(2)}) collective-permute-start(bf16[8,64,128]{2,1,0:T(8,128)(2,1)S(1)} %get-tuple-element.24), channel_id=1, source_target_pairs={{2,0},{0,2},{3,1},{1,3},{6,4},{4,6},{7,5},{5,7},{10,8},{8,10},{11,... | collective-permute-start | bytes 393224 | tf_op jit(solution)/shard_map/ppermute | solution.py:21
  10.7 12.6 %collective-permute-start.7 = (bf16[8,64,128]{2,1,0:T(8,128)(2,1)S(1)}, bf16[8,64,128]{2,1,0:T(8,128)(2,1)S(1)}, u32[]{:S(2)}, u32[]{:S(2)}) collective-permute-start(bf16[8,64,128]{2,1,0:T(8,128)(2,1)S(1)} %get-tuple-element.25), channel_id=1, source_target_pairs={{2,0},{0,2},{3,1},{1,3},{6,4},{4,6},{7,5},{5,7},{10,8},{8,10},{11,... | collective-permute-start | bytes 393224 | tf_op jit(solution)/shard_map/ppermute | solution.py:21
  13.7 22.9 %collective-permute-start.3 = (bf16[8,128,128]{2,1,0:T(8,128)(2,1)S(1)}, bf16[8,128,128]{2,1,0:T(8,128)(2,1)S(1)}, u32[]{:S(2)}, u32[]{:S(2)}) collective-permute-start(bf16[8,128,128]{2,1,0:T(8,128)(2,1)S(1)} %get-tuple-element.29), channel_id=1, source_target_pairs={{0,13},{1,12},{4,9},{5,8},{8,5},{9,4},{12,1},{13,0},{2,15},{3,14},... | collective-permute-start | bytes 786440 | tf_op jit(solution)/shard_map/ppermute | solution.py:373
  21.2 17.2 %collective-permute-start.5 = (bf16[8,64,128]{2,1,0:T(8,128)(2,1)S(1)}, bf16[8,64,128]{2,1,0:T(8,128)(2,1)S(1)}, u32[]{:S(2)}, u32[]{:S(2)}) collective-permute-start(bf16[8,64,128]{2,1,0:T(8,128)(2,1)S(1)} %collective-permute-done.4), channel_id=1, source_target_pairs={{0,13},{1,12},{4,9},{5,8},{8,5},{9,4},{12,1},{13,0},{2,15},{3,14},... | collective-permute-start | bytes 393224 | tf_op jit(solution)/shard_map/ppermute | solution.py:373
  23.3 18.9 %collective-permute-start.8 = (bf16[8,64,128]{2,1,0:T(8,128)(2,1)S(1)}, bf16[8,64,128]{2,1,0:T(8,128)(2,1)S(1)}, u32[]{:S(2)}, u32[]{:S(2)}) collective-permute-start(bf16[8,64,128]{2,1,0:T(8,128)(2,1)S(1)} %collective-permute-done.7), channel_id=1, source_target_pairs={{0,13},{1,12},{4,9},{5,8},{8,5},{9,4},{12,1},{13,0},{2,15},{3,14},... | collective-permute-start | bytes 393224 | tf_op jit(solution)/shard_map/ppermute | solution.py:373
  39.7 7.7 %collective-permute-start.6 = (bf16[65,8,128]{2,1,0:T(8,128)(2,1)S(1)}, bf16[65,8,128]{2,1,0:T(8,128)(2,1)S(1)}, u32[]{:S(2)}, u32[]{:S(2)}) collective-permute-start(bf16[65,8,128]{2,1,0:T(8,128)(2,1)S(1)} %give_0.1), channel_id=1, source_target_pairs={{0,2},{2,0},{1,3},{3,1},{4,6},{6,4},{5,7},{7,5},{8,10},{10,8},{9,1... | collective-permute-start | bytes 399368 | tf_op jit(solution)/shard_map/ppermute | solution.py:376
  43.6 3.9 %collective-permute-start.9 = (bf16[64,8,128]{2,1,0:T(8,128)(2,1)S(1)}, bf16[64,8,128]{2,1,0:T(8,128)(2,1)S(1)}, u32[]{:S(2)}, u32[]{:S(2)}) collective-permute-start(bf16[64,8,128]{2,1,0:T(8,128)(2,1)S(1)} %give_1.1), channel_id=1, source_target_pairs={{0,2},{2,0},{1,3},{3,1},{4,6},{6,4},{5,7},{7,5},{8,10},{10,8},{9,1... | collective-permute-start | bytes 393224 | tf_op jit(solution)/shard_map/ppermute | solution.py:376

commit v3 on v2

--- a/solution.py
+++ b/solution.py
@@ -13,6 +13,7 @@
 SMEM = pltpu.SMEM
 SMALL = pl.CostEstimate(flops=1 << 10, bytes_accessed=1 << 10, transcendentals=0)
 SOME = pl.CostEstimate(flops=1 << 28, bytes_accessed=1 << 20, transcendentals=0)
+MORE = pl.CostEstimate(flops=1 << 30, bytes_accessed=1 << 20, transcendentals=0)
 PAD = 1
 
 
@@ -21,41 +22,48 @@
     return lax.ppermute(block, axis, [((i + step) % count, i) for i in range(count)])
 
 
-def turn_kernel(which, info, dims, *refs):
+def turn_kernel(which, info, dims, psi, *refs):
     turned, plane = refs[-2:]
-    _, block, states, width = refs[0].shape
+    _, block, states, width = psi.shape
     place, places = info[0], info[1]
     odd = lax.rem(place, 2)
-    home = (place, place + 1 - 2 * odd, place - 1 + 2 * odd)[which]
+    home = (place, place + 1 - 2 * odd, place - 1 + 2 * odd)[min(which, 2)]
+    entry = slot_of(which, pl.program_id(0), info) % 2
     rows = lax.broadcasted_iota(jnp.int32, (block, width), 0)
     lanes = lax.broadcasted_iota(jnp.int32, (block, width), 1)
-
-    def move(psi, entry):
-        source = jnp.clip(home * 2 + entry, 0, 2 * places - 1)
-        keep = (rows < dims[source]) & (lanes < dims[2 * places - 1 - source])
-        plane[...] = psi.astype(F32).reshape(block * states, width)
-        for t in range(states):
-            piece = plane[pl.ds(t, block, stride=states), :]
-            turned[entry, :, t * width : (t + 1) * width] = jnp.where(keep, piece, 0.0).astype(BF16)
-
-    for e in range(2):
-        move(refs[0][e], e)
+    source = jnp.clip(home * 2 + entry, 0, 2 * places - 1)
+    keep = (rows < dims[source]) & (lanes < dims[2 * places - 1 - source])
+    plane[...] = psi[0].astype(F32).reshape(block * states, width)
+    for t in range(states):
+        piece = plane[pl.ds(t, block, stride=states), :]
+        turned[0, :, t * width : (t + 1) * width] = jnp.where(keep, piece, 0.0).astype(BF16)
+
+
+def slot_of(which, i, info):
+    if which < 2:
+        return 2 * which + i
+    return 4 + (info[3] if which == 2 else 1 - info[3])
 
 
 def turn(which, info, dims, psi, *before):
-    _, block, states, width = psi.shape
+    count, block, states, width = psi.shape
     return pl.pallas_call(
         functools.partial(turn_kernel, which),
-        grid=(1,),
         out_shape=jax.ShapeDtypeStruct((6, block, states * width), BF16),
-        in_specs=[pl.BlockSpec(memory_space=SMEM)] * 2
-        + [pl.BlockSpec(psi.shape, lambda i: (0, 0, 0, 0))]
-        + [pl.BlockSpec(memory_space=pl.ANY)] * len(before),
-        out_specs=pl.BlockSpec((2, block, states * width), lambda i: (which, 0, 0)),
-        scratch_shapes=[VMEM((block * states, width), F32)],
+        grid_spec=pltpu.PrefetchScalarGridSpec(
+            num_scalar_prefetch=2,
+            grid=(count,),
+            in_specs=[pl.BlockSpec((1, block, states, width), lambda i, info, dims: (i, 0, 0, 0))]
+            + [pl.BlockSpec(memory_space=pl.ANY)] * len(before),
+            out_specs=pl.BlockSpec(
+                (1, block, states * width),
+                lambda i, info, dims: (slot_of(which, i, info), 0, 0),
+            ),
+            scratch_shapes=[VMEM((block * states, width), F32)],
+        ),
         input_output_aliases={3: 0} if before else {},
         compiler_params=pltpu.CompilerParams(vmem_limit_bytes=16 << 20),
-        cost_estimate=SMALL,
+        cost_estimate=MORE if which == 2 else SMALL,
         name=f"turn_{which}",
     )(info, dims, psi, *before)
 
@@ -92,6 +100,22 @@
         cost_estimate=SMALL,
         name="pack",
     )(info, mask, shift, coef, left)
+
+
+def cut_psi_kernel(info, psi, out):
+    out[0] = psi[info[3]]
+
+
+def cut_psi(info, psi):
+    return pl.pallas_call(
+        cut_psi_kernel,
+        out_shape=jax.ShapeDtypeStruct((1, *psi.shape[1:]), BF16),
+        in_specs=[pl.BlockSpec(memory_space=SMEM), pl.BlockSpec(memory_space=VMEM)],
+        out_specs=pl.BlockSpec(memory_space=VMEM),
+        compiler_params=pltpu.CompilerParams(vmem_limit_bytes=8 << 20),
+        cost_estimate=SMALL,
+        name="cut_psi",
+    )(info, psi)
 
 
 def cut_env_kernel(entries, rows, info, env, *outs):
@@ -225,24 +249,24 @@
     return jnp.where(keep, total.reshape(cube), 0.0)
 
 
-def begin_kernel(info, given, kept, right, given_out, kept_out):
-    v_dev = right.shape[0]
-    blocks = [[right[v] for v in range(v_dev)]]
+def begin_kernel(info, given, kept, low, high, given_out, kept_out):
+    v_dev = low.shape[0]
+    blocks = [[jnp.concatenate([low[v], high[v]], axis=0) for v in range(v_dev)]]
     given_out[...] = product(given, blocks, [info[2] * v_dev])
     kept_out[...] = product(kept, blocks, [info[2] * v_dev])
 
 
-def begin(info, given, kept, right):
-    rows, width = given.shape[0], right.shape[1]
+def begin(info, given, kept, low, high):
+    rows, width = given.shape[0], 2 * low.shape[1]
     return pl.pallas_call(
         begin_kernel,
         out_shape=[jax.ShapeDtypeStruct((rows, width), F32)] * 2,
-        in_specs=[pl.BlockSpec(memory_space=SMEM)] + [pl.BlockSpec(memory_space=VMEM)] * 3,
+        in_specs=[pl.BlockSpec(memory_space=SMEM)] + [pl.BlockSpec(memory_space=VMEM)] * 4,
         out_specs=[pl.BlockSpec(memory_space=VMEM)] * 2,
         compiler_params=pltpu.CompilerParams(vmem_limit_bytes=24 << 20),
         cost_estimate=SOME,
         name="begin",
-    )(info, given, kept, right)
+    )(info, given, kept, low, high)
 
 
 def others(info, v_dev, groups):
@@ -353,7 +377,9 @@
     w_dev = left_env.shape[0]
     channels = mpo_coef.shape[1]
     groups = lax.axis_size("mpo")
+    reps = lax.axis_size("rep")
     spots = ("sec", "rep")
+    whole = ("sec", "mpo", "rep")
     places = lax.axis_size(spots)
     place = lax.axis_index(spots)
     group = lax.axis_index("mpo")
@@ -369,37 +395,58 @@
             route += [(low, low + 1), (low + 1, low)]
         return lax.ppermute(block, spots, route)
 
+    def spot(place, group):
+        return (place // reps * groups + group) * reps + place % reps
+
+    def cross(block):
+        route = []
+        for p in range(places):
+            for g in range(0, groups, 2):
+                source, target = (g + 1, g) if p % 2 == 0 else (g, g + 1)
+                route.append((spot(p, source), spot(p, target)))
+        return lax.ppermute(block, whole, route)
+
     def mirrored(block):
         return lax.ppermute(block, spots, [(i, places - 1 - i) for i in range(places)])
 
+    def slanted(block, step):
+        route = []
+        for p in range(places):
+            for g in range(groups):
+                route.append((spot(places - 1 - p, (g + step) % groups), spot(p, g)))
+        return lax.ppermute(block, whole, route)
+
     def beside(block):
         return lax.ppermute(block, "mpo", [(g, g ^ 1) for g in range(groups)])
 
     steps = range(1, groups)
-    far = swap(psi, 1)
     near = swap(psi, 0)
-    turned = turn(0, info, dims, psi)
-    sent = pack(after(info, turned), mpo_mask, shift, mpo_coef, left_env, groups - 1)
+    one = cut_psi(info, psi)
+    early = swap(one, 1)
+    turned = turn(1, after(info, one), dims, near)
+    size = width // 2
+    pairs = [(j, (r, size)) for r in (0, size) for j in range(groups)]
+    entries, rows = [(1 + j) % 2 for j, _ in pairs], [r for _, r in pairs]
+    cuts = cut_env(after(info, turned), right_env, entries, rows)
+    low, high = cuts[:groups], cuts[groups:]
+    sent = pack(after(info, *cuts), mpo_mask, shift, mpo_coef, left_env, groups - 1)
     parcels = [sent[0]] + [ring(p, "mpo", j) for j, p in zip(steps, sent)]
-    size = width // 2
-    pairs = [(0, (0, width))] + [(j, (r, size)) for r in (0, size) for j in steps]
-    entries, rows = [(1 + j) % 2 for j, _ in pairs], [r for _, r in pairs]
-    cuts = cut_env(after(info, *sent), right_env, entries, rows)
-    passed = [ring(c, "mpo", j) for c, (j, _) in zip(cuts[1:], pairs[1:])]
-    turned = turn(1, after(info, *cuts), dims, near, turned)
-    same = mirrored(after(cuts[0], turned))
-    rights = [mirrored(after(c, turned)) for c in passed]
-    turned = turn(2, info, dims, far, turned)
+    same = [mirrored(low[0]), mirrored(after(high[0], *sent))]
+    crossed = cross(after(early, *sent))
+    turned = turn(0, after(info, *sent), dims, psi, turned)
+    turned = turn(2, after(info, same[0]), dims, early, turned)
+    low = [slanted(after(c, turned), j) for c, j in zip(low[1:], steps)]
+    high = [slanted(after(c, turned), j) for c, j in zip(high[1:], steps)]
+    turned = turn(3, info, dims, crossed, turned)
     last = w_dev * block + channels * states
     shifts = jnp.concatenate([p[last, :w_dev] for p in parcels]).astype(jnp.int32)
     given, kept = mix(info, shifts, channels, turned, left_env, parcels)
-    given_sum, kept_sum = begin(info, given, kept, same)
-    low, high = rights[: groups - 1], rights[groups - 1 :]
+    given_sum, kept_sum = begin(info, given, kept, *same)
     to_give = give(0, after(info, given_sum), dims, given, given_sum, low)
     zero = beside(to_give)
     part = give(1, after(info, given_sum, to_give), dims, given, given_sum, high)
     one = beside(part)
-    result = keep(after(info, part), dims, kept, kept_sum, rights)
+    result = keep(after(info, part), dims, kept, kept_sum, low + high)
     result = finish(info, zero, one, result)
     if share != 8:
         result = lax.dynamic_slice_in_dim(result, group * share - begin_kept, share, 2)

time: 49 us -> 47.1 us (0.961)
  waiting for transfers between devices: 13.7 us -> 7.23 us
  starting transfers between devices: 13.4 us -> 16.6 us
  Pallas kernels: 19.5 us -> 20.8 us
    ppermute x0 -> x3, starting transfers between devices: none -> 8.21 us  [the longest x1 5.5 us: cross(): return lax.ppermute(block, whole, route)]
    ppermute x3 -> x1, waiting for transfers between devices: 7.28 us -> 0.01 us  [ring(): lax.ppermute(block, axis, [((i + step) % count, i) for i in range(count)])]
    ppermute x3 -> x2, starting transfers between devices: 4.03 us -> 0.91 us  [mirrored(): lax.ppermute(block, spots, [(i, places - 1 - i) for i in range(places)])]
    ppermute x2, waiting for transfers between devices: 1.84 us -> 3.46 us  [beside(): return lax.ppermute(block, 'mpo', [(g, g ^ 1) for g in range(groups)])]
    ppermute x3 -> x1, starting transfers between devices: 2.81 us -> 1.28 us  [ring(): lax.ppermute(block, axis, [((i + step) % count, i) for i in range(count)])]
    pallas_call x3 -> x5, Pallas kernels: 5.23 us -> 6.45 us  [the longest x4 5.87 us: turn(): pl.pallas_call(functools.partial(turn_kernel, which), out_shape=jax.Shape...]
    ppermute x2, waiting for transfers between devices: 4.6 us -> 3.5 us  [swap(): return lax.ppermute(block, spots, route)]
    unnamed x14 -> x18, local copies, waits for them, and re-layouts: 1.9 us -> 1.91 us
  transfers between devices with their start and end apart: 10 -> 10, of which waited for: 5 -> 3; matrix products, arithmetic and copies ran while one was open for 0% -> 0% of each run, Pallas kernels for 37% -> 41%
where the time goes in v3:
time: 47.1 us; the launch traced here: 46.9 us
  Pallas kernels  20.8 us (44%)
  starting transfers between devices  16.6 us (35%)
  waiting for transfers between devices  7.23 us (15%)
  local copies, waits for them, and re-layouts  2 us (4%)
    pallas_call x4, Pallas kernels, turn(): pl.pallas_call(functools.partial(turn_kernel, which), out_shape=jax.Shape...  5.87 us
    ppermute x1, starting transfers between devices, cross(): return lax.ppermute(block, whole, route)  5.5 us
    pallas_call x1, Pallas kernels, mix(): pl.pallas_call(mix_kernel, out_shape=[jax.ShapeDtypeStruct((block * 8, ch...  5.19 us
    ppermute x2, starting transfers between devices, swap(): return lax.ppermute(block, spots, route)  3.9 us
    ppermute x2, waiting for transfers between devices, swap(): return lax.ppermute(block, spots, route)  3.5 us
    ppermute x2, waiting for transfers between devices, beside(): return lax.ppermute(block, 'mpo', [(g, g ^ 1) for g in range(groups)])  3.46 us
    ppermute x2, starting transfers between devices, slanted(): return lax.ppermute(block, whole, route)  2.71 us
    pallas_call x2, Pallas kernels, give(): pl.pallas_call(functools.partial(give_kernel, piece), out_shape=jax.Shape...  2.61 us
  transfers between devices with their start and end apart: 10, of which 3 were waited for; matrix products, arithmetic and copies ran while one was open for 0% of the time, Pallas kernels for 41%

profile of v3, /device:TPU:9, one launch (start us, length us, event | category | flops | bytes accessed | tf_op | source)
XLA Modules:
  0.0 46.9 jit_solution(8715021839357564285)
XLA Ops:
  0.0 0.7 %collective-permute-start = (bf16[2,128,16,128]{3,2,1,0:T(8,128)(2,1)}, bf16[2,128,16,128]{3,2,1,0:T(8,128)(2,1)S(1)}, u32[]{:S(2)}, u32[]{:S(2)}) collective-permute-start(bf16[2,128,16,128]{3,2,1,0:T(8,128)(2,1)} %psi.3), channel_id=1, source_target_pairs={{0,1},{1,0},{4,5},{5,4},{8,9},{9,8},{12,13},{13,12},{2,3},{3,2},{6... | collective-permute-start | bytes 3145736 | tf_op jit(solution)/shard_map/ppermute | solution.py:396
  0.7 0.0 copy-start.7
  0.7 0.1 stack.23.info
  0.8 0.0 copy-start
  0.8 1.2 %copy-done = bf16[2,128,16,128]{3,2,1,0:T(8,128)(2,1)S(1)} copy-done((bf16[2,128,16,128]{3,2,1,0:T(8,128)(2,1)S(1)}, bf16[2,128,16,128]{3,2,1,0:T(8,128)(2,1)}, u32[]{:S(2)}) %copy-start) | copy-done | bytes 1048600
  2.0 0.0 copy-start.3
  2.0 0.0 copy-start.2
  2.0 0.0 copy-start.4
  2.0 0.0 copy-start.8
  2.0 0.6 %cut_psi.1 = bf16[1,128,16,128]{3,2,1,0:T(8,128)(2,1)S(1)} custom-call(s32[6]{0:T(128)S(1)} %stack.23.info, bf16[2,128,16,128]{3,2,1,0:T(8,128)(2,1)S(1)} %copy-done), custom_call_target="tpu_custom_call" | custom-call | flops 1024 | bytes 1024 | tf_op jit(solution)/shard_map/cut_psi/pallas_call | solution.py:110
  2.6 0.0 copy-start.1
  2.6 3.2 %collective-permute-start.2 = (bf16[1,128,16,128]{3,2,1,0:T(8,128)(2,1)S(1)}, bf16[1,128,16,128]{3,2,1,0:T(8,128)(2,1)S(1)}, u32[]{:S(2)}, u32[]{:S(2)}) collective-permute-start(bf16[1,128,16,128]{3,2,1,0:T(8,128)(2,1)S(1)} %cut_psi.1), channel_id=1, source_target_pairs={{1,4},{4,1},{5,8},{8,5},{9,12},{12,9},{3,6},{6,3},{7,10},{10,7},{1... | collective-permute-start | bytes 1572872 | tf_op jit(solution)/shard_map/ppermute | solution.py:396
  5.8 0.0 collective-permute-done.psi
  5.8 0.0 copy-start.5
  5.9 0.6 %copy-done.5 = s32[16]{0:T(128)S(1)} copy-done((s32[16]{0:T(128)S(1)}, s32[16]{0:T(128)}, u32[]{:S(2)}) %copy-start.5) | copy-done | bytes 88
  6.5 1.8 %turn_1.1.refs_0_ = bf16[6,128,2048]{2,1,0:T(8,128)(2,1)S(1)} custom-call(s32[6]{0:T(128)S(1)} %stack.23.info, s32[16]{0:T(128)S(1)} %copy-done.5, bf16[2,128,16,128]{3,2,1,0:T(8,128)(2,1)S(1)} %collective-permute-done.psi), custom_call_target="tpu_custom_call" | custom-call | flops 1024 | bytes 1024 | tf_op jit(solution)/shard_map/turn_1/pallas_call | solution.py:50
  8.3 0.0 copy-done.3
  8.3 0.6 %cut_env.1 = (bf16[8,64,128]{2,1,0:T(8,128)(2,1)S(1)}, bf16[8,64,128]{2,1,0:T(8,128)(2,1)S(1)}, bf16[8,64,128]{2,1,0:T(8,128)(2,1)S(1)}, bf16[8,64,128]{2,1,0:T(8,128)(2,1)S(1)}) custom-call(s32[6]{0:T(128)S(1)} %stack.23.info, bf16[8,2,128,128]{3,2,1,0:T(8,128)(2,1)S(1)} %copy-done.3), custom_call_target="tpu_custom_call" | custom-call | flops 1024 | bytes 1024 | tf_op jit(solution)/shard_map/cut_env/pallas_call | solution.py:129
  8.9 0.0 copy-done.7
  8.9 0.0 copy-done.2
  8.9 0.0 copy-done.4
  8.9 0.0 copy-done.8
  8.9 0.8 %pack.1.refs_2_ = bf16[1296,128]{1,0:T(8,128)(2,1)S(1)} custom-call(s32[6]{0:T(128)S(1)} %stack.23.info, s32[8,16]{1,0:T(8,128)S(1)} %copy-done.7, s32[8]{0:T(128)S(1)} %copy-done.8, bf16[8,16,16,16]{3,2,1,0:T(8,128)(2,1)S(1)} %copy-done.4, bf16[8,2,128,128]{3,2,1,0:T(8,128)(2,1)S(1)} %copy-done.2), custom_call_target="tpu_custom_call" | custom-call | flops 1024 | bytes 1024 | tf_op jit(solution)/shard_map/pack/pallas_call | solution.py:94
  9.8 1.3 %collective-permute-start.1 = (bf16[1296,128]{1,0:T(8,128)(2,1)S(1)}, bf16[1296,128]{1,0:T(8,128)(2,1)S(1)}, u32[]{:S(2)}, u32[]{:S(2)}) collective-permute-start(bf16[1296,128]{1,0:T(8,128)(2,1)S(1)} %pack.1.refs_2_), channel_id=1, source_target_pairs={{2,0},{0,2},{3,1},{1,3},{6,4},{4,6},{7,5},{5,7},{10,8},{8,10},{11,... | collective-permute-start | bytes 995336 | tf_op jit(solution)/shard_map/ppermute | solution.py:22
  11.0 0.8 %collective-permute-start.4 = (bf16[8,64,128]{2,1,0:T(8,128)(2,1)S(1)}, bf16[8,64,128]{2,1,0:T(8,128)(2,1)S(1)}, u32[]{:S(2)}, u32[]{:S(2)}) collective-permute-start(bf16[8,64,128]{2,1,0:T(8,128)(2,1)S(1)} %get-tuple-element.27), channel_id=1, source_target_pairs={{0,13},{1,12},{4,9},{5,8},{8,5},{9,4},{12,1},{13,0},{2,15},{3,14},... | collective-permute-start | bytes 393224 | tf_op jit(solution)/shard_map/ppermute | solution.py:410
  11.9 3.5 %collective-permute-done.2.psi = bf16[1,128,16,128]{3,2,1,0:T(8,128)(2,1)S(1)} collective-permute-done((bf16[1,128,16,128]{3,2,1,0:T(8,128)(2,1)S(1)}, bf16[1,128,16,128]{3,2,1,0:T(8,128)(2,1)S(1)}, u32[]{:S(2)}, u32[]{:S(2)}) %collective-permute-start.2) | collective-permute-done | bytes 524320 | tf_op jit(solution)/shard_map/ppermute | solution.py:396
  15.4 5.5 %collective-permute-start.3 = (bf16[1,128,16,128]{3,2,1,0:T(8,128)(2,1)S(1)}, bf16[1,128,16,128]{3,2,1,0:T(8,128)(2,1)S(1)}, u32[]{:S(2)}, u32[]{:S(2)}) collective-permute-start(bf16[1,128,16,128]{3,2,1,0:T(8,128)(2,1)S(1)} %collective-permute-done.2.psi), channel_id=1, source_target_pairs={{2,0},{1,3},{6,4},{5,7},{10,8},{9,11},{14,12},{13,15},{18,16},{17,... | collective-permute-start | bytes 1572872 | tf_op jit(solution)/shard_map/ppermute | solution.py:407
  20.9 0.0 copy-done.1
  20.9 1.8 %turn_0.1.refs_0_ = bf16[6,128,2048]{2,1,0:T(8,128)(2,1)S(1)} custom-call(s32[6]{0:T(128)S(1)} %stack.23.info, s32[16]{0:T(128)S(1)} %copy-done.5, bf16[2,128,16,128]{3,2,1,0:T(8,128)(2,1)S(1)} %copy-done.1, bf16[6,128,2048]{2,1,0:T(8,128)(2,1)S(1)} %turn_1.1.refs_0_), custom_call_target="tpu_custom_call", output_to_operand_aliasing={{}: (3, {})} | custom-call | flops 1024 | bytes 1024 | tf_op jit(solution)/shard_map/turn_0/pallas_call | solution.py:50
  22.7 0.1 collective-permute-start.5
  22.8 0.0 collective-permute-done.4.low
  22.8 1.1 %turn_2.1.refs_0_ = bf16[6,128,2048]{2,1,0:T(8,128)(2,1)S(1)} custom-call(s32[6]{0:T(128)S(1)} %stack.23.info, s32[16]{0:T(128)S(1)} %copy-done.5, bf16[1,128,16,128]{3,2,1,0:T(8,128)(2,1)S(1)} %collective-permute-done.2.psi, bf16[6,128,2048]{2,1,0:T(8,128)(2,1)S(1)} %turn_0.1.refs_0_), custom_call_target="tpu_custom_call", output_to_operand_aliasing={{}: (3, {})} | custom-call | flops 1073741824 | bytes 1048576 | tf_op jit(solution)/shard_map/turn_2/pallas_call | solution.py:50
  23.9 0.9 %collective-permute-start.6 = (bf16[8,64,128]{2,1,0:T(8,128)(2,1)S(1)}, bf16[8,64,128]{2,1,0:T(8,128)(2,1)S(1)}, u32[]{:S(2)}, u32[]{:S(2)}) collective-permute-start(bf16[8,64,128]{2,1,0:T(8,128)(2,1)S(1)} %get-tuple-element.40), channel_id=1, source_target_pairs={{15,0},{13,2},{14,1},{12,3},{11,4},{9,6},{10,5},{8,7},{7,8},{5,10}... | collective-permute-start | bytes 393224 | tf_op jit(solution)/shard_map/ppermute | solution.py:417
  24.8 1.9 %collective-permute-start.8 = (bf16[8,64,128]{2,1,0:T(8,128)(2,1)S(1)}, bf16[8,64,128]{2,1,0:T(8,128)(2,1)S(1)}, u32[]{:S(2)}, u32[]{:S(2)}) collective-permute-start(bf16[8,64,128]{2,1,0:T(8,128)(2,1)S(1)} %get-tuple-element.42), channel_id=1, source_target_pairs={{15,0},{13,2},{14,1},{12,3},{11,4},{9,6},{10,5},{8,7},{7,8},{5,10}... | collective-permute-start | bytes 393224 | tf_op jit(solution)/shard_map/ppermute | solution.py:417
  26.7 0.0 collective-permute-done.1.refs_3_
  26.7 0.1 maximum_convert_fusion.shift
  26.7 0.2 collective-permute-done.3.psi
  27.0 1.1 %turn_3.1.refs_0_ = bf16[6,128,2048]{2,1,0:T(8,128)(2,1)S(1)} custom-call(s32[6]{0:T(128)S(1)} %stack.23.info, s32[16]{0:T(128)S(1)} %copy-done.5, bf16[1,128,16,128]{3,2,1,0:T(8,128)(2,1)S(1)} %collective-permute-done.3.psi, bf16[6,128,2048]{2,1,0:T(8,128)(2,1)S(1)} %turn_2.1.refs_0_), custom_call_target="tpu_custom_call", output_to_operand_aliasing={{}: (3, {})} | custom-call | flops 1024 | bytes 1024 | tf_op jit(solution)/shard_map/turn_3/pallas_call | solution.py:50
  28.1 5.2 %mix.1 = (bf16[1024,2048]{1,0:T(8,128)(2,1)S(1)}, bf16[1024,2048]{1,0:T(8,128)(2,1)S(1)}) custom-call(s32[6]{0:T(128)S(1)} %stack.23.info, s32[16]{0:T(128)S(1)} %maximum_convert_fusion.shift, bf16[6,128,2048]{2,1,0:T(8,128)(2,1)S(1)} %turn_3.1.refs_0_, bf16[8,2,128,128]{3,2,1,0:T(8,128)(2,1)S(1)} %copy-done.2, bf16[1296,128]{1,0:T(8,128)(2,1)S(1)} %pack.1.refs_2_, ...), custom_call_target="tpu_custom_call" | custom-call | flops 1024 | bytes 1024 | tf_op jit(solution)/shard_map/mix/pallas_call | solution.py:211
  33.3 0.0 collective-permute-done.5.high
  33.3 0.0 copy-start.6
  33.3 1.8 %begin.1 = (f32[1024,128]{1,0:T(8,128)S(1)}, f32[1024,128]{1,0:T(8,128)S(1)}) custom-call(s32[6]{0:T(128)S(1)} %stack.23.info, bf16[1024,2048]{1,0:T(8,128)(2,1)S(1)} %get-tuple-element.35.given.mixed, bf16[1024,2048]{1,0:T(8,128)(2,1)S(1)} %get-tuple-element.36.kept.mixed, bf16[8,64,128]{2,1,0:T(8,128)(2,1)S(1)} %collective-permute-done.4.low, ...), custom_call_target="tpu_custom_call" | custom-call | flops 268435456 | bytes 1048576 | tf_op jit(solution)/shard_map/begin/pallas_call | solution.py:261
  35.1 0.0 collective-permute-done.6.refs_0_
  35.2 0.0 copy-done.6
  35.2 1.3 %give_0.1 = bf16[65,8,128]{2,1,0:T(8,128)(2,1)S(1)} custom-call(s32[6]{0:T(128)S(1)} %stack.23.info, s32[16]{0:T(128)S(1)} %copy-done.6, bf16[1024,2048]{1,0:T(8,128)(2,1)S(1)} %get-tuple-element.35.given.mixed, f32[1024,128]{1,0:T(8,128)S(1)} %get-tuple-element.38.before, bf16[8,64,128]{2,1,0:T(8,128)(2,1)S(1)} %collective-permute-done.6.refs_0_), custom_call_target="tpu_custom_call" | custom-call | flops 268435456 | bytes 1048576 | tf_op jit(solution)/shard_map/give_0/pallas_call | solution.py:291
  36.5 2.2 %collective-permute-start.7 = (bf16[65,8,128]{2,1,0:T(8,128)(2,1)S(1)}, bf16[65,8,128]{2,1,0:T(8,128)(2,1)S(1)}, u32[]{:S(2)}, u32[]{:S(2)}) collective-permute-start(bf16[65,8,128]{2,1,0:T(8,128)(2,1)S(1)} %give_0.1), channel_id=1, source_target_pairs={{0,2},{2,0},{1,3},{3,1},{4,6},{6,4},{5,7},{7,5},{8,10},{10,8},{9,1... | collective-permute-start | bytes 399368 | tf_op jit(solution)/shard_map/ppermute | solution.py:420
  38.7 0.0 collective-permute-done.8.refs_0_.refs_1_
  38.7 1.3 %give_1.1 = bf16[64,8,128]{2,1,0:T(8,128)(2,1)S(1)} custom-call(s32[6]{0:T(128)S(1)} %stack.23.info, s32[16]{0:T(128)S(1)} %copy-done.6, bf16[1024,2048]{1,0:T(8,128)(2,1)S(1)} %get-tuple-element.35.given.mixed, f32[1024,128]{1,0:T(8,128)S(1)} %get-tuple-element.38.before, bf16[8,64,128]{2,1,0:T(8,128)(2,1)S(1)} %collective-permute-done.8.refs_0_.refs_1_), custom_call_target="tpu_custom_call" | custom-call | flops 268435456 | bytes 1048576 | tf_op jit(solution)/shard_map/give_1/pallas_call | solution.py:291
  40.0 0.1 collective-permute-start.9
  40.1 2.0 %keep.1.result = bf16[2,128,8,128]{3,2,1,0:T(8,128)(2,1)} custom-call(s32[6]{0:T(128)S(1)} %stack.23.info, s32[16]{0:T(128)S(1)} %copy-done.6, bf16[1024,2048]{1,0:T(8,128)(2,1)S(1)} %get-tuple-element.36.kept.mixed, f32[1024,128]{1,0:T(8,128)S(1)} %get-tuple-element.44.before, bf16[8,64,128]{2,1,0:T(8,128)(2,1)S(1)} %collective-permute-done.6.refs_0_, ...), custom_call_target="tpu_custom_call" | custom-call | flops 1024 | bytes 1024 | tf_op jit(solution)/shard_map/keep/pallas_call | solution.py:318
  42.1 3.5 %collective-permute-done.9.one = bf16[64,8,128]{2,1,0:T(8,128)(2,1)S(1)} collective-permute-done((bf16[64,8,128]{2,1,0:T(8,128)(2,1)S(1)}, bf16[64,8,128]{2,1,0:T(8,128)(2,1)S(1)}, u32[]{:S(2)}, u32[]{:S(2)}) %collective-permute-start.9) | collective-permute-done | bytes 131104 | tf_op jit(solution)/shard_map/ppermute | solution.py:420
  45.5 0.0 collective-permute-done.7.zero
  45.5 1.4 %finish.1 = bf16[2,128,8,128]{3,2,1,0:T(8,128)(2,1)} custom-call(s32[6]{0:T(128)S(1)} %stack.23.info, bf16[65,8,128]{2,1,0:T(8,128)(2,1)S(1)} %collective-permute-done.7.zero, bf16[64,8,128]{2,1,0:T(8,128)(2,1)S(1)} %collective-permute-done.9.one, bf16[2,128,8,128]{3,2,1,0:T(8,128)(2,1)} %keep.1.result), custom_call_target="tpu_custom_call", output_to_operand_aliasing={{}: (3, {})} | custom-call | flops 1024 | bytes 1024 | tf_op jit(solution)/shard_map/finish/pallas_call | solution.py:353
  (2 shorter events, 0.0 us)
Async XLA Ops:
  0.0 5.8 %collective-permute-start = (bf16[2,128,16,128]{3,2,1,0:T(8,128)(2,1)}, bf16[2,128,16,128]{3,2,1,0:T(8,128)(2,1)S(1)}, u32[]{:S(2)}, u32[]{:S(2)}) collective-permute-start(bf16[2,128,16,128]{3,2,1,0:T(8,128)(2,1)} %psi.3), channel_id=1, source_target_pairs={{0,1},{1,0},{4,5},{5,4},{8,9},{9,8},{12,13},{13,12},{2,3},{3,2},{6... | collective-permute-start | bytes 3145736 | tf_op jit(solution)/shard_map/ppermute | solution.py:396
  0.7 8.2 %copy-start.7 = (s32[8,16]{1,0:T(8,128)S(1)}, s32[8,16]{1,0:T(8,128)}, u32[]{:S(2)}) copy-start(s32[8,16]{1,0:T(8,128)} %mask.1) | copy-start | bytes 1540
  0.8 1.2 %copy-start = (bf16[2,128,16,128]{3,2,1,0:T(8,128)(2,1)S(1)}, bf16[2,128,16,128]{3,2,1,0:T(8,128)(2,1)}, u32[]{:S(2)}) copy-start(bf16[2,128,16,128]{3,2,1,0:T(8,128)(2,1)} %psi.3) | copy-start | bytes 3145732
  2.0 6.3 %copy-start.3 = (bf16[8,2,128,128]{3,2,1,0:T(8,128)(2,1)S(1)}, bf16[8,2,128,128]{3,2,1,0:T(8,128)(2,1)}, u32[]{:S(2)}) copy-start(bf16[8,2,128,128]{3,2,1,0:T(8,128)(2,1)} %env.1) | copy-start | bytes 1572868
  2.0 6.9 %copy-start.2 = (bf16[8,2,128,128]{3,2,1,0:T(8,128)(2,1)S(1)}, bf16[8,2,128,128]{3,2,1,0:T(8,128)(2,1)}, u32[]{:S(2)}) copy-start(bf16[8,2,128,128]{3,2,1,0:T(8,128)(2,1)} %refs_1_.1) | copy-start | bytes 1572868
  2.0 6.9 %copy-start.4 = (bf16[8,16,16,16]{3,2,1,0:T(8,128)(2,1)S(1)}, bf16[8,16,16,16]{3,2,1,0:T(8,128)(2,1)}, u32[]{:S(2)}) copy-start(bf16[8,16,16,16]{3,2,1,0:T(8,128)(2,1)} %coef.1) | copy-start | bytes 196612
  2.0 6.9 %copy-start.8 = (s32[8]{0:T(128)S(1)}, s32[8]{0:T(128)}, u32[]{:S(2)}) copy-start(s32[8]{0:T(128)} %shift.1) | copy-start | bytes 100
  2.6 18.3 %copy-start.1 = (bf16[2,128,16,128]{3,2,1,0:T(8,128)(2,1)S(1)}, bf16[2,128,16,128]{3,2,1,0:T(8,128)(2,1)}, u32[]{:S(2)}) copy-start(bf16[2,128,16,128]{3,2,1,0:T(8,128)(2,1)} %psi.3) | copy-start | bytes 3145732
  2.6 12.8 %collective-permute-start.2 = (bf16[1,128,16,128]{3,2,1,0:T(8,128)(2,1)S(1)}, bf16[1,128,16,128]{3,2,1,0:T(8,128)(2,1)S(1)}, u32[]{:S(2)}, u32[]{:S(2)}) collective-permute-start(bf16[1,128,16,128]{3,2,1,0:T(8,128)(2,1)S(1)} %cut_psi.1), channel_id=1, source_target_pairs={{1,4},{4,1},{5,8},{8,5},{9,12},{12,9},{3,6},{6,3},{7,10},{10,7},{1... | collective-permute-start | bytes 1572872 | tf_op jit(solution)/shard_map/ppermute | solution.py:396
  5.8 0.7 %copy-start.5 = (s32[16]{0:T(128)S(1)}, s32[16]{0:T(128)}, u32[]{:S(2)}) copy-start(s32[16]{0:T(128)} %dims.13) | copy-start | bytes 196
  9.8 16.9 %collective-permute-start.1 = (bf16[1296,128]{1,0:T(8,128)(2,1)S(1)}, bf16[1296,128]{1,0:T(8,128)(2,1)S(1)}, u32[]{:S(2)}, u32[]{:S(2)}) collective-permute-start(bf16[1296,128]{1,0:T(8,128)(2,1)S(1)} %pack.1.refs_2_), channel_id=1, source_target_pairs={{2,0},{0,2},{3,1},{1,3},{6,4},{4,6},{7,5},{5,7},{10,8},{8,10},{11,... | collective-permute-start | bytes 995336 | tf_op jit(solution)/shard_map/ppermute | solution.py:22
  11.0 11.8 %collective-permute-start.4 = (bf16[8,64,128]{2,1,0:T(8,128)(2,1)S(1)}, bf16[8,64,128]{2,1,0:T(8,128)(2,1)S(1)}, u32[]{:S(2)}, u32[]{:S(2)}) collective-permute-start(bf16[8,64,128]{2,1,0:T(8,128)(2,1)S(1)} %get-tuple-element.27), channel_id=1, source_target_pairs={{0,13},{1,12},{4,9},{5,8},{8,5},{9,4},{12,1},{13,0},{2,15},{3,14},... | collective-permute-start | bytes 393224 | tf_op jit(solution)/shard_map/ppermute | solution.py:410
  15.4 11.6 %collective-permute-start.3 = (bf16[1,128,16,128]{3,2,1,0:T(8,128)(2,1)S(1)}, bf16[1,128,16,128]{3,2,1,0:T(8,128)(2,1)S(1)}, u32[]{:S(2)}, u32[]{:S(2)}) collective-permute-start(bf16[1,128,16,128]{3,2,1,0:T(8,128)(2,1)S(1)} %collective-permute-done.2.psi), channel_id=1, source_target_pairs={{2,0},{1,3},{6,4},{5,7},{10,8},{9,11},{14,12},{13,15},{18,16},{17,... | collective-permute-start | bytes 1572872 | tf_op jit(solution)/shard_map/ppermute | solution.py:407
  22.7 10.6 %collective-permute-start.5 = (bf16[8,64,128]{2,1,0:T(8,128)(2,1)S(1)}, bf16[8,64,128]{2,1,0:T(8,128)(2,1)S(1)}, u32[]{:S(2)}, u32[]{:S(2)}) collective-permute-start(bf16[8,64,128]{2,1,0:T(8,128)(2,1)S(1)} %get-tuple-element.37), channel_id=1, source_target_pairs={{0,13},{1,12},{4,9},{5,8},{8,5},{9,4},{12,1},{13,0},{2,15},{3,14},... | collective-permute-start | bytes 393224 | tf_op jit(solution)/shard_map/ppermute | solution.py:410
  23.9 11.2 %collective-permute-start.6 = (bf16[8,64,128]{2,1,0:T(8,128)(2,1)S(1)}, bf16[8,64,128]{2,1,0:T(8,128)(2,1)S(1)}, u32[]{:S(2)}, u32[]{:S(2)}) collective-permute-start(bf16[8,64,128]{2,1,0:T(8,128)(2,1)S(1)} %get-tuple-element.40), channel_id=1, source_target_pairs={{15,0},{13,2},{14,1},{12,3},{11,4},{9,6},{10,5},{8,7},{7,8},{5,10}... | collective-permute-start | bytes 393224 | tf_op jit(solution)/shard_map/ppermute | solution.py:417
  24.8 13.9 %collective-permute-start.8 = (bf16[8,64,128]{2,1,0:T(8,128)(2,1)S(1)}, bf16[8,64,128]{2,1,0:T(8,128)(2,1)S(1)}, u32[]{:S(2)}, u32[]{:S(2)}) collective-permute-start(bf16[8,64,128]{2,1,0:T(8,128)(2,1)S(1)} %get-tuple-element.42), channel_id=1, source_target_pairs={{15,0},{13,2},{14,1},{12,3},{11,4},{9,6},{10,5},{8,7},{7,8},{5,10}... | collective-permute-start | bytes 393224 | tf_op jit(solution)/shard_map/ppermute | solution.py:417
  33.3 1.8 %copy-start.6 = (s32[16]{0:T(128)S(1)}, s32[16]{0:T(128)}, u32[]{:S(2)}) copy-start(s32[16]{0:T(128)} %dims.13) | copy-start | bytes 196
  36.5 9.1 %collective-permute-start.7 = (bf16[65,8,128]{2,1,0:T(8,128)(2,1)S(1)}, bf16[65,8,128]{2,1,0:T(8,128)(2,1)S(1)}, u32[]{:S(2)}, u32[]{:S(2)}) collective-permute-start(bf16[65,8,128]{2,1,0:T(8,128)(2,1)S(1)} %give_0.1), channel_id=1, source_target_pairs={{0,2},{2,0},{1,3},{3,1},{4,6},{6,4},{5,7},{7,5},{8,10},{10,8},{9,1... | collective-permute-start | bytes 399368 | tf_op jit(solution)/shard_map/ppermute | solution.py:420
  40.0 5.5 %collective-permute-start.9 = (bf16[64,8,128]{2,1,0:T(8,128)(2,1)S(1)}, bf16[64,8,128]{2,1,0:T(8,128)(2,1)S(1)}, u32[]{:S(2)}, u32[]{:S(2)}) collective-permute-start(bf16[64,8,128]{2,1,0:T(8,128)(2,1)S(1)} %give_1.1), channel_id=1, source_target_pairs={{0,2},{2,0},{1,3},{3,1},{4,6},{6,4},{5,7},{7,5},{8,10},{10,8},{9,1... | collective-permute-start | bytes 393224 | tf_op jit(solution)/shard_map/ppermute | solution.py:420

commit v4 on v3

--- a/solution.py
+++ b/solution.py
@@ -249,36 +249,19 @@
     return jnp.where(keep, total.reshape(cube), 0.0)
 
 
-def begin_kernel(info, given, kept, low, high, given_out, kept_out):
-    v_dev = low.shape[0]
-    blocks = [[jnp.concatenate([low[v], high[v]], axis=0) for v in range(v_dev)]]
-    given_out[...] = product(given, blocks, [info[2] * v_dev])
-    kept_out[...] = product(kept, blocks, [info[2] * v_dev])
-
-
-def begin(info, given, kept, low, high):
-    rows, width = given.shape[0], 2 * low.shape[1]
-    return pl.pallas_call(
-        begin_kernel,
-        out_shape=[jax.ShapeDtypeStruct((rows, width), F32)] * 2,
-        in_specs=[pl.BlockSpec(memory_space=SMEM)] + [pl.BlockSpec(memory_space=VMEM)] * 4,
-        out_specs=[pl.BlockSpec(memory_space=VMEM)] * 2,
-        compiler_params=pltpu.CompilerParams(vmem_limit_bytes=24 << 20),
-        cost_estimate=SOME,
-        name="begin",
-    )(info, given, kept, low, high)
-
-
 def others(info, v_dev, groups):
     return [lax.rem(info[2] + j, groups) * v_dev for j in range(1, groups)]
 
 
-def give_kernel(piece, info, dims, mixed, before, *refs):
+def spots_of(info, v_dev, count):
+    return [info[2] * v_dev] + others(info, v_dev, count)
+
+
+def give_kernel(piece, info, dims, mixed, *refs):
     rights, out = refs[:-1], refs[-1]
     v_dev, size, _ = rights[0].shape
     blocks = [[right[v] for v in range(v_dev)] for right in rights]
-    total = product(mixed, blocks, others(info, v_dev, len(rights) + 1))
-    total += before[:, piece * size : (piece + 1) * size]
+    total = product(mixed, blocks, spots_of(info, v_dev, len(rights)))
     cube = masked(total, info, dims, piece * size)
     half = cube.shape[0] // 2
     out[:half] = jnp.concatenate([cube[:half], cube[half:]], axis=2).astype(BF16)
@@ -286,21 +269,21 @@
         out[half:] = jnp.zeros((1, *out.shape[1:]), BF16)
 
 
-def give(piece, info, dims, mixed, before, rights):
+def give(piece, info, dims, mixed, rights):
     size = rights[0].shape[1]
     return pl.pallas_call(
         functools.partial(give_kernel, piece),
         out_shape=jax.ShapeDtypeStruct((mixed.shape[0] // 16 + 1 - piece, 8, 2 * size), BF16),
         in_specs=[pl.BlockSpec(memory_space=SMEM)] * 2
-        + [pl.BlockSpec(memory_space=VMEM)] * (2 + len(rights)),
+        + [pl.BlockSpec(memory_space=VMEM)] * (1 + len(rights)),
         out_specs=pl.BlockSpec(memory_space=VMEM),
         compiler_params=pltpu.CompilerParams(vmem_limit_bytes=24 << 20),
         cost_estimate=SOME,
         name=f"give_{piece}",
-    )(info, dims, mixed, before, *rights)
-
-
-def keep_kernel(info, dims, mixed, before, *refs):
+    )(info, dims, mixed, *rights)
+
+
+def keep_kernel(info, dims, mixed, *refs):
     rights, out = refs[:-1], refs[-1]
     half = len(rights) // 2
     v_dev = rights[0].shape[0]
@@ -308,20 +291,19 @@
         [jnp.concatenate([low[v], high[v]], axis=0) for v in range(v_dev)]
         for low, high in zip(rights[:half], rights[half:])
     ]
-    total = before[...] + product(mixed, blocks, others(info, v_dev, half + 1))
+    total = product(mixed, blocks, spots_of(info, v_dev, half))
     out[0] = masked(total, info, dims, 0).astype(BF16)
 
 
-def keep(info, dims, mixed, before, rights):
-    rows, width = before.shape
-    whole = lambda a: pl.BlockSpec(a.shape, lambda i, info, dims, n=a.ndim: (0,) * n)
+def keep(info, dims, mixed, rights):
+    rows, width = mixed.shape[0], rights[0].shape[2]
     return pl.pallas_call(
         keep_kernel,
         out_shape=jax.ShapeDtypeStruct((2, rows // 8, 8, width), BF16),
         grid_spec=pltpu.PrefetchScalarGridSpec(
             num_scalar_prefetch=2,
             grid=(1,),
-            in_specs=[whole(a) for a in (mixed, before, *rights)],
+            in_specs=[pl.BlockSpec(memory_space=VMEM)] * (1 + len(rights)),
             out_specs=pl.BlockSpec(
                 (1, rows // 8, 8, width), lambda i, info, dims: (info[3], 0, 0, 0)
             ),
@@ -329,7 +311,7 @@
         compiler_params=pltpu.CompilerParams(vmem_limit_bytes=24 << 20),
         cost_estimate=SMALL,
         name="keep",
-    )(info, dims, mixed, before, *rights)
+    )(info, dims, mixed, *rights)
 
 
 def finish_kernel(info, zero, one, result, out):
@@ -431,22 +413,23 @@
     low, high = cuts[:groups], cuts[groups:]
     sent = pack(after(info, *cuts), mpo_mask, shift, mpo_coef, left_env, groups - 1)
     parcels = [sent[0]] + [ring(p, "mpo", j) for j, p in zip(steps, sent)]
+    passed = [ring(c, "mpo", j) for c, j in zip(high[1:], steps)]
     same = [mirrored(low[0]), mirrored(after(high[0], *sent))]
     crossed = cross(after(early, *sent))
     turned = turn(0, after(info, *sent), dims, psi, turned)
     turned = turn(2, after(info, same[0]), dims, early, turned)
     low = [slanted(after(c, turned), j) for c, j in zip(low[1:], steps)]
-    high = [slanted(after(c, turned), j) for c, j in zip(high[1:], steps)]
+    high = [mirrored(after(p, turned)) for p in passed]
     turned = turn(3, info, dims, crossed, turned)
     last = w_dev * block + channels * states
     shifts = jnp.concatenate([p[last, :w_dev] for p in parcels]).astype(jnp.int32)
     given, kept = mix(info, shifts, channels, turned, left_env, parcels)
-    given_sum, kept_sum = begin(info, given, kept, *same)
-    to_give = give(0, after(info, given_sum), dims, given, given_sum, low)
+    low, high = [same[0], *low], [same[1], *high]
+    to_give = give(0, info, dims, given, low)
     zero = beside(to_give)
-    part = give(1, after(info, given_sum, to_give), dims, given, given_sum, high)
+    part = give(1, after(info, to_give), dims, given, high)
     one = beside(part)
-    result = keep(after(info, part), dims, kept, kept_sum, low + high)
+    result = keep(after(info, part), dims, kept, low + high)
     result = finish(info, zero, one, result)
     if share != 8:
         result = lax.dynamic_slice_in_dim(result, group * share - begin_kept, share, 2)

time: 47.1 us -> 47.2 us (level)
  waiting for transfers between devices: 7.23 us -> 8.66 us
  starting transfers between devices: 16.6 us -> 15.5 us
    ppermute x2 -> x1, waiting for transfers between devices: 0.05 us -> 2.18 us  [slanted(): return lax.ppermute(block, whole, route)]
    ppermute x2 -> x1, starting transfers between devices: 2.71 us -> 0.86 us  [slanted(): return lax.ppermute(block, whole, route)]
    pallas_call x1 -> x0, Pallas kernels: 1.78 us -> none  [begin(): pl.pallas_call(begin_kernel, out_shape=[jax.ShapeDtypeStruct((rows, width...]
    ppermute x2, waiting for transfers between devices: 3.46 us -> 2.18 us  [beside(): return lax.ppermute(block, 'mpo', [(g, g ^ 1) for g in range(groups)])]
    pallas_call x2, Pallas kernels: 2.61 us -> 3.69 us  [give(): pl.pallas_call(functools.partial(give_kernel, piece), out_shape=jax.Shape...]
    ppermute x2 -> x3, starting transfers between devices: 0.91 us -> 1.92 us  [mirrored(): lax.ppermute(block, spots, [(i, places - 1 - i) for i in range(places)])]
    ppermute x1, waiting for transfers between devices: 0.22 us -> 1.05 us  [cross(): return lax.ppermute(block, whole, route)]
    ppermute x2, starting transfers between devices: 2.32 us -> 1.75 us  [beside(): return lax.ppermute(block, 'mpo', [(g, g ^ 1) for g in range(groups)])]
  transfers between devices with their start and end apart: 10 -> 11, of which waited for: 3 -> 4; matrix products, arithmetic and copies ran while one was open for 0% -> 0% of each run, Pallas kernels for 41% -> 41%
where the time goes in v4:
time: 47.2 us; the launch traced here: 47 us
  Pallas kernels  20.6 us (44%)
  starting transfers between devices  15.5 us (33%)
  waiting for transfers between devices  8.66 us (18%)
  local copies, waits for them, and re-layouts  2 us (4%)
    pallas_call x4, Pallas kernels, turn(): pl.pallas_call(functools.partial(turn_kernel, which), out_shape=jax.Shape...  5.87 us
    ppermute x1, starting transfers between devices, cross(): return lax.ppermute(block, whole, route)  5.5 us
    pallas_call x1, Pallas kernels, mix(): pl.pallas_call(mix_kernel, out_shape=[jax.ShapeDtypeStruct((block * 8, ch...  5.19 us
    ppermute x2, starting transfers between devices, swap(): return lax.ppermute(block, spots, route)  3.9 us
    pallas_call x2, Pallas kernels, give(): pl.pallas_call(functools.partial(give_kernel, piece), out_shape=jax.Shape...  3.69 us
    ppermute x2, waiting for transfers between devices, swap(): return lax.ppermute(block, spots, route)  3.25 us
    pallas_call x1, Pallas kernels, keep(): pl.pallas_call(keep_kernel, out_shape=jax.ShapeDtypeStruct((2, rows // 8,...  2.5 us
    ppermute x1, waiting for transfers between devices, slanted(): return lax.ppermute(block, whole, route)  2.18 us
  transfers between devices with their start and end apart: 11, of which 4 were waited for; matrix products, arithmetic and copies ran while one was open for 0% of the time, Pallas kernels for 41%

profile of v4, /device:TPU:9, one launch (start us, length us, event | category | flops | bytes accessed | tf_op | source)
XLA Modules:
  0.0 47.0 jit_solution(4485690386891018053)
XLA Ops:
  0.0 0.7 %collective-permute-start = (bf16[2,128,16,128]{3,2,1,0:T(8,128)(2,1)}, bf16[2,128,16,128]{3,2,1,0:T(8,128)(2,1)S(1)}, u32[]{:S(2)}, u32[]{:S(2)}) collective-permute-start(bf16[2,128,16,128]{3,2,1,0:T(8,128)(2,1)} %psi.3), channel_id=1, source_target_pairs={{0,1},{1,0},{4,5},{5,4},{8,9},{9,8},{12,13},{13,12},{2,3},{3,2},{6... | collective-permute-start | bytes 3145736 | tf_op jit(solution)/shard_map/ppermute | solution.py:378
  0.7 0.0 copy-start.7
  0.7 0.1 stack.23.info
  0.8 0.0 copy-start
  0.8 1.2 %copy-done = bf16[2,128,16,128]{3,2,1,0:T(8,128)(2,1)S(1)} copy-done((bf16[2,128,16,128]{3,2,1,0:T(8,128)(2,1)S(1)}, bf16[2,128,16,128]{3,2,1,0:T(8,128)(2,1)}, u32[]{:S(2)}) %copy-start) | copy-done | bytes 1048600
  2.0 0.0 copy-start.3
  2.0 0.0 copy-start.2
  2.0 0.0 copy-start.4
  2.0 0.0 copy-start.8
  2.0 0.6 %cut_psi.1 = bf16[1,128,16,128]{3,2,1,0:T(8,128)(2,1)S(1)} custom-call(s32[6]{0:T(128)S(1)} %stack.23.info, bf16[2,128,16,128]{3,2,1,0:T(8,128)(2,1)S(1)} %copy-done), custom_call_target="tpu_custom_call" | custom-call | flops 1024 | bytes 1024 | tf_op jit(solution)/shard_map/cut_psi/pallas_call | solution.py:110
  2.6 0.0 copy-start.1
  2.6 3.2 %collective-permute-start.2 = (bf16[1,128,16,128]{3,2,1,0:T(8,128)(2,1)S(1)}, bf16[1,128,16,128]{3,2,1,0:T(8,128)(2,1)S(1)}, u32[]{:S(2)}, u32[]{:S(2)}) collective-permute-start(bf16[1,128,16,128]{3,2,1,0:T(8,128)(2,1)S(1)} %cut_psi.1), channel_id=1, source_target_pairs={{1,4},{4,1},{5,8},{8,5},{9,12},{12,9},{3,6},{6,3},{7,10},{10,7},{1... | collective-permute-start | bytes 1572872 | tf_op jit(solution)/shard_map/ppermute | solution.py:378
  5.8 0.0 collective-permute-done.psi
  5.8 0.0 copy-start.5
  5.9 0.6 %copy-done.5 = s32[16]{0:T(128)S(1)} copy-done((s32[16]{0:T(128)S(1)}, s32[16]{0:T(128)}, u32[]{:S(2)}) %copy-start.5) | copy-done | bytes 88
  6.5 1.8 %turn_1.1.refs_0_ = bf16[6,128,2048]{2,1,0:T(8,128)(2,1)S(1)} custom-call(s32[6]{0:T(128)S(1)} %stack.23.info, s32[16]{0:T(128)S(1)} %copy-done.5, bf16[2,128,16,128]{3,2,1,0:T(8,128)(2,1)S(1)} %collective-permute-done.psi), custom_call_target="tpu_custom_call" | custom-call | flops 1024 | bytes 1024 | tf_op jit(solution)/shard_map/turn_1/pallas_call | solution.py:50
  8.3 0.0 copy-done.3
  8.3 0.6 %cut_env.1 = (bf16[8,64,128]{2,1,0:T(8,128)(2,1)S(1)}, bf16[8,64,128]{2,1,0:T(8,128)(2,1)S(1)}, bf16[8,64,128]{2,1,0:T(8,128)(2,1)S(1)}, bf16[8,64,128]{2,1,0:T(8,128)(2,1)S(1)}) custom-call(s32[6]{0:T(128)S(1)} %stack.23.info, bf16[8,2,128,128]{3,2,1,0:T(8,128)(2,1)S(1)} %copy-done.3), custom_call_target="tpu_custom_call" | custom-call | flops 1024 | bytes 1024 | tf_op jit(solution)/shard_map/cut_env/pallas_call | solution.py:129
  8.9 0.0 copy-done.7
  8.9 0.0 copy-done.2
  8.9 0.0 copy-done.4
  8.9 0.0 copy-done.8
  8.9 0.8 %pack.1.refs_2_ = bf16[1296,128]{1,0:T(8,128)(2,1)S(1)} custom-call(s32[6]{0:T(128)S(1)} %stack.23.info, s32[8,16]{1,0:T(8,128)S(1)} %copy-done.7, s32[8]{0:T(128)S(1)} %copy-done.8, bf16[8,16,16,16]{3,2,1,0:T(8,128)(2,1)S(1)} %copy-done.4, bf16[8,2,128,128]{3,2,1,0:T(8,128)(2,1)S(1)} %copy-done.2), custom_call_target="tpu_custom_call" | custom-call | flops 1024 | bytes 1024 | tf_op jit(solution)/shard_map/pack/pallas_call | solution.py:94
  9.8 1.3 %collective-permute-start.1 = (bf16[1296,128]{1,0:T(8,128)(2,1)S(1)}, bf16[1296,128]{1,0:T(8,128)(2,1)S(1)}, u32[]{:S(2)}, u32[]{:S(2)}) collective-permute-start(bf16[1296,128]{1,0:T(8,128)(2,1)S(1)} %pack.1.refs_2_), channel_id=1, source_target_pairs={{2,0},{0,2},{3,1},{1,3},{6,4},{4,6},{7,5},{5,7},{10,8},{8,10},{11,... | collective-permute-start | bytes 995336 | tf_op jit(solution)/shard_map/ppermute | solution.py:22
  11.0 0.8 %collective-permute-start.4 = (bf16[8,64,128]{2,1,0:T(8,128)(2,1)S(1)}, bf16[8,64,128]{2,1,0:T(8,128)(2,1)S(1)}, u32[]{:S(2)}, u32[]{:S(2)}) collective-permute-start(bf16[8,64,128]{2,1,0:T(8,128)(2,1)S(1)} %get-tuple-element.24), channel_id=1, source_target_pairs={{0,13},{1,12},{4,9},{5,8},{8,5},{9,4},{12,1},{13,0},{2,15},{3,14},... | collective-permute-start | bytes 393224 | tf_op jit(solution)/shard_map/ppermute | solution.py:392
  11.9 0.3 collective-permute-start.8
  12.1 3.2 %collective-permute-done.2.psi = bf16[1,128,16,128]{3,2,1,0:T(8,128)(2,1)S(1)} collective-permute-done((bf16[1,128,16,128]{3,2,1,0:T(8,128)(2,1)S(1)}, bf16[1,128,16,128]{3,2,1,0:T(8,128)(2,1)S(1)}, u32[]{:S(2)}, u32[]{:S(2)}) %collective-permute-start.2) | collective-permute-done | bytes 524320 | tf_op jit(solution)/shard_map/ppermute | solution.py:378
  15.4 5.5 %collective-permute-start.3 = (bf16[1,128,16,128]{3,2,1,0:T(8,128)(2,1)S(1)}, bf16[1,128,16,128]{3,2,1,0:T(8,128)(2,1)S(1)}, u32[]{:S(2)}, u32[]{:S(2)}) collective-permute-start(bf16[1,128,16,128]{3,2,1,0:T(8,128)(2,1)S(1)} %collective-permute-done.2.psi), channel_id=1, source_target_pairs={{2,0},{1,3},{6,4},{5,7},{10,8},{9,11},{14,12},{13,15},{18,16},{17,... | collective-permute-start | bytes 1572872 | tf_op jit(solution)/shard_map/ppermute | solution.py:389
  20.9 0.0 copy-done.1
  20.9 1.8 %turn_0.1.refs_0_ = bf16[6,128,2048]{2,1,0:T(8,128)(2,1)S(1)} custom-call(s32[6]{0:T(128)S(1)} %stack.23.info, s32[16]{0:T(128)S(1)} %copy-done.5, bf16[2,128,16,128]{3,2,1,0:T(8,128)(2,1)S(1)} %copy-done.1, bf16[6,128,2048]{2,1,0:T(8,128)(2,1)S(1)} %turn_1.1.refs_0_), custom_call_target="tpu_custom_call", output_to_operand_aliasing={{}: (3, {})} | custom-call | flops 1024 | bytes 1024 | tf_op jit(solution)/shard_map/turn_0/pallas_call | solution.py:50
  22.7 0.1 collective-permute-start.7
  22.8 0.0 collective-permute-done.4.refs_0_
  22.8 1.1 %turn_2.1.refs_0_ = bf16[6,128,2048]{2,1,0:T(8,128)(2,1)S(1)} custom-call(s32[6]{0:T(128)S(1)} %stack.23.info, s32[16]{0:T(128)S(1)} %copy-done.5, bf16[1,128,16,128]{3,2,1,0:T(8,128)(2,1)S(1)} %collective-permute-done.2.psi, bf16[6,128,2048]{2,1,0:T(8,128)(2,1)S(1)} %turn_0.1.refs_0_), custom_call_target="tpu_custom_call", output_to_operand_aliasing={{}: (3, {})} | custom-call | flops 1073741824 | bytes 1048576 | tf_op jit(solution)/shard_map/turn_2/pallas_call | solution.py:50
  23.9 0.0 collective-permute-done.8
  24.0 0.9 %collective-permute-start.5 = (bf16[8,64,128]{2,1,0:T(8,128)(2,1)S(1)}, bf16[8,64,128]{2,1,0:T(8,128)(2,1)S(1)}, u32[]{:S(2)}, u32[]{:S(2)}) collective-permute-start(bf16[8,64,128]{2,1,0:T(8,128)(2,1)S(1)} %get-tuple-element.33), channel_id=1, source_target_pairs={{15,0},{13,2},{14,1},{12,3},{11,4},{9,6},{10,5},{8,7},{7,8},{5,10}... | collective-permute-start | bytes 393224 | tf_op jit(solution)/shard_map/ppermute | solution.py:399
  24.8 1.0 %collective-permute-start.9 = (bf16[8,64,128]{2,1,0:T(8,128)(2,1)S(1)}, bf16[8,64,128]{2,1,0:T(8,128)(2,1)S(1)}, u32[]{:S(2)}, u32[]{:S(2)}) collective-permute-start(bf16[8,64,128]{2,1,0:T(8,128)(2,1)S(1)} %collective-permute-done.8), channel_id=1, source_target_pairs={{0,13},{1,12},{4,9},{5,8},{8,5},{9,4},{12,1},{13,0},{2,15},{3,14},... | collective-permute-start | bytes 393224 | tf_op jit(solution)/shard_map/ppermute | solution.py:392
  25.8 0.0 collective-permute-done.1.refs_3_
  25.8 0.1 maximum_convert_fusion.shift
  25.9 1.0 %collective-permute-done.3.psi = bf16[1,128,16,128]{3,2,1,0:T(8,128)(2,1)S(1)} collective-permute-done((bf16[1,128,16,128]{3,2,1,0:T(8,128)(2,1)S(1)}, bf16[1,128,16,128]{3,2,1,0:T(8,128)(2,1)S(1)}, u32[]{:S(2)}, u32[]{:S(2)}) %collective-permute-start.3) | collective-permute-done | bytes 524320 | tf_op jit(solution)/shard_map/ppermute | solution.py:389
  27.0 1.1 %turn_3.1.refs_0_ = bf16[6,128,2048]{2,1,0:T(8,128)(2,1)S(1)} custom-call(s32[6]{0:T(128)S(1)} %stack.23.info, s32[16]{0:T(128)S(1)} %copy-done.5, bf16[1,128,16,128]{3,2,1,0:T(8,128)(2,1)S(1)} %collective-permute-done.3.psi, bf16[6,128,2048]{2,1,0:T(8,128)(2,1)S(1)} %turn_2.1.refs_0_), custom_call_target="tpu_custom_call", output_to_operand_aliasing={{}: (3, {})} | custom-call | flops 1024 | bytes 1024 | tf_op jit(solution)/shard_map/turn_3/pallas_call | solution.py:50
  28.1 0.0 copy-start.6
  28.1 5.2 %mix.1 = (bf16[1024,2048]{1,0:T(8,128)(2,1)S(1)}, bf16[1024,2048]{1,0:T(8,128)(2,1)S(1)}) custom-call(s32[6]{0:T(128)S(1)} %stack.23.info, s32[16]{0:T(128)S(1)} %maximum_convert_fusion.shift, bf16[6,128,2048]{2,1,0:T(8,128)(2,1)S(1)} %turn_3.1.refs_0_, bf16[8,2,128,128]{3,2,1,0:T(8,128)(2,1)S(1)} %copy-done.2, bf16[1296,128]{1,0:T(8,128)(2,1)S(1)} %pack.1.refs_2_, ...), custom_call_target="tpu_custom_call" | custom-call | flops 1024 | bytes 1024 | tf_op jit(solution)/shard_map/mix/pallas_call | solution.py:211
  33.3 2.2 %collective-permute-done.5.refs_1_ = bf16[8,64,128]{2,1,0:T(8,128)(2,1)S(1)} collective-permute-done((bf16[8,64,128]{2,1,0:T(8,128)(2,1)S(1)}, bf16[8,64,128]{2,1,0:T(8,128)(2,1)S(1)}, u32[]{:S(2)}, u32[]{:S(2)}) %collective-permute-start.5) | collective-permute-done | bytes 131104 | tf_op jit(solution)/shard_map/ppermute | solution.py:399
  35.5 0.0 copy-done.6
  35.5 1.8 %give_0.1 = bf16[65,8,128]{2,1,0:T(8,128)(2,1)S(1)} custom-call(s32[6]{0:T(128)S(1)} %stack.23.info, s32[16]{0:T(128)S(1)} %copy-done.6, bf16[1024,2048]{1,0:T(8,128)(2,1)S(1)} %get-tuple-element.32.mixed, bf16[8,64,128]{2,1,0:T(8,128)(2,1)S(1)} %collective-permute-done.4.refs_0_, bf16[8,64,128]{2,1,0:T(8,128)(2,1)S(1)} %collective-permute-done.5.refs_1_), custom_call_target="tpu_custom_call" | custom-call | flops 268435456 | bytes 1048576 | tf_op jit(solution)/shard_map/give_0/pallas_call | solution.py:274
  37.4 1.7 %collective-permute-start.6 = (bf16[65,8,128]{2,1,0:T(8,128)(2,1)S(1)}, bf16[65,8,128]{2,1,0:T(8,128)(2,1)S(1)}, u32[]{:S(2)}, u32[]{:S(2)}) collective-permute-start(bf16[65,8,128]{2,1,0:T(8,128)(2,1)S(1)} %give_0.1), channel_id=1, source_target_pairs={{0,2},{2,0},{1,3},{3,1},{4,6},{6,4},{5,7},{7,5},{8,10},{10,8},{9,1... | collective-permute-start | bytes 399368 | tf_op jit(solution)/shard_map/ppermute | solution.py:402
  39.0 0.0 collective-permute-done.7.refs_0_.refs_2_
  39.0 0.0 collective-permute-done.9.refs_1_.refs_3_
  39.0 1.8 %give_1.1 = bf16[64,8,128]{2,1,0:T(8,128)(2,1)S(1)} custom-call(s32[6]{0:T(128)S(1)} %stack.23.info, s32[16]{0:T(128)S(1)} %copy-done.6, bf16[1024,2048]{1,0:T(8,128)(2,1)S(1)} %get-tuple-element.32.mixed, bf16[8,64,128]{2,1,0:T(8,128)(2,1)S(1)} %collective-permute-done.7.refs_0_.refs_2_, bf16[8,64,128]{2,1,0:T(8,128)(2,1)S(1)} %collective-permute-done.9.refs_1_.refs_3_), custom_call_target="tpu_custom_call" | custom-call | flops 268435456 | bytes 1048576 | tf_op jit(solution)/shard_map/give_1/pallas_call | solution.py:274
  40.9 0.1 collective-permute-start.10
  40.9 2.5 %keep.1.result = bf16[2,128,8,128]{3,2,1,0:T(8,128)(2,1)} custom-call(s32[6]{0:T(128)S(1)} %stack.23.info, s32[16]{0:T(128)S(1)} %copy-done.6, bf16[1024,2048]{1,0:T(8,128)(2,1)S(1)} %get-tuple-element.38.mixed, bf16[8,64,128]{2,1,0:T(8,128)(2,1)S(1)} %collective-permute-done.4.refs_0_, bf16[8,64,128]{2,1,0:T(8,128)(2,1)S(1)} %collective-permute-done.5.refs_1_, ...), custom_call_target="tpu_custom_call" | custom-call | flops 1024 | bytes 1024 | tf_op jit(solution)/shard_map/keep/pallas_call | solution.py:300
  43.4 2.2 %collective-permute-done.10.one = bf16[64,8,128]{2,1,0:T(8,128)(2,1)S(1)} collective-permute-done((bf16[64,8,128]{2,1,0:T(8,128)(2,1)S(1)}, bf16[64,8,128]{2,1,0:T(8,128)(2,1)S(1)}, u32[]{:S(2)}, u32[]{:S(2)}) %collective-permute-start.10) | collective-permute-done | bytes 131104 | tf_op jit(solution)/shard_map/ppermute | solution.py:402
  45.6 0.0 collective-permute-done.6.zero
  45.6 1.4 %finish.1 = bf16[2,128,8,128]{3,2,1,0:T(8,128)(2,1)} custom-call(s32[6]{0:T(128)S(1)} %stack.23.info, bf16[65,8,128]{2,1,0:T(8,128)(2,1)S(1)} %collective-permute-done.6.zero, bf16[64,8,128]{2,1,0:T(8,128)(2,1)S(1)} %collective-permute-done.10.one, bf16[2,128,8,128]{3,2,1,0:T(8,128)(2,1)} %keep.1.result), custom_call_target="tpu_custom_call", output_to_operand_aliasing={{}: (3, {})} | custom-call | flops 1024 | bytes 1024 | tf_op jit(solution)/shard_map/finish/pallas_call | solution.py:335
  (2 shorter events, 0.0 us)
Async XLA Ops:
  0.0 5.8 %collective-permute-start = (bf16[2,128,16,128]{3,2,1,0:T(8,128)(2,1)}, bf16[2,128,16,128]{3,2,1,0:T(8,128)(2,1)S(1)}, u32[]{:S(2)}, u32[]{:S(2)}) collective-permute-start(bf16[2,128,16,128]{3,2,1,0:T(8,128)(2,1)} %psi.3), channel_id=1, source_target_pairs={{0,1},{1,0},{4,5},{5,4},{8,9},{9,8},{12,13},{13,12},{2,3},{3,2},{6... | collective-permute-start | bytes 3145736 | tf_op jit(solution)/shard_map/ppermute | solution.py:378
  0.7 8.2 %copy-start.7 = (s32[8,16]{1,0:T(8,128)S(1)}, s32[8,16]{1,0:T(8,128)}, u32[]{:S(2)}) copy-start(s32[8,16]{1,0:T(8,128)} %mask.1) | copy-start | bytes 1540
  0.8 1.2 %copy-start = (bf16[2,128,16,128]{3,2,1,0:T(8,128)(2,1)S(1)}, bf16[2,128,16,128]{3,2,1,0:T(8,128)(2,1)}, u32[]{:S(2)}) copy-start(bf16[2,128,16,128]{3,2,1,0:T(8,128)(2,1)} %psi.3) | copy-start | bytes 3145732
  2.0 6.3 %copy-start.3 = (bf16[8,2,128,128]{3,2,1,0:T(8,128)(2,1)S(1)}, bf16[8,2,128,128]{3,2,1,0:T(8,128)(2,1)}, u32[]{:S(2)}) copy-start(bf16[8,2,128,128]{3,2,1,0:T(8,128)(2,1)} %env.1) | copy-start | bytes 1572868
  2.0 6.9 %copy-start.2 = (bf16[8,2,128,128]{3,2,1,0:T(8,128)(2,1)S(1)}, bf16[8,2,128,128]{3,2,1,0:T(8,128)(2,1)}, u32[]{:S(2)}) copy-start(bf16[8,2,128,128]{3,2,1,0:T(8,128)(2,1)} %refs_1_.1) | copy-start | bytes 1572868
  2.0 6.9 %copy-start.4 = (bf16[8,16,16,16]{3,2,1,0:T(8,128)(2,1)S(1)}, bf16[8,16,16,16]{3,2,1,0:T(8,128)(2,1)}, u32[]{:S(2)}) copy-start(bf16[8,16,16,16]{3,2,1,0:T(8,128)(2,1)} %coef.1) | copy-start | bytes 196612
  2.0 6.9 %copy-start.8 = (s32[8]{0:T(128)S(1)}, s32[8]{0:T(128)}, u32[]{:S(2)}) copy-start(s32[8]{0:T(128)} %shift.1) | copy-start | bytes 100
  2.6 18.3 %copy-start.1 = (bf16[2,128,16,128]{3,2,1,0:T(8,128)(2,1)S(1)}, bf16[2,128,16,128]{3,2,1,0:T(8,128)(2,1)}, u32[]{:S(2)}) copy-start(bf16[2,128,16,128]{3,2,1,0:T(8,128)(2,1)} %psi.3) | copy-start | bytes 3145732
  2.6 12.8 %collective-permute-start.2 = (bf16[1,128,16,128]{3,2,1,0:T(8,128)(2,1)S(1)}, bf16[1,128,16,128]{3,2,1,0:T(8,128)(2,1)S(1)}, u32[]{:S(2)}, u32[]{:S(2)}) collective-permute-start(bf16[1,128,16,128]{3,2,1,0:T(8,128)(2,1)S(1)} %cut_psi.1), channel_id=1, source_target_pairs={{1,4},{4,1},{5,8},{8,5},{9,12},{12,9},{3,6},{6,3},{7,10},{10,7},{1... | collective-permute-start | bytes 1572872 | tf_op jit(solution)/shard_map/ppermute | solution.py:378
  5.8 0.7 %copy-start.5 = (s32[16]{0:T(128)S(1)}, s32[16]{0:T(128)}, u32[]{:S(2)}) copy-start(s32[16]{0:T(128)} %dims.13) | copy-start | bytes 196
  9.8 16.1 %collective-permute-start.1 = (bf16[1296,128]{1,0:T(8,128)(2,1)S(1)}, bf16[1296,128]{1,0:T(8,128)(2,1)S(1)}, u32[]{:S(2)}, u32[]{:S(2)}) collective-permute-start(bf16[1296,128]{1,0:T(8,128)(2,1)S(1)} %pack.1.refs_2_), channel_id=1, source_target_pairs={{2,0},{0,2},{3,1},{1,3},{6,4},{4,6},{7,5},{5,7},{10,8},{8,10},{11,... | collective-permute-start | bytes 995336 | tf_op jit(solution)/shard_map/ppermute | solution.py:22
  11.0 11.8 %collective-permute-start.4 = (bf16[8,64,128]{2,1,0:T(8,128)(2,1)S(1)}, bf16[8,64,128]{2,1,0:T(8,128)(2,1)S(1)}, u32[]{:S(2)}, u32[]{:S(2)}) collective-permute-start(bf16[8,64,128]{2,1,0:T(8,128)(2,1)S(1)} %get-tuple-element.24), channel_id=1, source_target_pairs={{0,13},{1,12},{4,9},{5,8},{8,5},{9,4},{12,1},{13,0},{2,15},{3,14},... | collective-permute-start | bytes 393224 | tf_op jit(solution)/shard_map/ppermute | solution.py:392
  11.9 12.1 %collective-permute-start.8 = (bf16[8,64,128]{2,1,0:T(8,128)(2,1)S(1)}, bf16[8,64,128]{2,1,0:T(8,128)(2,1)S(1)}, u32[]{:S(2)}, u32[]{:S(2)}) collective-permute-start(bf16[8,64,128]{2,1,0:T(8,128)(2,1)S(1)} %get-tuple-element.27), channel_id=1, source_target_pairs={{2,0},{0,2},{3,1},{1,3},{6,4},{4,6},{7,5},{5,7},{10,8},{8,10},{11,... | collective-permute-start | bytes 393224 | tf_op jit(solution)/shard_map/ppermute | solution.py:22
  15.4 11.6 %collective-permute-start.3 = (bf16[1,128,16,128]{3,2,1,0:T(8,128)(2,1)S(1)}, bf16[1,128,16,128]{3,2,1,0:T(8,128)(2,1)S(1)}, u32[]{:S(2)}, u32[]{:S(2)}) collective-permute-start(bf16[1,128,16,128]{3,2,1,0:T(8,128)(2,1)S(1)} %collective-permute-done.2.psi), channel_id=1, source_target_pairs={{2,0},{1,3},{6,4},{5,7},{10,8},{9,11},{14,12},{13,15},{18,16},{17,... | collective-permute-start | bytes 1572872 | tf_op jit(solution)/shard_map/ppermute | solution.py:389
  22.7 16.3 %collective-permute-start.7 = (bf16[8,64,128]{2,1,0:T(8,128)(2,1)S(1)}, bf16[8,64,128]{2,1,0:T(8,128)(2,1)S(1)}, u32[]{:S(2)}, u32[]{:S(2)}) collective-permute-start(bf16[8,64,128]{2,1,0:T(8,128)(2,1)S(1)} %get-tuple-element.35), channel_id=1, source_target_pairs={{0,13},{1,12},{4,9},{5,8},{8,5},{9,4},{12,1},{13,0},{2,15},{3,14},... | collective-permute-start | bytes 393224 | tf_op jit(solution)/shard_map/ppermute | solution.py:392
  24.0 11.5 %collective-permute-start.5 = (bf16[8,64,128]{2,1,0:T(8,128)(2,1)S(1)}, bf16[8,64,128]{2,1,0:T(8,128)(2,1)S(1)}, u32[]{:S(2)}, u32[]{:S(2)}) collective-permute-start(bf16[8,64,128]{2,1,0:T(8,128)(2,1)S(1)} %get-tuple-element.33), channel_id=1, source_target_pairs={{15,0},{13,2},{14,1},{12,3},{11,4},{9,6},{10,5},{8,7},{7,8},{5,10}... | collective-permute-start | bytes 393224 | tf_op jit(solution)/shard_map/ppermute | solution.py:399
  24.8 14.2 %collective-permute-start.9 = (bf16[8,64,128]{2,1,0:T(8,128)(2,1)S(1)}, bf16[8,64,128]{2,1,0:T(8,128)(2,1)S(1)}, u32[]{:S(2)}, u32[]{:S(2)}) collective-permute-start(bf16[8,64,128]{2,1,0:T(8,128)(2,1)S(1)} %collective-permute-done.8), channel_id=1, source_target_pairs={{0,13},{1,12},{4,9},{5,8},{8,5},{9,4},{12,1},{13,0},{2,15},{3,14},... | collective-permute-start | bytes 393224 | tf_op jit(solution)/shard_map/ppermute | solution.py:392
  28.1 7.4 %copy-start.6 = (s32[16]{0:T(128)S(1)}, s32[16]{0:T(128)}, u32[]{:S(2)}) copy-start(s32[16]{0:T(128)} %dims.13) | copy-start | bytes 196
  37.4 8.3 %collective-permute-start.6 = (bf16[65,8,128]{2,1,0:T(8,128)(2,1)S(1)}, bf16[65,8,128]{2,1,0:T(8,128)(2,1)S(1)}, u32[]{:S(2)}, u32[]{:S(2)}) collective-permute-start(bf16[65,8,128]{2,1,0:T(8,128)(2,1)S(1)} %give_0.1), channel_id=1, source_target_pairs={{0,2},{2,0},{1,3},{3,1},{4,6},{6,4},{5,7},{7,5},{8,10},{10,8},{9,1... | collective-permute-start | bytes 399368 | tf_op jit(solution)/shard_map/ppermute | solution.py:402
  40.9 4.8 %collective-permute-start.10 = (bf16[64,8,128]{2,1,0:T(8,128)(2,1)S(1)}, bf16[64,8,128]{2,1,0:T(8,128)(2,1)S(1)}, u32[]{:S(2)}, u32[]{:S(2)}) collective-permute-start(bf16[64,8,128]{2,1,0:T(8,128)(2,1)S(1)} %give_1.1), channel_id=1, source_target_pairs={{0,2},{2,0},{1,3},{3,1},{4,6},{6,4},{5,7},{7,5},{8,10},{10,8},{9,1... | collective-permute-start | bytes 393224 | tf_op jit(solution)/shard_map/ppermute | solution.py:402

commit v5 on v3

--- a/solution.py
+++ b/solution.py
@@ -33,7 +33,7 @@
     lanes = lax.broadcasted_iota(jnp.int32, (block, width), 1)
     source = jnp.clip(home * 2 + entry, 0, 2 * places - 1)
     keep = (rows < dims[source]) & (lanes < dims[2 * places - 1 - source])
-    plane[...] = psi[0].astype(F32).reshape(block * states, width)
+    plane[: block * states] = psi[0].astype(F32).reshape(block * states, width)
     for t in range(states):
         piece = plane[pl.ds(t, block, stride=states), :]
         turned[0, :, t * width : (t + 1) * width] = jnp.where(keep, piece, 0.0).astype(BF16)
@@ -59,7 +59,7 @@
                 (1, block, states * width),
                 lambda i, info, dims: (slot_of(which, i, info), 0, 0),
             ),
-            scratch_shapes=[VMEM((block * states, width), F32)],
+            scratch_shapes=[VMEM(((block + 1) * states, width), F32)],
         ),
         input_output_aliases={3: 0} if before else {},
         compiler_params=pltpu.CompilerParams(vmem_limit_bytes=16 << 20),
@@ -215,7 +215,7 @@
         + [pl.BlockSpec(memory_space=VMEM)] * (2 + len(parcels)),
         out_specs=[pl.BlockSpec(memory_space=VMEM)] * 2,
         scratch_shapes=[
-            VMEM((inner * (block + PAD), width), F32),
+            VMEM(((inner + 1) * (block + PAD) + 7, width), F32),
             VMEM((channels * 16, inner), BF16),
         ],
         compiler_params=pltpu.CompilerParams(vmem_limit_bytes=(40 if inner <= 256 else 62) << 20),

time: 47.1 us -> 47.1 us (level)
  no operation moved by 1% of the time
where the time goes in v5:
time: 47.1 us; the launch traced here: 46.9 us
  Pallas kernels  20.8 us (44%)
  starting transfers between devices  16.6 us (35%)
  waiting for transfers between devices  7.23 us (15%)
  local copies, waits for them, and re-layouts  2 us (4%)
    pallas_call x4, Pallas kernels, turn(): pl.pallas_call(functools.partial(turn_kernel, which), out_shape=jax.Shape...  5.87 us
    ppermute x1, starting transfers between devices, cross(): return lax.ppermute(block, whole, route)  5.5 us
    pallas_call x1, Pallas kernels, mix(): pl.pallas_call(mix_kernel, out_shape=[jax.ShapeDtypeStruct((block * 8, ch...  5.19 us
    ppermute x2, starting transfers between devices, swap(): return lax.ppermute(block, spots, route)  3.9 us
    ppermute x2, waiting for transfers between devices, swap(): return lax.ppermute(block, spots, route)  3.5 us
    ppermute x2, waiting for transfers between devices, beside(): return lax.ppermute(block, 'mpo', [(g, g ^ 1) for g in range(groups)])  3.46 us
    ppermute x2, starting transfers between devices, slanted(): return lax.ppermute(block, whole, route)  2.71 us
    pallas_call x2, Pallas kernels, give(): pl.pallas_call(functools.partial(give_kernel, piece), out_shape=jax.Shape...  2.61 us
  transfers between devices with their start and end apart: 10, of which 3 were waited for; matrix products, arithmetic and copies ran while one was open for 0% of the time, Pallas kernels for 41%

profile of v5, /device:TPU:9, one launch (start us, length us, event | category | flops | bytes accessed | tf_op | source)
XLA Modules:
  0.0 46.9 jit_solution(107681246580435525)
XLA Ops:
  0.0 0.7 %collective-permute-start = (bf16[2,128,16,128]{3,2,1,0:T(8,128)(2,1)}, bf16[2,128,16,128]{3,2,1,0:T(8,128)(2,1)S(1)}, u32[]{:S(2)}, u32[]{:S(2)}) collective-permute-start(bf16[2,128,16,128]{3,2,1,0:T(8,128)(2,1)} %psi.3), channel_id=1, source_target_pairs={{0,1},{1,0},{4,5},{5,4},{8,9},{9,8},{12,13},{13,12},{2,3},{3,2},{6... | collective-permute-start | bytes 3145736 | tf_op jit(solution)/shard_map/ppermute | solution.py:396
  0.7 0.0 copy-start.7
  0.7 0.1 stack.23.info
  0.8 0.0 copy-start
  0.8 1.2 %copy-done = bf16[2,128,16,128]{3,2,1,0:T(8,128)(2,1)S(1)} copy-done((bf16[2,128,16,128]{3,2,1,0:T(8,128)(2,1)S(1)}, bf16[2,128,16,128]{3,2,1,0:T(8,128)(2,1)}, u32[]{:S(2)}) %copy-start) | copy-done | bytes 1048600
  2.0 0.0 copy-start.3
  2.0 0.0 copy-start.2
  2.0 0.0 copy-start.4
  2.0 0.0 copy-start.8
  2.0 0.6 %cut_psi.1 = bf16[1,128,16,128]{3,2,1,0:T(8,128)(2,1)S(1)} custom-call(s32[6]{0:T(128)S(1)} %stack.23.info, bf16[2,128,16,128]{3,2,1,0:T(8,128)(2,1)S(1)} %copy-done), custom_call_target="tpu_custom_call" | custom-call | flops 1024 | bytes 1024 | tf_op jit(solution)/shard_map/cut_psi/pallas_call | solution.py:110
  2.6 0.0 copy-start.1
  2.6 3.2 %collective-permute-start.2 = (bf16[1,128,16,128]{3,2,1,0:T(8,128)(2,1)S(1)}, bf16[1,128,16,128]{3,2,1,0:T(8,128)(2,1)S(1)}, u32[]{:S(2)}, u32[]{:S(2)}) collective-permute-start(bf16[1,128,16,128]{3,2,1,0:T(8,128)(2,1)S(1)} %cut_psi.1), channel_id=1, source_target_pairs={{1,4},{4,1},{5,8},{8,5},{9,12},{12,9},{3,6},{6,3},{7,10},{10,7},{1... | collective-permute-start | bytes 1572872 | tf_op jit(solution)/shard_map/ppermute | solution.py:396
  5.8 0.0 collective-permute-done.psi
  5.8 0.0 copy-start.5
  5.9 0.6 %copy-done.5 = s32[16]{0:T(128)S(1)} copy-done((s32[16]{0:T(128)S(1)}, s32[16]{0:T(128)}, u32[]{:S(2)}) %copy-start.5) | copy-done | bytes 88
  6.5 1.8 %turn_1.1.refs_0_ = bf16[6,128,2048]{2,1,0:T(8,128)(2,1)S(1)} custom-call(s32[6]{0:T(128)S(1)} %stack.23.info, s32[16]{0:T(128)S(1)} %copy-done.5, bf16[2,128,16,128]{3,2,1,0:T(8,128)(2,1)S(1)} %collective-permute-done.psi), custom_call_target="tpu_custom_call" | custom-call | flops 1024 | bytes 1024 | tf_op jit(solution)/shard_map/turn_1/pallas_call | solution.py:50
  8.3 0.0 copy-done.3
  8.3 0.6 %cut_env.1 = (bf16[8,64,128]{2,1,0:T(8,128)(2,1)S(1)}, bf16[8,64,128]{2,1,0:T(8,128)(2,1)S(1)}, bf16[8,64,128]{2,1,0:T(8,128)(2,1)S(1)}, bf16[8,64,128]{2,1,0:T(8,128)(2,1)S(1)}) custom-call(s32[6]{0:T(128)S(1)} %stack.23.info, bf16[8,2,128,128]{3,2,1,0:T(8,128)(2,1)S(1)} %copy-done.3), custom_call_target="tpu_custom_call" | custom-call | flops 1024 | bytes 1024 | tf_op jit(solution)/shard_map/cut_env/pallas_call | solution.py:129
  8.9 0.0 copy-done.7
  8.9 0.0 copy-done.2
  8.9 0.0 copy-done.4
  8.9 0.0 copy-done.8
  8.9 0.8 %pack.1.refs_2_ = bf16[1296,128]{1,0:T(8,128)(2,1)S(1)} custom-call(s32[6]{0:T(128)S(1)} %stack.23.info, s32[8,16]{1,0:T(8,128)S(1)} %copy-done.7, s32[8]{0:T(128)S(1)} %copy-done.8, bf16[8,16,16,16]{3,2,1,0:T(8,128)(2,1)S(1)} %copy-done.4, bf16[8,2,128,128]{3,2,1,0:T(8,128)(2,1)S(1)} %copy-done.2), custom_call_target="tpu_custom_call" | custom-call | flops 1024 | bytes 1024 | tf_op jit(solution)/shard_map/pack/pallas_call | solution.py:94
  9.8 1.3 %collective-permute-start.1 = (bf16[1296,128]{1,0:T(8,128)(2,1)S(1)}, bf16[1296,128]{1,0:T(8,128)(2,1)S(1)}, u32[]{:S(2)}, u32[]{:S(2)}) collective-permute-start(bf16[1296,128]{1,0:T(8,128)(2,1)S(1)} %pack.1.refs_2_), channel_id=1, source_target_pairs={{2,0},{0,2},{3,1},{1,3},{6,4},{4,6},{7,5},{5,7},{10,8},{8,10},{11,... | collective-permute-start | bytes 995336 | tf_op jit(solution)/shard_map/ppermute | solution.py:22
  11.0 0.8 %collective-permute-start.4 = (bf16[8,64,128]{2,1,0:T(8,128)(2,1)S(1)}, bf16[8,64,128]{2,1,0:T(8,128)(2,1)S(1)}, u32[]{:S(2)}, u32[]{:S(2)}) collective-permute-start(bf16[8,64,128]{2,1,0:T(8,128)(2,1)S(1)} %get-tuple-element.27), channel_id=1, source_target_pairs={{0,13},{1,12},{4,9},{5,8},{8,5},{9,4},{12,1},{13,0},{2,15},{3,14},... | collective-permute-start | bytes 393224 | tf_op jit(solution)/shard_map/ppermute | solution.py:410
  11.9 3.5 %collective-permute-done.2.psi = bf16[1,128,16,128]{3,2,1,0:T(8,128)(2,1)S(1)} collective-permute-done((bf16[1,128,16,128]{3,2,1,0:T(8,128)(2,1)S(1)}, bf16[1,128,16,128]{3,2,1,0:T(8,128)(2,1)S(1)}, u32[]{:S(2)}, u32[]{:S(2)}) %collective-permute-start.2) | collective-permute-done | bytes 524320 | tf_op jit(solution)/shard_map/ppermute | solution.py:396
  15.4 5.5 %collective-permute-start.3 = (bf16[1,128,16,128]{3,2,1,0:T(8,128)(2,1)S(1)}, bf16[1,128,16,128]{3,2,1,0:T(8,128)(2,1)S(1)}, u32[]{:S(2)}, u32[]{:S(2)}) collective-permute-start(bf16[1,128,16,128]{3,2,1,0:T(8,128)(2,1)S(1)} %collective-permute-done.2.psi), channel_id=1, source_target_pairs={{2,0},{1,3},{6,4},{5,7},{10,8},{9,11},{14,12},{13,15},{18,16},{17,... | collective-permute-start | bytes 1572872 | tf_op jit(solution)/shard_map/ppermute | solution.py:407
  20.9 0.0 copy-done.1
  20.9 1.8 %turn_0.1.refs_0_ = bf16[6,128,2048]{2,1,0:T(8,128)(2,1)S(1)} custom-call(s32[6]{0:T(128)S(1)} %stack.23.info, s32[16]{0:T(128)S(1)} %copy-done.5, bf16[2,128,16,128]{3,2,1,0:T(8,128)(2,1)S(1)} %copy-done.1, bf16[6,128,2048]{2,1,0:T(8,128)(2,1)S(1)} %turn_1.1.refs_0_), custom_call_target="tpu_custom_call", output_to_operand_aliasing={{}: (3, {})} | custom-call | flops 1024 | bytes 1024 | tf_op jit(solution)/shard_map/turn_0/pallas_call | solution.py:50
  22.7 0.1 collective-permute-start.5
  22.8 0.0 collective-permute-done.4.low
  22.8 1.1 %turn_2.1.refs_0_ = bf16[6,128,2048]{2,1,0:T(8,128)(2,1)S(1)} custom-call(s32[6]{0:T(128)S(1)} %stack.23.info, s32[16]{0:T(128)S(1)} %copy-done.5, bf16[1,128,16,128]{3,2,1,0:T(8,128)(2,1)S(1)} %collective-permute-done.2.psi, bf16[6,128,2048]{2,1,0:T(8,128)(2,1)S(1)} %turn_0.1.refs_0_), custom_call_target="tpu_custom_call", output_to_operand_aliasing={{}: (3, {})} | custom-call | flops 1073741824 | bytes 1048576 | tf_op jit(solution)/shard_map/turn_2/pallas_call | solution.py:50
  23.9 0.9 %collective-permute-start.6 = (bf16[8,64,128]{2,1,0:T(8,128)(2,1)S(1)}, bf16[8,64,128]{2,1,0:T(8,128)(2,1)S(1)}, u32[]{:S(2)}, u32[]{:S(2)}) collective-permute-start(bf16[8,64,128]{2,1,0:T(8,128)(2,1)S(1)} %get-tuple-element.40), channel_id=1, source_target_pairs={{15,0},{13,2},{14,1},{12,3},{11,4},{9,6},{10,5},{8,7},{7,8},{5,10}... | collective-permute-start | bytes 393224 | tf_op jit(solution)/shard_map/ppermute | solution.py:417
  24.8 1.9 %collective-permute-start.8 = (bf16[8,64,128]{2,1,0:T(8,128)(2,1)S(1)}, bf16[8,64,128]{2,1,0:T(8,128)(2,1)S(1)}, u32[]{:S(2)}, u32[]{:S(2)}) collective-permute-start(bf16[8,64,128]{2,1,0:T(8,128)(2,1)S(1)} %get-tuple-element.42), channel_id=1, source_target_pairs={{15,0},{13,2},{14,1},{12,3},{11,4},{9,6},{10,5},{8,7},{7,8},{5,10}... | collective-permute-start | bytes 393224 | tf_op jit(solution)/shard_map/ppermute | solution.py:417
  26.7 0.0 collective-permute-done.1.refs_3_
  26.7 0.1 maximum_convert_fusion.shift
  26.7 0.2 collective-permute-done.3.psi
  27.0 1.1 %turn_3.1.refs_0_ = bf16[6,128,2048]{2,1,0:T(8,128)(2,1)S(1)} custom-call(s32[6]{0:T(128)S(1)} %stack.23.info, s32[16]{0:T(128)S(1)} %copy-done.5, bf16[1,128,16,128]{3,2,1,0:T(8,128)(2,1)S(1)} %collective-permute-done.3.psi, bf16[6,128,2048]{2,1,0:T(8,128)(2,1)S(1)} %turn_2.1.refs_0_), custom_call_target="tpu_custom_call", output_to_operand_aliasing={{}: (3, {})} | custom-call | flops 1024 | bytes 1024 | tf_op jit(solution)/shard_map/turn_3/pallas_call | solution.py:50
  28.1 5.2 %mix.1 = (bf16[1024,2048]{1,0:T(8,128)(2,1)S(1)}, bf16[1024,2048]{1,0:T(8,128)(2,1)S(1)}) custom-call(s32[6]{0:T(128)S(1)} %stack.23.info, s32[16]{0:T(128)S(1)} %maximum_convert_fusion.shift, bf16[6,128,2048]{2,1,0:T(8,128)(2,1)S(1)} %turn_3.1.refs_0_, bf16[8,2,128,128]{3,2,1,0:T(8,128)(2,1)S(1)} %copy-done.2, bf16[1296,128]{1,0:T(8,128)(2,1)S(1)} %pack.1.refs_2_, ...), custom_call_target="tpu_custom_call" | custom-call | flops 1024 | bytes 1024 | tf_op jit(solution)/shard_map/mix/pallas_call | solution.py:211
  33.3 0.0 collective-permute-done.5.high
  33.3 0.0 copy-start.6
  33.3 1.8 %begin.1 = (f32[1024,128]{1,0:T(8,128)S(1)}, f32[1024,128]{1,0:T(8,128)S(1)}) custom-call(s32[6]{0:T(128)S(1)} %stack.23.info, bf16[1024,2048]{1,0:T(8,128)(2,1)S(1)} %get-tuple-element.35.given.mixed, bf16[1024,2048]{1,0:T(8,128)(2,1)S(1)} %get-tuple-element.36.kept.mixed, bf16[8,64,128]{2,1,0:T(8,128)(2,1)S(1)} %collective-permute-done.4.low, ...), custom_call_target="tpu_custom_call" | custom-call | flops 268435456 | bytes 1048576 | tf_op jit(solution)/shard_map/begin/pallas_call | solution.py:261
  35.1 0.0 collective-permute-done.6.refs_0_
  35.2 0.0 copy-done.6
  35.2 1.3 %give_0.1 = bf16[65,8,128]{2,1,0:T(8,128)(2,1)S(1)} custom-call(s32[6]{0:T(128)S(1)} %stack.23.info, s32[16]{0:T(128)S(1)} %copy-done.6, bf16[1024,2048]{1,0:T(8,128)(2,1)S(1)} %get-tuple-element.35.given.mixed, f32[1024,128]{1,0:T(8,128)S(1)} %get-tuple-element.38.before, bf16[8,64,128]{2,1,0:T(8,128)(2,1)S(1)} %collective-permute-done.6.refs_0_), custom_call_target="tpu_custom_call" | custom-call | flops 268435456 | bytes 1048576 | tf_op jit(solution)/shard_map/give_0/pallas_call | solution.py:291
  36.5 2.2 %collective-permute-start.7 = (bf16[65,8,128]{2,1,0:T(8,128)(2,1)S(1)}, bf16[65,8,128]{2,1,0:T(8,128)(2,1)S(1)}, u32[]{:S(2)}, u32[]{:S(2)}) collective-permute-start(bf16[65,8,128]{2,1,0:T(8,128)(2,1)S(1)} %give_0.1), channel_id=1, source_target_pairs={{0,2},{2,0},{1,3},{3,1},{4,6},{6,4},{5,7},{7,5},{8,10},{10,8},{9,1... | collective-permute-start | bytes 399368 | tf_op jit(solution)/shard_map/ppermute | solution.py:420
  38.7 0.0 collective-permute-done.8.refs_0_.refs_1_
  38.7 1.3 %give_1.1 = bf16[64,8,128]{2,1,0:T(8,128)(2,1)S(1)} custom-call(s32[6]{0:T(128)S(1)} %stack.23.info, s32[16]{0:T(128)S(1)} %copy-done.6, bf16[1024,2048]{1,0:T(8,128)(2,1)S(1)} %get-tuple-element.35.given.mixed, f32[1024,128]{1,0:T(8,128)S(1)} %get-tuple-element.38.before, bf16[8,64,128]{2,1,0:T(8,128)(2,1)S(1)} %collective-permute-done.8.refs_0_.refs_1_), custom_call_target="tpu_custom_call" | custom-call | flops 268435456 | bytes 1048576 | tf_op jit(solution)/shard_map/give_1/pallas_call | solution.py:291
  40.0 0.1 collective-permute-start.9
  40.1 2.0 %keep.1.result = bf16[2,128,8,128]{3,2,1,0:T(8,128)(2,1)} custom-call(s32[6]{0:T(128)S(1)} %stack.23.info, s32[16]{0:T(128)S(1)} %copy-done.6, bf16[1024,2048]{1,0:T(8,128)(2,1)S(1)} %get-tuple-element.36.kept.mixed, f32[1024,128]{1,0:T(8,128)S(1)} %get-tuple-element.44.before, bf16[8,64,128]{2,1,0:T(8,128)(2,1)S(1)} %collective-permute-done.6.refs_0_, ...), custom_call_target="tpu_custom_call" | custom-call | flops 1024 | bytes 1024 | tf_op jit(solution)/shard_map/keep/pallas_call | solution.py:318
  42.1 3.5 %collective-permute-done.9.one = bf16[64,8,128]{2,1,0:T(8,128)(2,1)S(1)} collective-permute-done((bf16[64,8,128]{2,1,0:T(8,128)(2,1)S(1)}, bf16[64,8,128]{2,1,0:T(8,128)(2,1)S(1)}, u32[]{:S(2)}, u32[]{:S(2)}) %collective-permute-start.9) | collective-permute-done | bytes 131104 | tf_op jit(solution)/shard_map/ppermute | solution.py:420
  45.5 0.0 collective-permute-done.7.zero
  45.5 1.4 %finish.1 = bf16[2,128,8,128]{3,2,1,0:T(8,128)(2,1)} custom-call(s32[6]{0:T(128)S(1)} %stack.23.info, bf16[65,8,128]{2,1,0:T(8,128)(2,1)S(1)} %collective-permute-done.7.zero, bf16[64,8,128]{2,1,0:T(8,128)(2,1)S(1)} %collective-permute-done.9.one, bf16[2,128,8,128]{3,2,1,0:T(8,128)(2,1)} %keep.1.result), custom_call_target="tpu_custom_call", output_to_operand_aliasing={{}: (3, {})} | custom-call | flops 1024 | bytes 1024 | tf_op jit(solution)/shard_map/finish/pallas_call | solution.py:353
  (2 shorter events, 0.0 us)
Async XLA Ops:
  0.0 5.8 %collective-permute-start = (bf16[2,128,16,128]{3,2,1,0:T(8,128)(2,1)}, bf16[2,128,16,128]{3,2,1,0:T(8,128)(2,1)S(1)}, u32[]{:S(2)}, u32[]{:S(2)}) collective-permute-start(bf16[2,128,16,128]{3,2,1,0:T(8,128)(2,1)} %psi.3), channel_id=1, source_target_pairs={{0,1},{1,0},{4,5},{5,4},{8,9},{9,8},{12,13},{13,12},{2,3},{3,2},{6... | collective-permute-start | bytes 3145736 | tf_op jit(solution)/shard_map/ppermute | solution.py:396
  0.7 8.2 %copy-start.7 = (s32[8,16]{1,0:T(8,128)S(1)}, s32[8,16]{1,0:T(8,128)}, u32[]{:S(2)}) copy-start(s32[8,16]{1,0:T(8,128)} %mask.1) | copy-start | bytes 1540
  0.8 1.2 %copy-start = (bf16[2,128,16,128]{3,2,1,0:T(8,128)(2,1)S(1)}, bf16[2,128,16,128]{3,2,1,0:T(8,128)(2,1)}, u32[]{:S(2)}) copy-start(bf16[2,128,16,128]{3,2,1,0:T(8,128)(2,1)} %psi.3) | copy-start | bytes 3145732
  2.0 6.3 %copy-start.3 = (bf16[8,2,128,128]{3,2,1,0:T(8,128)(2,1)S(1)}, bf16[8,2,128,128]{3,2,1,0:T(8,128)(2,1)}, u32[]{:S(2)}) copy-start(bf16[8,2,128,128]{3,2,1,0:T(8,128)(2,1)} %env.1) | copy-start | bytes 1572868
  2.0 6.9 %copy-start.2 = (bf16[8,2,128,128]{3,2,1,0:T(8,128)(2,1)S(1)}, bf16[8,2,128,128]{3,2,1,0:T(8,128)(2,1)}, u32[]{:S(2)}) copy-start(bf16[8,2,128,128]{3,2,1,0:T(8,128)(2,1)} %refs_1_.1) | copy-start | bytes 1572868
  2.0 6.9 %copy-start.4 = (bf16[8,16,16,16]{3,2,1,0:T(8,128)(2,1)S(1)}, bf16[8,16,16,16]{3,2,1,0:T(8,128)(2,1)}, u32[]{:S(2)}) copy-start(bf16[8,16,16,16]{3,2,1,0:T(8,128)(2,1)} %coef.1) | copy-start | bytes 196612
  2.0 6.9 %copy-start.8 = (s32[8]{0:T(128)S(1)}, s32[8]{0:T(128)}, u32[]{:S(2)}) copy-start(s32[8]{0:T(128)} %shift.1) | copy-start | bytes 100
  2.6 18.3 %copy-start.1 = (bf16[2,128,16,128]{3,2,1,0:T(8,128)(2,1)S(1)}, bf16[2,128,16,128]{3,2,1,0:T(8,128)(2,1)}, u32[]{:S(2)}) copy-start(bf16[2,128,16,128]{3,2,1,0:T(8,128)(2,1)} %psi.3) | copy-start | bytes 3145732
  2.6 12.8 %collective-permute-start.2 = (bf16[1,128,16,128]{3,2,1,0:T(8,128)(2,1)S(1)}, bf16[1,128,16,128]{3,2,1,0:T(8,128)(2,1)S(1)}, u32[]{:S(2)}, u32[]{:S(2)}) collective-permute-start(bf16[1,128,16,128]{3,2,1,0:T(8,128)(2,1)S(1)} %cut_psi.1), channel_id=1, source_target_pairs={{1,4},{4,1},{5,8},{8,5},{9,12},{12,9},{3,6},{6,3},{7,10},{10,7},{1... | collective-permute-start | bytes 1572872 | tf_op jit(solution)/shard_map/ppermute | solution.py:396
  5.8 0.7 %copy-start.5 = (s32[16]{0:T(128)S(1)}, s32[16]{0:T(128)}, u32[]{:S(2)}) copy-start(s32[16]{0:T(128)} %dims.13) | copy-start | bytes 196
  9.8 16.9 %collective-permute-start.1 = (bf16[1296,128]{1,0:T(8,128)(2,1)S(1)}, bf16[1296,128]{1,0:T(8,128)(2,1)S(1)}, u32[]{:S(2)}, u32[]{:S(2)}) collective-permute-start(bf16[1296,128]{1,0:T(8,128)(2,1)S(1)} %pack.1.refs_2_), channel_id=1, source_target_pairs={{2,0},{0,2},{3,1},{1,3},{6,4},{4,6},{7,5},{5,7},{10,8},{8,10},{11,... | collective-permute-start | bytes 995336 | tf_op jit(solution)/shard_map/ppermute | solution.py:22
  11.0 11.8 %collective-permute-start.4 = (bf16[8,64,128]{2,1,0:T(8,128)(2,1)S(1)}, bf16[8,64,128]{2,1,0:T(8,128)(2,1)S(1)}, u32[]{:S(2)}, u32[]{:S(2)}) collective-permute-start(bf16[8,64,128]{2,1,0:T(8,128)(2,1)S(1)} %get-tuple-element.27), channel_id=1, source_target_pairs={{0,13},{1,12},{4,9},{5,8},{8,5},{9,4},{12,1},{13,0},{2,15},{3,14},... | collective-permute-start | bytes 393224 | tf_op jit(solution)/shard_map/ppermute | solution.py:410
  15.4 11.6 %collective-permute-start.3 = (bf16[1,128,16,128]{3,2,1,0:T(8,128)(2,1)S(1)}, bf16[1,128,16,128]{3,2,1,0:T(8,128)(2,1)S(1)}, u32[]{:S(2)}, u32[]{:S(2)}) collective-permute-start(bf16[1,128,16,128]{3,2,1,0:T(8,128)(2,1)S(1)} %collective-permute-done.2.psi), channel_id=1, source_target_pairs={{2,0},{1,3},{6,4},{5,7},{10,8},{9,11},{14,12},{13,15},{18,16},{17,... | collective-permute-start | bytes 1572872 | tf_op jit(solution)/shard_map/ppermute | solution.py:407
  22.7 10.6 %collective-permute-start.5 = (bf16[8,64,128]{2,1,0:T(8,128)(2,1)S(1)}, bf16[8,64,128]{2,1,0:T(8,128)(2,1)S(1)}, u32[]{:S(2)}, u32[]{:S(2)}) collective-permute-start(bf16[8,64,128]{2,1,0:T(8,128)(2,1)S(1)} %get-tuple-element.37), channel_id=1, source_target_pairs={{0,13},{1,12},{4,9},{5,8},{8,5},{9,4},{12,1},{13,0},{2,15},{3,14},... | collective-permute-start | bytes 393224 | tf_op jit(solution)/shard_map/ppermute | solution.py:410
  23.9 11.2 %collective-permute-start.6 = (bf16[8,64,128]{2,1,0:T(8,128)(2,1)S(1)}, bf16[8,64,128]{2,1,0:T(8,128)(2,1)S(1)}, u32[]{:S(2)}, u32[]{:S(2)}) collective-permute-start(bf16[8,64,128]{2,1,0:T(8,128)(2,1)S(1)} %get-tuple-element.40), channel_id=1, source_target_pairs={{15,0},{13,2},{14,1},{12,3},{11,4},{9,6},{10,5},{8,7},{7,8},{5,10}... | collective-permute-start | bytes 393224 | tf_op jit(solution)/shard_map/ppermute | solution.py:417
  24.8 13.9 %collective-permute-start.8 = (bf16[8,64,128]{2,1,0:T(8,128)(2,1)S(1)}, bf16[8,64,128]{2,1,0:T(8,128)(2,1)S(1)}, u32[]{:S(2)}, u32[]{:S(2)}) collective-permute-start(bf16[8,64,128]{2,1,0:T(8,128)(2,1)S(1)} %get-tuple-element.42), channel_id=1, source_target_pairs={{15,0},{13,2},{14,1},{12,3},{11,4},{9,6},{10,5},{8,7},{7,8},{5,10}... | collective-permute-start | bytes 393224 | tf_op jit(solution)/shard_map/ppermute | solution.py:417
  33.3 1.8 %copy-start.6 = (s32[16]{0:T(128)S(1)}, s32[16]{0:T(128)}, u32[]{:S(2)}) copy-start(s32[16]{0:T(128)} %dims.13) | copy-start | bytes 196
  36.5 9.1 %collective-permute-start.7 = (bf16[65,8,128]{2,1,0:T(8,128)(2,1)S(1)}, bf16[65,8,128]{2,1,0:T(8,128)(2,1)S(1)}, u32[]{:S(2)}, u32[]{:S(2)}) collective-permute-start(bf16[65,8,128]{2,1,0:T(8,128)(2,1)S(1)} %give_0.1), channel_id=1, source_target_pairs={{0,2},{2,0},{1,3},{3,1},{4,6},{6,4},{5,7},{7,5},{8,10},{10,8},{9,1... | collective-permute-start | bytes 399368 | tf_op jit(solution)/shard_map/ppermute | solution.py:420
  40.0 5.5 %collective-permute-start.9 = (bf16[64,8,128]{2,1,0:T(8,128)(2,1)S(1)}, bf16[64,8,128]{2,1,0:T(8,128)(2,1)S(1)}, u32[]{:S(2)}, u32[]{:S(2)}) collective-permute-start(bf16[64,8,128]{2,1,0:T(8,128)(2,1)S(1)} %give_1.1), channel_id=1, source_target_pairs={{0,2},{2,0},{1,3},{3,1},{4,6},{6,4},{5,7},{7,5},{8,10},{10,8},{9,1... | collective-permute-start | bytes 393224 | tf_op jit(solution)/shard_map/ppermute | solution.py:420

commit v6 on v4

--- a/solution.py
+++ b/solution.py
@@ -33,7 +33,7 @@
     lanes = lax.broadcasted_iota(jnp.int32, (block, width), 1)
     source = jnp.clip(home * 2 + entry, 0, 2 * places - 1)
     keep = (rows < dims[source]) & (lanes < dims[2 * places - 1 - source])
-    plane[...] = psi[0].astype(F32).reshape(block * states, width)
+    plane[: block * states] = psi[0].astype(F32).reshape(block * states, width)
     for t in range(states):
         piece = plane[pl.ds(t, block, stride=states), :]
         turned[0, :, t * width : (t + 1) * width] = jnp.where(keep, piece, 0.0).astype(BF16)
@@ -59,7 +59,7 @@
                 (1, block, states * width),
                 lambda i, info, dims: (slot_of(which, i, info), 0, 0),
             ),
-            scratch_shapes=[VMEM((block * states, width), F32)],
+            scratch_shapes=[VMEM(((block + 1) * states, width), F32)],
         ),
         input_output_aliases={3: 0} if before else {},
         compiler_params=pltpu.CompilerParams(vmem_limit_bytes=16 << 20),
@@ -215,7 +215,7 @@
         + [pl.BlockSpec(memory_space=VMEM)] * (2 + len(parcels)),
         out_specs=[pl.BlockSpec(memory_space=VMEM)] * 2,
         scratch_shapes=[
-            VMEM((inner * (block + PAD), width), F32),
+            VMEM(((inner + 1) * (block + PAD) + 7, width), F32),
             VMEM((channels * 16, inner), BF16),
         ],
         compiler_params=pltpu.CompilerParams(vmem_limit_bytes=(40 if inner <= 256 else 62) << 20),
@@ -413,13 +413,12 @@
     low, high = cuts[:groups], cuts[groups:]
     sent = pack(after(info, *cuts), mpo_mask, shift, mpo_coef, left_env, groups - 1)
     parcels = [sent[0]] + [ring(p, "mpo", j) for j, p in zip(steps, sent)]
-    passed = [ring(c, "mpo", j) for c, j in zip(high[1:], steps)]
     same = [mirrored(low[0]), mirrored(after(high[0], *sent))]
     crossed = cross(after(early, *sent))
     turned = turn(0, after(info, *sent), dims, psi, turned)
     turned = turn(2, after(info, same[0]), dims, early, turned)
     low = [slanted(after(c, turned), j) for c, j in zip(low[1:], steps)]
-    high = [mirrored(after(p, turned)) for p in passed]
+    high = [slanted(after(c, turned), j) for c, j in zip(high[1:], steps)]
     turned = turn(3, info, dims, crossed, turned)
     last = w_dev * block + channels * states
     shifts = jnp.concatenate([p[last, :w_dev] for p in parcels]).astype(jnp.int32)

time: 47.2 us -> 46.9 us (level)
  waiting for transfers between devices: 8.66 us -> 7.49 us
  starting transfers between devices: 15.5 us -> 16 us
    ppermute x1 -> x2, starting transfers between devices: 0.86 us -> 2.71 us  [slanted(): return lax.ppermute(block, whole, route)]
    ppermute x3 -> x2, starting transfers between devices: 1.92 us -> 0.91 us  [mirrored(): lax.ppermute(block, spots, [(i, places - 1 - i) for i in range(places)])]
    ppermute x1, waiting for transfers between devices: 1.05 us -> 0.22 us  [cross(): return lax.ppermute(block, whole, route)]
    ppermute x1 -> x2, waiting for transfers between devices: 2.18 us -> 1.85 us  [slanted(): return lax.ppermute(block, whole, route)]
    ppermute x2 -> x1, starting transfers between devices: 1.53 us -> 1.28 us  [ring(): lax.ppermute(block, axis, [((i + step) % count, i) for i in range(count)])]
  transfers between devices with their start and end apart: 11 -> 10, of which waited for: 4 -> 4; matrix products, arithmetic and copies ran while one was open for 0% -> 0% of each run, Pallas kernels for 41% -> 41%
where the time goes in v6:
time: 46.9 us; the launch traced here: 46.4 us
  Pallas kernels  20.6 us (44%)
  starting transfers between devices  16 us (34%)
  waiting for transfers between devices  7.49 us (16%)
  local copies, waits for them, and re-layouts  2 us (4%)
    pallas_call x4, Pallas kernels, turn(): pl.pallas_call(functools.partial(turn_kernel, which), out_shape=jax.Shape...  5.87 us
    ppermute x1, starting transfers between devices, cross(): return lax.ppermute(block, whole, route)  5.5 us
    pallas_call x1, Pallas kernels, mix(): pl.pallas_call(mix_kernel, out_shape=[jax.ShapeDtypeStruct((block * 8, ch...  5.19 us
    ppermute x2, starting transfers between devices, swap(): return lax.ppermute(block, spots, route)  3.9 us
    pallas_call x2, Pallas kernels, give(): pl.pallas_call(functools.partial(give_kernel, piece), out_shape=jax.Shape...  3.68 us
    ppermute x2, waiting for transfers between devices, swap(): return lax.ppermute(block, spots, route)  3.5 us
    ppermute x2, starting transfers between devices, slanted(): return lax.ppermute(block, whole, route)  2.71 us
    pallas_call x1, Pallas kernels, keep(): pl.pallas_call(keep_kernel, out_shape=jax.ShapeDtypeStruct((2, rows // 8,...  2.5 us
  transfers between devices with their start and end apart: 10, of which 4 were waited for; matrix products, arithmetic and copies ran while one was open for 0% of the time, Pallas kernels for 41%

profile of v6, /device:TPU:9, one launch (start us, length us, event | category | flops | bytes accessed | tf_op | source)
XLA Modules:
  0.0 46.4 jit_solution(2447915080322384759)
XLA Ops:
  0.0 0.7 %collective-permute-start = (bf16[2,128,16,128]{3,2,1,0:T(8,128)(2,1)}, bf16[2,128,16,128]{3,2,1,0:T(8,128)(2,1)S(1)}, u32[]{:S(2)}, u32[]{:S(2)}) collective-permute-start(bf16[2,128,16,128]{3,2,1,0:T(8,128)(2,1)} %psi.3), channel_id=1, source_target_pairs={{0,1},{1,0},{4,5},{5,4},{8,9},{9,8},{12,13},{13,12},{2,3},{3,2},{6... | collective-permute-start | bytes 3145736 | tf_op jit(solution)/shard_map/ppermute | solution.py:378
  0.7 0.0 copy-start.7
  0.7 0.1 stack.23.info
  0.8 0.0 copy-start
  0.8 1.2 %copy-done = bf16[2,128,16,128]{3,2,1,0:T(8,128)(2,1)S(1)} copy-done((bf16[2,128,16,128]{3,2,1,0:T(8,128)(2,1)S(1)}, bf16[2,128,16,128]{3,2,1,0:T(8,128)(2,1)}, u32[]{:S(2)}) %copy-start) | copy-done | bytes 1048600
  2.0 0.0 copy-start.3
  2.0 0.0 copy-start.2
  2.0 0.0 copy-start.4
  2.0 0.0 copy-start.8
  2.0 0.6 %cut_psi.1 = bf16[1,128,16,128]{3,2,1,0:T(8,128)(2,1)S(1)} custom-call(s32[6]{0:T(128)S(1)} %stack.23.info, bf16[2,128,16,128]{3,2,1,0:T(8,128)(2,1)S(1)} %copy-done), custom_call_target="tpu_custom_call" | custom-call | flops 1024 | bytes 1024 | tf_op jit(solution)/shard_map/cut_psi/pallas_call | solution.py:110
  2.6 0.0 copy-start.1
  2.6 3.2 %collective-permute-start.2 = (bf16[1,128,16,128]{3,2,1,0:T(8,128)(2,1)S(1)}, bf16[1,128,16,128]{3,2,1,0:T(8,128)(2,1)S(1)}, u32[]{:S(2)}, u32[]{:S(2)}) collective-permute-start(bf16[1,128,16,128]{3,2,1,0:T(8,128)(2,1)S(1)} %cut_psi.1), channel_id=1, source_target_pairs={{1,4},{4,1},{5,8},{8,5},{9,12},{12,9},{3,6},{6,3},{7,10},{10,7},{1... | collective-permute-start | bytes 1572872 | tf_op jit(solution)/shard_map/ppermute | solution.py:378
  5.8 0.0 collective-permute-done.psi
  5.8 0.0 copy-start.5
  5.9 0.6 %copy-done.5 = s32[16]{0:T(128)S(1)} copy-done((s32[16]{0:T(128)S(1)}, s32[16]{0:T(128)}, u32[]{:S(2)}) %copy-start.5) | copy-done | bytes 88
  6.5 1.8 %turn_1.1.refs_0_ = bf16[6,128,2048]{2,1,0:T(8,128)(2,1)S(1)} custom-call(s32[6]{0:T(128)S(1)} %stack.23.info, s32[16]{0:T(128)S(1)} %copy-done.5, bf16[2,128,16,128]{3,2,1,0:T(8,128)(2,1)S(1)} %collective-permute-done.psi), custom_call_target="tpu_custom_call" | custom-call | flops 1024 | bytes 1024 | tf_op jit(solution)/shard_map/turn_1/pallas_call | solution.py:50
  8.3 0.0 copy-done.3
  8.3 0.6 %cut_env.1 = (bf16[8,64,128]{2,1,0:T(8,128)(2,1)S(1)}, bf16[8,64,128]{2,1,0:T(8,128)(2,1)S(1)}, bf16[8,64,128]{2,1,0:T(8,128)(2,1)S(1)}, bf16[8,64,128]{2,1,0:T(8,128)(2,1)S(1)}) custom-call(s32[6]{0:T(128)S(1)} %stack.23.info, bf16[8,2,128,128]{3,2,1,0:T(8,128)(2,1)S(1)} %copy-done.3), custom_call_target="tpu_custom_call" | custom-call | flops 1024 | bytes 1024 | tf_op jit(solution)/shard_map/cut_env/pallas_call | solution.py:129
  8.9 0.0 copy-done.7
  8.9 0.0 copy-done.2
  8.9 0.0 copy-done.4
  8.9 0.0 copy-done.8
  8.9 0.8 %pack.1.refs_2_ = bf16[1296,128]{1,0:T(8,128)(2,1)S(1)} custom-call(s32[6]{0:T(128)S(1)} %stack.23.info, s32[8,16]{1,0:T(8,128)S(1)} %copy-done.7, s32[8]{0:T(128)S(1)} %copy-done.8, bf16[8,16,16,16]{3,2,1,0:T(8,128)(2,1)S(1)} %copy-done.4, bf16[8,2,128,128]{3,2,1,0:T(8,128)(2,1)S(1)} %copy-done.2), custom_call_target="tpu_custom_call" | custom-call | flops 1024 | bytes 1024 | tf_op jit(solution)/shard_map/pack/pallas_call | solution.py:94
  9.8 1.3 %collective-permute-start.1 = (bf16[1296,128]{1,0:T(8,128)(2,1)S(1)}, bf16[1296,128]{1,0:T(8,128)(2,1)S(1)}, u32[]{:S(2)}, u32[]{:S(2)}) collective-permute-start(bf16[1296,128]{1,0:T(8,128)(2,1)S(1)} %pack.1.refs_2_), channel_id=1, source_target_pairs={{2,0},{0,2},{3,1},{1,3},{6,4},{4,6},{7,5},{5,7},{10,8},{8,10},{11,... | collective-permute-start | bytes 995336 | tf_op jit(solution)/shard_map/ppermute | solution.py:22
  11.0 0.8 %collective-permute-start.4 = (bf16[8,64,128]{2,1,0:T(8,128)(2,1)S(1)}, bf16[8,64,128]{2,1,0:T(8,128)(2,1)S(1)}, u32[]{:S(2)}, u32[]{:S(2)}) collective-permute-start(bf16[8,64,128]{2,1,0:T(8,128)(2,1)S(1)} %get-tuple-element.24), channel_id=1, source_target_pairs={{0,13},{1,12},{4,9},{5,8},{8,5},{9,4},{12,1},{13,0},{2,15},{3,14},... | collective-permute-start | bytes 393224 | tf_op jit(solution)/shard_map/ppermute | solution.py:392
  11.9 3.5 %collective-permute-done.2.psi = bf16[1,128,16,128]{3,2,1,0:T(8,128)(2,1)S(1)} collective-permute-done((bf16[1,128,16,128]{3,2,1,0:T(8,128)(2,1)S(1)}, bf16[1,128,16,128]{3,2,1,0:T(8,128)(2,1)S(1)}, u32[]{:S(2)}, u32[]{:S(2)}) %collective-permute-start.2) | collective-permute-done | bytes 524320 | tf_op jit(solution)/shard_map/ppermute | solution.py:378
  15.4 5.5 %collective-permute-start.3 = (bf16[1,128,16,128]{3,2,1,0:T(8,128)(2,1)S(1)}, bf16[1,128,16,128]{3,2,1,0:T(8,128)(2,1)S(1)}, u32[]{:S(2)}, u32[]{:S(2)}) collective-permute-start(bf16[1,128,16,128]{3,2,1,0:T(8,128)(2,1)S(1)} %collective-permute-done.2.psi), channel_id=1, source_target_pairs={{2,0},{1,3},{6,4},{5,7},{10,8},{9,11},{14,12},{13,15},{18,16},{17,... | collective-permute-start | bytes 1572872 | tf_op jit(solution)/shard_map/ppermute | solution.py:389
  20.9 0.0 copy-done.1
  20.9 1.8 %turn_0.1.refs_0_ = bf16[6,128,2048]{2,1,0:T(8,128)(2,1)S(1)} custom-call(s32[6]{0:T(128)S(1)} %stack.23.info, s32[16]{0:T(128)S(1)} %copy-done.5, bf16[2,128,16,128]{3,2,1,0:T(8,128)(2,1)S(1)} %copy-done.1, bf16[6,128,2048]{2,1,0:T(8,128)(2,1)S(1)} %turn_1.1.refs_0_), custom_call_target="tpu_custom_call", output_to_operand_aliasing={{}: (3, {})} | custom-call | flops 1024 | bytes 1024 | tf_op jit(solution)/shard_map/turn_0/pallas_call | solution.py:50
  22.7 0.1 collective-permute-start.7
  22.8 0.0 collective-permute-done.4.refs_0_
  22.8 1.1 %turn_2.1.refs_0_ = bf16[6,128,2048]{2,1,0:T(8,128)(2,1)S(1)} custom-call(s32[6]{0:T(128)S(1)} %stack.23.info, s32[16]{0:T(128)S(1)} %copy-done.5, bf16[1,128,16,128]{3,2,1,0:T(8,128)(2,1)S(1)} %collective-permute-done.2.psi, bf16[6,128,2048]{2,1,0:T(8,128)(2,1)S(1)} %turn_0.1.refs_0_), custom_call_target="tpu_custom_call", output_to_operand_aliasing={{}: (3, {})} | custom-call | flops 1073741824 | bytes 1048576 | tf_op jit(solution)/shard_map/turn_2/pallas_call | solution.py:50
  23.9 0.9 %collective-permute-start.5 = (bf16[8,64,128]{2,1,0:T(8,128)(2,1)S(1)}, bf16[8,64,128]{2,1,0:T(8,128)(2,1)S(1)}, u32[]{:S(2)}, u32[]{:S(2)}) collective-permute-start(bf16[8,64,128]{2,1,0:T(8,128)(2,1)S(1)} %get-tuple-element.33), channel_id=1, source_target_pairs={{15,0},{13,2},{14,1},{12,3},{11,4},{9,6},{10,5},{8,7},{7,8},{5,10}... | collective-permute-start | bytes 393224 | tf_op jit(solution)/shard_map/ppermute | solution.py:399
  24.8 1.9 %collective-permute-start.8 = (bf16[8,64,128]{2,1,0:T(8,128)(2,1)S(1)}, bf16[8,64,128]{2,1,0:T(8,128)(2,1)S(1)}, u32[]{:S(2)}, u32[]{:S(2)}) collective-permute-start(bf16[8,64,128]{2,1,0:T(8,128)(2,1)S(1)} %get-tuple-element.36), channel_id=1, source_target_pairs={{15,0},{13,2},{14,1},{12,3},{11,4},{9,6},{10,5},{8,7},{7,8},{5,10}... | collective-permute-start | bytes 393224 | tf_op jit(solution)/shard_map/ppermute | solution.py:399
  26.7 0.0 collective-permute-done.1.refs_3_
  26.7 0.1 maximum_convert_fusion.shift
  26.7 0.2 collective-permute-done.3.psi
  27.0 1.1 %turn_3.1.refs_0_ = bf16[6,128,2048]{2,1,0:T(8,128)(2,1)S(1)} custom-call(s32[6]{0:T(128)S(1)} %stack.23.info, s32[16]{0:T(128)S(1)} %copy-done.5, bf16[1,128,16,128]{3,2,1,0:T(8,128)(2,1)S(1)} %collective-permute-done.3.psi, bf16[6,128,2048]{2,1,0:T(8,128)(2,1)S(1)} %turn_2.1.refs_0_), custom_call_target="tpu_custom_call", output_to_operand_aliasing={{}: (3, {})} | custom-call | flops 1024 | bytes 1024 | tf_op jit(solution)/shard_map/turn_3/pallas_call | solution.py:50
  28.1 0.0 copy-start.6
  28.1 5.2 %mix.1 = (bf16[1024,2048]{1,0:T(8,128)(2,1)S(1)}, bf16[1024,2048]{1,0:T(8,128)(2,1)S(1)}) custom-call(s32[6]{0:T(128)S(1)} %stack.23.info, s32[16]{0:T(128)S(1)} %maximum_convert_fusion.shift, bf16[6,128,2048]{2,1,0:T(8,128)(2,1)S(1)} %turn_3.1.refs_0_, bf16[8,2,128,128]{3,2,1,0:T(8,128)(2,1)S(1)} %copy-done.2, bf16[1296,128]{1,0:T(8,128)(2,1)S(1)} %pack.1.refs_2_, ...), custom_call_target="tpu_custom_call" | custom-call | flops 1024 | bytes 1024 | tf_op jit(solution)/shard_map/mix/pallas_call | solution.py:211
  33.3 1.8 %collective-permute-done.5.refs_1_ = bf16[8,64,128]{2,1,0:T(8,128)(2,1)S(1)} collective-permute-done((bf16[8,64,128]{2,1,0:T(8,128)(2,1)S(1)}, bf16[8,64,128]{2,1,0:T(8,128)(2,1)S(1)}, u32[]{:S(2)}, u32[]{:S(2)}) %collective-permute-start.5) | collective-permute-done | bytes 131104 | tf_op jit(solution)/shard_map/ppermute | solution.py:399
  35.2 0.0 copy-done.6
  35.2 1.8 %give_0.1 = bf16[65,8,128]{2,1,0:T(8,128)(2,1)S(1)} custom-call(s32[6]{0:T(128)S(1)} %stack.23.info, s32[16]{0:T(128)S(1)} %copy-done.6, bf16[1024,2048]{1,0:T(8,128)(2,1)S(1)} %get-tuple-element.32.mixed, bf16[8,64,128]{2,1,0:T(8,128)(2,1)S(1)} %collective-permute-done.4.refs_0_, bf16[8,64,128]{2,1,0:T(8,128)(2,1)S(1)} %collective-permute-done.5.refs_1_), custom_call_target="tpu_custom_call" | custom-call | flops 268435456 | bytes 1048576 | tf_op jit(solution)/shard_map/give_0/pallas_call | solution.py:274
  37.0 1.2 %collective-permute-start.6 = (bf16[65,8,128]{2,1,0:T(8,128)(2,1)S(1)}, bf16[65,8,128]{2,1,0:T(8,128)(2,1)S(1)}, u32[]{:S(2)}, u32[]{:S(2)}) collective-permute-start(bf16[65,8,128]{2,1,0:T(8,128)(2,1)S(1)} %give_0.1), channel_id=1, source_target_pairs={{0,2},{2,0},{1,3},{3,1},{4,6},{6,4},{5,7},{7,5},{8,10},{10,8},{9,1... | collective-permute-start | bytes 399368 | tf_op jit(solution)/shard_map/ppermute | solution.py:402
  38.2 0.0 collective-permute-done.7.refs_0_.refs_2_
  38.2 0.0 collective-permute-done.8.refs_1_.refs_3_
  38.2 1.8 %give_1.1 = bf16[64,8,128]{2,1,0:T(8,128)(2,1)S(1)} custom-call(s32[6]{0:T(128)S(1)} %stack.23.info, s32[16]{0:T(128)S(1)} %copy-done.6, bf16[1024,2048]{1,0:T(8,128)(2,1)S(1)} %get-tuple-element.32.mixed, bf16[8,64,128]{2,1,0:T(8,128)(2,1)S(1)} %collective-permute-done.7.refs_0_.refs_2_, bf16[8,64,128]{2,1,0:T(8,128)(2,1)S(1)} %collective-permute-done.8.refs_1_.refs_3_), custom_call_target="tpu_custom_call" | custom-call | flops 268435456 | bytes 1048576 | tf_op jit(solution)/shard_map/give_1/pallas_call | solution.py:274
  40.1 0.5 %collective-permute-start.9 = (bf16[64,8,128]{2,1,0:T(8,128)(2,1)S(1)}, bf16[64,8,128]{2,1,0:T(8,128)(2,1)S(1)}, u32[]{:S(2)}, u32[]{:S(2)}) collective-permute-start(bf16[64,8,128]{2,1,0:T(8,128)(2,1)S(1)} %give_1.1), channel_id=1, source_target_pairs={{0,2},{2,0},{1,3},{3,1},{4,6},{6,4},{5,7},{7,5},{8,10},{10,8},{9,1... | collective-permute-start | bytes 393224 | tf_op jit(solution)/shard_map/ppermute | solution.py:402
  40.6 2.5 %keep.1.result = bf16[2,128,8,128]{3,2,1,0:T(8,128)(2,1)} custom-call(s32[6]{0:T(128)S(1)} %stack.23.info, s32[16]{0:T(128)S(1)} %copy-done.6, bf16[1024,2048]{1,0:T(8,128)(2,1)S(1)} %get-tuple-element.38.mixed, bf16[8,64,128]{2,1,0:T(8,128)(2,1)S(1)} %collective-permute-done.4.refs_0_, bf16[8,64,128]{2,1,0:T(8,128)(2,1)S(1)} %collective-permute-done.5.refs_1_, ...), custom_call_target="tpu_custom_call" | custom-call | flops 1024 | bytes 1024 | tf_op jit(solution)/shard_map/keep/pallas_call | solution.py:300
  43.1 1.9 %collective-permute-done.9.one = bf16[64,8,128]{2,1,0:T(8,128)(2,1)S(1)} collective-permute-done((bf16[64,8,128]{2,1,0:T(8,128)(2,1)S(1)}, bf16[64,8,128]{2,1,0:T(8,128)(2,1)S(1)}, u32[]{:S(2)}, u32[]{:S(2)}) %collective-permute-start.9) | collective-permute-done | bytes 131104 | tf_op jit(solution)/shard_map/ppermute | solution.py:402
  45.0 0.0 collective-permute-done.6.zero
  45.0 1.4 %finish.1 = bf16[2,128,8,128]{3,2,1,0:T(8,128)(2,1)} custom-call(s32[6]{0:T(128)S(1)} %stack.23.info, bf16[65,8,128]{2,1,0:T(8,128)(2,1)S(1)} %collective-permute-done.6.zero, bf16[64,8,128]{2,1,0:T(8,128)(2,1)S(1)} %collective-permute-done.9.one, bf16[2,128,8,128]{3,2,1,0:T(8,128)(2,1)} %keep.1.result), custom_call_target="tpu_custom_call", output_to_operand_aliasing={{}: (3, {})} | custom-call | flops 1024 | bytes 1024 | tf_op jit(solution)/shard_map/finish/pallas_call | solution.py:335
  (2 shorter events, 0.0 us)
Async XLA Ops:
  0.0 5.8 %collective-permute-start = (bf16[2,128,16,128]{3,2,1,0:T(8,128)(2,1)}, bf16[2,128,16,128]{3,2,1,0:T(8,128)(2,1)S(1)}, u32[]{:S(2)}, u32[]{:S(2)}) collective-permute-start(bf16[2,128,16,128]{3,2,1,0:T(8,128)(2,1)} %psi.3), channel_id=1, source_target_pairs={{0,1},{1,0},{4,5},{5,4},{8,9},{9,8},{12,13},{13,12},{2,3},{3,2},{6... | collective-permute-start | bytes 3145736 | tf_op jit(solution)/shard_map/ppermute | solution.py:378
  0.7 8.2 %copy-start.7 = (s32[8,16]{1,0:T(8,128)S(1)}, s32[8,16]{1,0:T(8,128)}, u32[]{:S(2)}) copy-start(s32[8,16]{1,0:T(8,128)} %mask.1) | copy-start | bytes 1540
  0.8 1.2 %copy-start = (bf16[2,128,16,128]{3,2,1,0:T(8,128)(2,1)S(1)}, bf16[2,128,16,128]{3,2,1,0:T(8,128)(2,1)}, u32[]{:S(2)}) copy-start(bf16[2,128,16,128]{3,2,1,0:T(8,128)(2,1)} %psi.3) | copy-start | bytes 3145732
  2.0 6.3 %copy-start.3 = (bf16[8,2,128,128]{3,2,1,0:T(8,128)(2,1)S(1)}, bf16[8,2,128,128]{3,2,1,0:T(8,128)(2,1)}, u32[]{:S(2)}) copy-start(bf16[8,2,128,128]{3,2,1,0:T(8,128)(2,1)} %env.1) | copy-start | bytes 1572868
  2.0 6.9 %copy-start.2 = (bf16[8,2,128,128]{3,2,1,0:T(8,128)(2,1)S(1)}, bf16[8,2,128,128]{3,2,1,0:T(8,128)(2,1)}, u32[]{:S(2)}) copy-start(bf16[8,2,128,128]{3,2,1,0:T(8,128)(2,1)} %refs_1_.1) | copy-start | bytes 1572868
  2.0 6.9 %copy-start.4 = (bf16[8,16,16,16]{3,2,1,0:T(8,128)(2,1)S(1)}, bf16[8,16,16,16]{3,2,1,0:T(8,128)(2,1)}, u32[]{:S(2)}) copy-start(bf16[8,16,16,16]{3,2,1,0:T(8,128)(2,1)} %coef.1) | copy-start | bytes 196612
  2.0 6.9 %copy-start.8 = (s32[8]{0:T(128)S(1)}, s32[8]{0:T(128)}, u32[]{:S(2)}) copy-start(s32[8]{0:T(128)} %shift.1) | copy-start | bytes 100
  2.6 18.3 %copy-start.1 = (bf16[2,128,16,128]{3,2,1,0:T(8,128)(2,1)S(1)}, bf16[2,128,16,128]{3,2,1,0:T(8,128)(2,1)}, u32[]{:S(2)}) copy-start(bf16[2,128,16,128]{3,2,1,0:T(8,128)(2,1)} %psi.3) | copy-start | bytes 3145732
  2.6 12.8 %collective-permute-start.2 = (bf16[1,128,16,128]{3,2,1,0:T(8,128)(2,1)S(1)}, bf16[1,128,16,128]{3,2,1,0:T(8,128)(2,1)S(1)}, u32[]{:S(2)}, u32[]{:S(2)}) collective-permute-start(bf16[1,128,16,128]{3,2,1,0:T(8,128)(2,1)S(1)} %cut_psi.1), channel_id=1, source_target_pairs={{1,4},{4,1},{5,8},{8,5},{9,12},{12,9},{3,6},{6,3},{7,10},{10,7},{1... | collective-permute-start | bytes 1572872 | tf_op jit(solution)/shard_map/ppermute | solution.py:378
  5.8 0.7 %copy-start.5 = (s32[16]{0:T(128)S(1)}, s32[16]{0:T(128)}, u32[]{:S(2)}) copy-start(s32[16]{0:T(128)} %dims.13) | copy-start | bytes 196
  9.8 16.9 %collective-permute-start.1 = (bf16[1296,128]{1,0:T(8,128)(2,1)S(1)}, bf16[1296,128]{1,0:T(8,128)(2,1)S(1)}, u32[]{:S(2)}, u32[]{:S(2)}) collective-permute-start(bf16[1296,128]{1,0:T(8,128)(2,1)S(1)} %pack.1.refs_2_), channel_id=1, source_target_pairs={{2,0},{0,2},{3,1},{1,3},{6,4},{4,6},{7,5},{5,7},{10,8},{8,10},{11,... | collective-permute-start | bytes 995336 | tf_op jit(solution)/shard_map/ppermute | solution.py:22
  11.0 11.8 %collective-permute-start.4 = (bf16[8,64,128]{2,1,0:T(8,128)(2,1)S(1)}, bf16[8,64,128]{2,1,0:T(8,128)(2,1)S(1)}, u32[]{:S(2)}, u32[]{:S(2)}) collective-permute-start(bf16[8,64,128]{2,1,0:T(8,128)(2,1)S(1)} %get-tuple-element.24), channel_id=1, source_target_pairs={{0,13},{1,12},{4,9},{5,8},{8,5},{9,4},{12,1},{13,0},{2,15},{3,14},... | collective-permute-start | bytes 393224 | tf_op jit(solution)/shard_map/ppermute | solution.py:392
  15.4 11.6 %collective-permute-start.3 = (bf16[1,128,16,128]{3,2,1,0:T(8,128)(2,1)S(1)}, bf16[1,128,16,128]{3,2,1,0:T(8,128)(2,1)S(1)}, u32[]{:S(2)}, u32[]{:S(2)}) collective-permute-start(bf16[1,128,16,128]{3,2,1,0:T(8,128)(2,1)S(1)} %collective-permute-done.2.psi), channel_id=1, source_target_pairs={{2,0},{1,3},{6,4},{5,7},{10,8},{9,11},{14,12},{13,15},{18,16},{17,... | collective-permute-start | bytes 1572872 | tf_op jit(solution)/shard_map/ppermute | solution.py:389
  22.7 15.5 %collective-permute-start.7 = (bf16[8,64,128]{2,1,0:T(8,128)(2,1)S(1)}, bf16[8,64,128]{2,1,0:T(8,128)(2,1)S(1)}, u32[]{:S(2)}, u32[]{:S(2)}) collective-permute-start(bf16[8,64,128]{2,1,0:T(8,128)(2,1)S(1)} %get-tuple-element.35), channel_id=1, source_target_pairs={{0,13},{1,12},{4,9},{5,8},{8,5},{9,4},{12,1},{13,0},{2,15},{3,14},... | collective-permute-start | bytes 393224 | tf_op jit(solution)/shard_map/ppermute | solution.py:392
  23.9 11.2 %collective-permute-start.5 = (bf16[8,64,128]{2,1,0:T(8,128)(2,1)S(1)}, bf16[8,64,128]{2,1,0:T(8,128)(2,1)S(1)}, u32[]{:S(2)}, u32[]{:S(2)}) collective-permute-start(bf16[8,64,128]{2,1,0:T(8,128)(2,1)S(1)} %get-tuple-element.33), channel_id=1, source_target_pairs={{15,0},{13,2},{14,1},{12,3},{11,4},{9,6},{10,5},{8,7},{7,8},{5,10}... | collective-permute-start | bytes 393224 | tf_op jit(solution)/shard_map/ppermute | solution.py:399
  24.8 13.4 %collective-permute-start.8 = (bf16[8,64,128]{2,1,0:T(8,128)(2,1)S(1)}, bf16[8,64,128]{2,1,0:T(8,128)(2,1)S(1)}, u32[]{:S(2)}, u32[]{:S(2)}) collective-permute-start(bf16[8,64,128]{2,1,0:T(8,128)(2,1)S(1)} %get-tuple-element.36), channel_id=1, source_target_pairs={{15,0},{13,2},{14,1},{12,3},{11,4},{9,6},{10,5},{8,7},{7,8},{5,10}... | collective-permute-start | bytes 393224 | tf_op jit(solution)/shard_map/ppermute | solution.py:399
  28.1 7.1 %copy-start.6 = (s32[16]{0:T(128)S(1)}, s32[16]{0:T(128)}, u32[]{:S(2)}) copy-start(s32[16]{0:T(128)} %dims.13) | copy-start | bytes 196
  37.0 8.0 %collective-permute-start.6 = (bf16[65,8,128]{2,1,0:T(8,128)(2,1)S(1)}, bf16[65,8,128]{2,1,0:T(8,128)(2,1)S(1)}, u32[]{:S(2)}, u32[]{:S(2)}) collective-permute-start(bf16[65,8,128]{2,1,0:T(8,128)(2,1)S(1)} %give_0.1), channel_id=1, source_target_pairs={{0,2},{2,0},{1,3},{3,1},{4,6},{6,4},{5,7},{7,5},{8,10},{10,8},{9,1... | collective-permute-start | bytes 399368 | tf_op jit(solution)/shard_map/ppermute | solution.py:402
  40.1 4.9 %collective-permute-start.9 = (bf16[64,8,128]{2,1,0:T(8,128)(2,1)S(1)}, bf16[64,8,128]{2,1,0:T(8,128)(2,1)S(1)}, u32[]{:S(2)}, u32[]{:S(2)}) collective-permute-start(bf16[64,8,128]{2,1,0:T(8,128)(2,1)S(1)} %give_1.1), channel_id=1, source_target_pairs={{0,2},{2,0},{1,3},{3,1},{4,6},{6,4},{5,7},{7,5},{8,10},{10,8},{9,1... | collective-permute-start | bytes 393224 | tf_op jit(solution)/shard_map/ppermute | solution.py:402
